TPU v7x, 32 devices: a whole 2x2x4 slice. The times are simulated.
32 devices in a mesh: patch: 16 (over z, y, core), seq: 2 (over x).
Axes of the slice: x: 2, y: 2, z: 4, core: 2. Of those that a mesh axis runs over, the one named last changes fastest.
Arguments:
- tokens: bfloat16 [2, 16, 256, 1152], P('seq', None, 'patch'), may hold values from -6 to 6
- cotangent: bfloat16 [2, 16, 256, 1152], P('seq', None, 'patch'), may hold values from -6 to 6
- class_ids: int32 [2], P('seq'), may hold values from 0 to 100
- timesteps: int32 [2], P('seq'), may hold values from 0 to 999
- segments: int32 [2, 16], P('seq'), may hold values from 0 to 3, never falling along the last dimension, each value on 1 to 8 neighbouring positions
- class_table: bfloat16 [101, 1152], replicated, may hold values from -6 to 6
- mod_spatial: bfloat16 [1152, 6912], P('patch', 'seq'), may hold values from -0.1875 to 0.1875
- qkv_spatial: bfloat16 [1152, 3456], P('patch', 'seq'), may hold values from -0.1875 to 0.1875
- out_spatial: bfloat16 [1152, 1152], P('patch', 'seq'), may hold values from -2 to 2
- up_spatial: bfloat16 [1152, 4608], P('patch', 'seq'), may hold values from -0.1875 to 0.1875
- down_spatial: bfloat16 [4608, 1152], P('patch', 'seq'), may hold values from -0.125 to 0.125
- mod_temporal: bfloat16 [1152, 6912], P('patch', 'seq'), may hold values from -0.1875 to 0.1875
- qkv_temporal: bfloat16 [1152, 3456], P('patch', 'seq'), may hold values from -0.1875 to 0.1875
- out_temporal: bfloat16 [1152, 1152], P('patch', 'seq'), may hold values from -0.375 to 0.375
- up_temporal: bfloat16 [1152, 4608], P('patch', 'seq'), may hold values from -0.1875 to 0.1875
- down_temporal: bfloat16 [4608, 1152], P('patch', 'seq'), may hold values from -0.125 to 0.125
Outputs:
- out_tokens: bfloat16 [2, 16, 256, 1152], P('seq', None, 'patch')
- grad_tokens: float32 [2, 16, 256, 1152], P('seq', None, 'patch')
- grad_class_table: float32 [101, 1152], replicated
- grad_mod_spatial: float32 [1152, 6912], P('patch', 'seq')
- grad_qkv_spatial: float32 [1152, 3456], P('patch', 'seq')
- grad_out_spatial: float32 [1152, 1152], P('patch', 'seq')
- grad_up_spatial: float32 [1152, 4608], P('patch', 'seq')
- grad_down_spatial: float32 [4608, 1152], P('patch', 'seq')
- grad_mod_temporal: float32 [1152, 6912], P('patch', 'seq')
- grad_qkv_temporal: float32 [1152, 3456], P('patch', 'seq')
- grad_out_temporal: float32 [1152, 1152], P('patch', 'seq')
- grad_up_temporal: float32 [1152, 4608], P('patch', 'seq')
- grad_down_temporal: float32 [4608, 1152], P('patch', 'seq')
Inputs may be any that keep to these rules, and one draw needn't show every extreme that they name: `segments`: along the frame slots of a sequence the clip numbers never fall; every clip number occurs, each clip holds 1 to 8 slots, and one holds exactly 8.
All inputs are finite; a program needn't handle non-finite values.
Results may differ from a plain program's by a relative error of at most 0.02.
Values may be sent and summed in bfloat16 or wider, within the bound.
No kernel may reach another device: no remote copies, remote signals or barrier semaphores. Data moves between devices by JAX's collectives and lax.ppermute only.
A program may use at most 384 MiB of HBM per device.

v0:
```python
from functools import partial
import math

import jax
import jax.numpy as jnp
from jax import lax
from jax.sharding import PartitionSpec as P

HEADS = 16


PRECISE = lax.Precision.HIGHEST
EPSILON = 1e-06


def time_features(step_ids, features):
    half_width = features // 2
    frequency = jnp.exp(-math.log(10000.0) * jnp.arange(half_width, dtype=jnp.float32) / half_width)
    angles = step_ids.astype(jnp.float32)[:, None] * frequency[None, :]
    return jnp.concatenate([jnp.cos(angles), jnp.sin(angles)], axis=-1)


def normalize(values):
    centred = values - jnp.mean(values, axis=-1, keepdims=True)
    inverse = lax.rsqrt(jnp.mean(centred * centred, axis=-1, keepdims=True) + EPSILON)
    return (centred * inverse, inverse)


def normalize_back(grad_norm, normed, inverse):
    return inverse * (
        grad_norm
        - jnp.mean(grad_norm, axis=-1, keepdims=True)
        - normed * jnp.mean(grad_norm * normed, axis=-1, keepdims=True)
    )


def split_heads(values):
    return values.reshape(values.shape[:-1] + (HEADS, values.shape[-1] // HEADS))


def merge_heads(values):
    return values.reshape(values.shape[:-2] + (values.shape[-2] * values.shape[-1],))


def spread_rows(modulation, count):
    return jnp.broadcast_to(
        modulation[:, None, :], (modulation.shape[0], count, modulation.shape[1])
    ).reshape(-1, modulation.shape[1])


def per_sequence(values, groups):
    return jnp.sum(values.reshape(groups, -1, values.shape[-1]), axis=1)


def matmul(left, right):
    return jnp.dot(left, right, preferred_element_type=jnp.float32)


def fetch_weights(mod_weight, qkv_weight, out_weight, up_weight, down_weight):
    wide = (
        lax.all_gather(mod_weight, "seq", axis=1, tiled=True),
        lax.all_gather(qkv_weight, "seq", axis=1, tiled=True),
        lax.all_gather(out_weight, "seq", axis=1, tiled=True),
        lax.all_gather(up_weight, "seq", axis=1, tiled=True),
        lax.all_gather(down_weight, "seq", axis=1, tiled=True),
    )
    return (
        lax.all_gather(wide[0], "patch", axis=0, tiled=True),
        lax.all_gather(wide[1], "patch", axis=0, tiled=True),
        lax.all_gather(wide[2], "patch", axis=0, tiled=True),
        lax.all_gather(wide[3], "patch", axis=0, tiled=True),
        lax.all_gather(wide[4], "patch", axis=0, tiled=True),
    )


def reduce_grads(grad_mod, grad_qkv, grad_out, grad_up, grad_down):
    first = (
        lax.psum_scatter(
            grad_mod.astype(jnp.bfloat16), "patch", scatter_dimension=0, tiled=True
        ).astype(jnp.float32),
        lax.psum_scatter(
            grad_qkv.astype(jnp.bfloat16), "patch", scatter_dimension=0, tiled=True
        ).astype(jnp.float32),
        lax.psum_scatter(
            grad_out.astype(jnp.bfloat16), "patch", scatter_dimension=0, tiled=True
        ).astype(jnp.float32),
        lax.psum_scatter(
            grad_up.astype(jnp.bfloat16), "patch", scatter_dimension=0, tiled=True
        ).astype(jnp.float32),
        lax.psum_scatter(
            grad_down.astype(jnp.bfloat16), "patch", scatter_dimension=0, tiled=True
        ).astype(jnp.float32),
    )
    final = (
        lax.psum_scatter(
            first[0].astype(jnp.bfloat16), "seq", scatter_dimension=1, tiled=True
        ).astype(jnp.float32),
        lax.psum_scatter(
            first[1].astype(jnp.bfloat16), "seq", scatter_dimension=1, tiled=True
        ).astype(jnp.float32),
        lax.psum_scatter(
            first[2].astype(jnp.bfloat16), "seq", scatter_dimension=1, tiled=True
        ).astype(jnp.float32),
        lax.psum_scatter(
            first[3].astype(jnp.bfloat16), "seq", scatter_dimension=1, tiled=True
        ).astype(jnp.float32),
        lax.psum_scatter(
            first[4].astype(jnp.bfloat16), "seq", scatter_dimension=1, tiled=True
        ).astype(jnp.float32),
    )
    return final


def block_forward(residual, mod_rows, matrices, attend):
    mod_weight, qkv_weight, out_weight, up_weight, down_weight = matrices
    features = residual.shape[1]
    pieces = [mod_rows[:, number * features : (number + 1) * features] for number in range(6)]
    normed_one, inverse_one = normalize(residual)
    hidden_one = (normed_one * (1.0 + pieces[1]) + pieces[0]).astype(jnp.bfloat16)
    qkv_rows = matmul(hidden_one, qkv_weight).astype(jnp.bfloat16)
    attended, mix_state = attend(qkv_rows)
    branch = matmul(attended, out_weight)
    middle = residual + pieces[2] * branch
    normed_two, inverse_two = normalize(middle)
    hidden_two = (normed_two * (1.0 + pieces[4]) + pieces[3]).astype(jnp.bfloat16)
    pre_gelu = matmul(hidden_two, up_weight)
    activated = jax.nn.gelu(pre_gelu, approximate=True).astype(jnp.bfloat16)
    mlp_output = matmul(activated, down_weight)
    result = middle + pieces[5] * mlp_output
    saved = (
        normed_one,
        inverse_one,
        hidden_one,
        qkv_rows,
        attended,
        mix_state,
        branch,
        normed_two,
        inverse_two,
        hidden_two,
        pre_gelu,
        activated,
        mlp_output,
    )
    return (result, saved)


def block_backward(incoming, matrices, mod_rows, saved, attend_back, groups):
    mod_weight, qkv_weight, out_weight, up_weight, down_weight = matrices
    (
        normed_one,
        inverse_one,
        hidden_one,
        qkv_rows,
        attended,
        mix_state,
        branch,
        normed_two,
        inverse_two,
        hidden_two,
        pre_gelu,
        activated,
        mlp_output,
    ) = saved
    features = incoming.shape[1]
    pieces = [mod_rows[:, number * features : (number + 1) * features] for number in range(6)]
    grad_mlp = (pieces[5] * incoming).astype(jnp.bfloat16)
    grad_gelu = matmul(grad_mlp, down_weight.T)
    gelu_value, gelu_back = jax.vjp(partial(jax.nn.gelu, approximate=True), pre_gelu)
    grad_pre = gelu_back(grad_gelu)[0].astype(jnp.bfloat16)
    grad_down = matmul(activated.T, grad_mlp)
    grad_up = matmul(hidden_two.T, grad_pre)
    grad_hidden_two = matmul(grad_pre, up_weight.T)
    grad_middle = incoming + normalize_back(
        grad_hidden_two * (1.0 + pieces[4]), normed_two, inverse_two
    )
    grad_branch = (pieces[2] * grad_middle).astype(jnp.bfloat16)
    grad_attended = matmul(grad_branch, out_weight.T).astype(jnp.bfloat16)
    grad_out = matmul(attended.T, grad_branch)
    grad_qkv_rows = attend_back(grad_attended, qkv_rows, mix_state)
    grad_qkv = matmul(hidden_one.T, grad_qkv_rows)
    grad_hidden_one = matmul(grad_qkv_rows, qkv_weight.T)
    grad_residual = grad_middle + normalize_back(
        grad_hidden_one * (1.0 + pieces[1]), normed_one, inverse_one
    )
    grad_rows = jnp.concatenate(
        [
            grad_hidden_one,
            grad_hidden_one * normed_one,
            grad_middle * branch,
            grad_hidden_two,
            grad_hidden_two * normed_two,
            incoming * mlp_output,
        ],
        axis=-1,
    )
    grad_mods = per_sequence(grad_rows, groups)
    return (grad_residual, grad_mods, (grad_qkv, grad_out, grad_up, grad_down))


def per_device(
    tokens,
    cotangent,
    class_ids,
    timesteps,
    segments,
    class_table,
    mod_spatial,
    qkv_spatial,
    out_spatial,
    up_spatial,
    down_spatial,
    mod_temporal,
    qkv_temporal,
    out_temporal,
    up_temporal,
    down_temporal,
):
    groups, frames, patch_rows, features = tokens.shape
    row_count = groups * frames * patch_rows
    factor = (features // HEADS) ** (-0.5)
    residual = tokens.astype(jnp.float32).reshape(row_count, features)
    one_hot = (
        class_ids[:, None] == jnp.arange(class_table.shape[0], dtype=jnp.int32)[None, :]
    ).astype(jnp.bfloat16)
    condition = matmul(one_hot, class_table) + time_features(timesteps, features)
    cond_low = jax.nn.silu(condition).astype(jnp.bfloat16)
    same_clip = segments[:, :, None] == segments[:, None, :]

    def spatial_attend(qkv_rows):
        packed = qkv_rows.reshape(groups, frames, patch_rows, 3 * features)
        key_all, value_all = (
            lax.all_gather(packed[..., features : 2 * features], "patch", axis=2, tiled=True),
            lax.all_gather(packed[..., 2 * features :], "patch", axis=2, tiled=True),
        )
        queries = split_heads(packed[..., :features])
        scores = (
            jnp.einsum(
                "sfphd,sfkhd->sfhpk",
                queries,
                split_heads(key_all),
                preferred_element_type=jnp.float32,
            )
            * factor
        )
        log_total = jax.nn.logsumexp(scores, axis=-1, keepdims=True)
        attention_low = jnp.exp(scores - log_total).astype(jnp.bfloat16)
        mixture = jnp.einsum(
            "sfhpk,sfkhd->sfphd",
            attention_low,
            split_heads(value_all),
            preferred_element_type=jnp.float32,
        )
        attended = merge_heads(mixture).reshape(row_count, features).astype(jnp.bfloat16)
        return (attended, (log_total,))

    def spatial_back(grad_attended, qkv_rows, mix_state):
        packed = qkv_rows.reshape(groups, frames, patch_rows, 3 * features)
        key_all, value_all = (
            lax.all_gather(packed[..., features : 2 * features], "patch", axis=2, tiled=True),
            lax.all_gather(packed[..., 2 * features :], "patch", axis=2, tiled=True),
        )
        query_local = packed[..., :features]
        grad_local = grad_attended.reshape(groups, frames, patch_rows, features)
        queries = split_heads(query_local)
        key_heads = split_heads(key_all)
        value_heads = split_heads(value_all)
        grad_heads = split_heads(grad_local)
        scores = (
            jnp.einsum("sfphd,sfkhd->sfhpk", queries, key_heads, preferred_element_type=jnp.float32)
            * factor
        )
        attention = jnp.exp(scores - mix_state[0])
        grad_attention = jnp.einsum(
            "sfphd,sfkhd->sfhpk", grad_heads, value_heads, preferred_element_type=jnp.float32
        )
        row_delta = jnp.sum(grad_attention * attention, axis=-1, keepdims=True)
        grad_scores = (attention * (grad_attention - row_delta)).astype(jnp.bfloat16)
        grad_queries = (
            jnp.einsum(
                "sfhpk,sfkhd->sfphd", grad_scores, key_heads, preferred_element_type=jnp.float32
            )
            * factor
        )
        query_all, grad_all = (
            lax.all_gather(query_local, "patch", axis=2, tiled=True),
            lax.all_gather(grad_local, "patch", axis=2, tiled=True),
        )
        log_all, delta_all = (
            lax.all_gather(jnp.moveaxis(mix_state[0][..., 0], 2, 3), "patch", axis=2, tiled=True),
            lax.all_gather(jnp.moveaxis(row_delta[..., 0], 2, 3), "patch", axis=2, tiled=True),
        )
        log_all = jnp.moveaxis(log_all, 3, 2)[..., None]
        delta_all = jnp.moveaxis(delta_all, 3, 2)[..., None]
        query_heads_all = split_heads(query_all)
        grad_heads_all = split_heads(grad_all)
        own_keys = split_heads(packed[..., features : 2 * features])
        own_values = split_heads(packed[..., 2 * features :])
        scores_own = (
            jnp.einsum(
                "sfphd,sfkhd->sfhpk", query_heads_all, own_keys, preferred_element_type=jnp.float32
            )
            * factor
        )
        attention_own = jnp.exp(scores_own - log_all)
        attention_own_low = attention_own.astype(jnp.bfloat16)
        grad_attention_own = jnp.einsum(
            "sfphd,sfkhd->sfhpk", grad_heads_all, own_values, preferred_element_type=jnp.float32
        )
        grad_scores_own = (attention_own * (grad_attention_own - delta_all)).astype(jnp.bfloat16)
        grad_keys = (
            jnp.einsum(
                "sfhpk,sfphd->sfkhd",
                grad_scores_own,
                query_heads_all,
                preferred_element_type=jnp.float32,
            )
            * factor
        )
        grad_values = jnp.einsum(
            "sfhpk,sfphd->sfkhd",
            attention_own_low,
            grad_heads_all,
            preferred_element_type=jnp.float32,
        )
        joined = jnp.concatenate(
            [merge_heads(grad_queries), merge_heads(grad_keys), merge_heads(grad_values)], axis=-1
        )
        return joined.reshape(row_count, 3 * features).astype(jnp.bfloat16)

    def temporal_scores(queries, key_heads):
        scores = (
            jnp.einsum("sfphd,sgphd->sphfg", queries, key_heads, preferred_element_type=jnp.float32)
            * factor
        )
        return jnp.where(same_clip[:, None, None, :, :], scores, -1e30)

    def temporal_attend(qkv_rows):
        packed = qkv_rows.reshape(groups, frames, patch_rows, 3 * features)
        queries = split_heads(packed[..., :features])
        scores = temporal_scores(queries, split_heads(packed[..., features : 2 * features]))
        log_total = jax.nn.logsumexp(scores, axis=-1, keepdims=True)
        attention_low = jnp.exp(scores - log_total).astype(jnp.bfloat16)
        mixture = jnp.einsum(
            "sphfg,sgphd->sfphd",
            attention_low,
            split_heads(packed[..., 2 * features :]),
            preferred_element_type=jnp.float32,
        )
        return (
            merge_heads(mixture).reshape(row_count, features).astype(jnp.bfloat16),
            (log_total,),
        )

    def temporal_back(grad_attended, qkv_rows, mix_state):
        packed = qkv_rows.reshape(groups, frames, patch_rows, 3 * features)
        queries = split_heads(packed[..., :features])
        key_heads = split_heads(packed[..., features : 2 * features])
        value_heads = split_heads(packed[..., 2 * features :])
        grad_heads = split_heads(grad_attended.reshape(groups, frames, patch_rows, features))
        attention = jnp.exp(temporal_scores(queries, key_heads) - mix_state[0])
        attention_low = attention.astype(jnp.bfloat16)
        grad_attention = jnp.einsum(
            "sfphd,sgphd->sphfg", grad_heads, value_heads, preferred_element_type=jnp.float32
        )
        grad_scores = (
            attention
            * (grad_attention - jnp.sum(grad_attention * attention, axis=-1, keepdims=True))
        ).astype(jnp.bfloat16)
        grad_queries = (
            jnp.einsum(
                "sphfg,sgphd->sfphd", grad_scores, key_heads, preferred_element_type=jnp.float32
            )
            * factor
        )
        grad_keys = (
            jnp.einsum(
                "sphfg,sfphd->sgphd", grad_scores, queries, preferred_element_type=jnp.float32
            )
            * factor
        )
        grad_values = jnp.einsum(
            "sphfg,sfphd->sgphd", attention_low, grad_heads, preferred_element_type=jnp.float32
        )
        joined = jnp.concatenate(
            [merge_heads(grad_queries), merge_heads(grad_keys), merge_heads(grad_values)], axis=-1
        )
        return joined.reshape(row_count, 3 * features).astype(jnp.bfloat16)

    spatial_weights = fetch_weights(mod_spatial, qkv_spatial, out_spatial, up_spatial, down_spatial)
    spatial_rows = spread_rows(matmul(cond_low, spatial_weights[0]), frames * patch_rows)
    middle_rows, spatial_saved = block_forward(
        residual, spatial_rows, spatial_weights, spatial_attend
    )
    temporal_weights = fetch_weights(
        mod_temporal, qkv_temporal, out_temporal, up_temporal, down_temporal
    )
    temporal_rows = spread_rows(matmul(cond_low, temporal_weights[0]), frames * patch_rows)
    result, temporal_saved = block_forward(
        middle_rows, temporal_rows, temporal_weights, temporal_attend
    )
    out_tokens = result.astype(jnp.bfloat16).reshape(tokens.shape)
    cond_float = cond_low.astype(jnp.float32)
    incoming = cotangent.astype(jnp.float32).reshape(row_count, features)
    temporal_again = fetch_weights(
        mod_temporal, qkv_temporal, out_temporal, up_temporal, down_temporal
    )
    grad_middle_rows, temporal_grad_mods, temporal_grads = block_backward(
        incoming, temporal_again, temporal_rows, temporal_saved, temporal_back, groups
    )
    temporal_grad_mod = jnp.dot(cond_float.T, temporal_grad_mods, precision=PRECISE)
    grad_condition = jnp.dot(
        temporal_grad_mods,
        temporal_again[0].T,
        precision=PRECISE,
        preferred_element_type=jnp.float32,
    )
    temporal_final = reduce_grads(
        temporal_grad_mod,
        temporal_grads[0],
        temporal_grads[1],
        temporal_grads[2],
        temporal_grads[3],
    )
    spatial_again = fetch_weights(mod_spatial, qkv_spatial, out_spatial, up_spatial, down_spatial)
    grad_residual, spatial_grad_mods, spatial_grads = block_backward(
        grad_middle_rows, spatial_again, spatial_rows, spatial_saved, spatial_back, groups
    )
    spatial_grad_mod = jnp.dot(cond_float.T, spatial_grad_mods, precision=PRECISE)
    grad_condition = (
        jnp.dot(
            spatial_grad_mods,
            spatial_again[0].T,
            precision=PRECISE,
            preferred_element_type=jnp.float32,
        )
        + grad_condition
    )
    spatial_final = reduce_grads(
        spatial_grad_mod, spatial_grads[0], spatial_grads[1], spatial_grads[2], spatial_grads[3]
    )
    silu_value, silu_back = jax.vjp(jax.nn.silu, condition)
    grad_cond_full = silu_back(grad_condition)[0]
    table_part = jnp.dot(one_hot.astype(jnp.float32).T, grad_cond_full, precision=PRECISE)
    grad_class_table = lax.psum(table_part, ("patch", "seq"))
    return (
        out_tokens,
        grad_residual.reshape(tokens.shape),
        grad_class_table,
        spatial_final[0],
        spatial_final[1],
        spatial_final[2],
        spatial_final[3],
        spatial_final[4],
        temporal_final[0],
        temporal_final[1],
        temporal_final[2],
        temporal_final[3],
        temporal_final[4],
    )


def solution(mesh):
    placed = (
        P("seq", None, "patch", None),
        P("seq", None, "patch", None),
        P("seq"),
        P("seq"),
        P("seq", None),
        P(),
        P("patch", "seq"),
        P("patch", "seq"),
        P("patch", "seq"),
        P("patch", "seq"),
        P("patch", "seq"),
        P("patch", "seq"),
        P("patch", "seq"),
        P("patch", "seq"),
        P("patch", "seq"),
        P("patch", "seq"),
    )
    return jax.shard_map(
        per_device,
        mesh=mesh,
        in_specs=placed,
        out_specs=(
            P("seq", None, "patch", None),
            P("seq", None, "patch", None),
            P(),
            P("patch", "seq"),
            P("patch", "seq"),
            P("patch", "seq"),
            P("patch", "seq"),
            P("patch", "seq"),
            P("patch", "seq"),
            P("patch", "seq"),
            P("patch", "seq"),
            P("patch", "seq"),
            P("patch", "seq"),
        ),
        check_vma=False,
    )
```

profile of v0, /device:TPU:0, one launch (start us, length us, event | category | flops | bytes accessed | tf_op | source)
XLA Modules:
  0.0 2747.9 jit_solution(14811526287116750349)
XLA Ops:
  7.3 18.1 all_gather.100
  61.8 85.5 %all-gather.21.cloned.1.call-done = bf16[1152,6912]{1,0:T(8,128)(2,1)} async-done(((bf16[72,6912]{1,0:T(8,128)(2,1)}), bf16[1152,6912]{1,0:T(8,128)(2,1)}) %all-gather.21.cloned.1.call-update) | async-done | bytes 15925264 | tf_op jit(solution)/shard_map/all_gather | solution.py:68
  155.4 65.1 %all-gather.23.cloned.1.call-done = bf16[1152,3456]{1,0:T(8,128)(2,1)} async-done(((bf16[72,3456]{1,0:T(8,128)(2,1)}), bf16[1152,3456]{1,0:T(8,128)(2,1)}) %all-gather.23.cloned.1.call-update) | async-done | bytes 7962640 | tf_op jit(solution)/shard_map/all_gather | solution.py:69
  282.0 60.6 %all-gather.35.cloned.1.call-done = bf16[1152,6912]{1,0:T(8,128)(2,1)} async-done(((bf16[72,6912]{1,0:T(8,128)(2,1)}), bf16[1152,6912]{1,0:T(8,128)(2,1)}) %all-gather.35.cloned.1.call-update) | async-done | bytes 15925264 | tf_op jit(solution)/shard_map/all_gather | solution.py:68
  350.6 81.6 %all-gather.43.cloned.1.call-done = bf16[4608,1152]{1,0:T(8,128)(2,1)} async-done(((bf16[288,1152]{1,0:T(8,128)(2,1)}), bf16[4608,1152]{1,0:T(8,128)(2,1)}) %all-gather.43.cloned.1.call-update) | async-done | bytes 10616848 | tf_op jit(solution)/shard_map/all_gather | solution.py:72
  444.5 69.7 %all-gather.27.cloned.1.call-done = bf16[1,16,256,1152]{3,2,1,0:T(8,128)(2,1)} async-done(((bf16[1,16,16,1152]{3,2,1,0:T(8,128)(2,1)}), bf16[1,16,256,1152]{3,2,1,0:T(8,128)(2,1)}) %all-gather.27.cloned.1.call-update) | async-done | bytes 9437200 | tf_op jit(solution)/shard_map/all_gather | solution.py:233
  534.6 61.9 %all-gather.25.cloned.1.call-done = bf16[1,16,256,1152]{3,2,1,0:T(8,128)(2,1)} async-done(((bf16[1,16,16,1152]{3,2,1,0:T(8,128)(2,1)}), bf16[1,16,256,1152]{3,2,1,0:T(8,128)(2,1)}) %all-gather.25.cloned.1.call-update) | async-done | bytes 9437200 | tf_op jit(solution)/shard_map/all_gather | solution.py:234
  618.2 22.8 all-gather.29.cloned.1.call-done
  645.0 85.6 %all-gather.31.cloned.1.call-done = bf16[1152,4608]{1,0:T(8,128)(2,1)} async-done(((bf16[72,4608]{1,0:T(8,128)(2,1)}), bf16[1152,4608]{1,0:T(8,128)(2,1)}) %all-gather.31.cloned.1.call-update) | async-done | bytes 10616848 | tf_op jit(solution)/shard_map/all_gather | solution.py:71
  740.1 80.2 %all-gather.33.cloned.1.call-done = bf16[4608,1152]{1,0:T(8,128)(2,1)} async-done(((bf16[288,1152]{1,0:T(8,128)(2,1)}), bf16[4608,1152]{1,0:T(8,128)(2,1)}) %all-gather.33.cloned.1.call-update) | async-done | bytes 10616848 | tf_op jit(solution)/shard_map/all_gather | solution.py:72
  830.7 62.7 %all-gather.37.cloned.1.call-done = bf16[1152,3456]{1,0:T(8,128)(2,1)} async-done(((bf16[72,3456]{1,0:T(8,128)(2,1)}), bf16[1152,3456]{1,0:T(8,128)(2,1)}) %all-gather.37.cloned.1.call-update) | async-done | bytes 7962640 | tf_op jit(solution)/shard_map/all_gather | solution.py:69
  917.8 20.0 all-gather.39.cloned.1.call-done
  943.4 84.0 %all-gather.41.cloned.1.call-done = bf16[1152,4608]{1,0:T(8,128)(2,1)} async-done(((bf16[72,4608]{1,0:T(8,128)(2,1)}), bf16[1152,4608]{1,0:T(8,128)(2,1)}) %all-gather.41.cloned.1.call-update) | async-done | bytes 10616848 | tf_op jit(solution)/shard_map/all_gather | solution.py:71
  1206.4 36.1 %all_gather.125 = f32[1,16,256,16]{3,1,0,2:T(8,128)} all-gather(f32[1,16,16,16]{3,1,0,2:T(8,128)S(1)} %copy.180), channel_id=1, replica_groups=mesh['patch'=16,'seq'=2] {'patch'}, dimensions={2}, use_global_device_ids=true | all-gather | bytes 278528 | tf_op jit(solution)/shard_map/all_gather | solution.py:291
  1245.9 32.7 %all_gather.123 = f32[1,16,256,16]{3,1,0,2:T(8,128)} all-gather(f32[1,16,16,16]{3,1,0,2:T(8,128)S(1)} %copy.176), channel_id=1, replica_groups=mesh['patch'=16,'seq'=2] {'patch'}, dimensions={2}, use_global_device_ids=true | all-gather | bytes 278528 | tf_op jit(solution)/shard_map/all_gather | solution.py:290
  1410.0 31.5 %reduce-scatter.81.cloned.1.call-done = bf16[72,3456]{1,0:T(8,128)(2,1)} async-done(((bf16[1152,3456]{1,0:T(8,128)(2,1)}), bf16[72,3456]{1,0:T(8,128)(2,1)}) %reduce-scatter.81.cloned.1.call-update) | async-done | bytes 497680
  1443.9 122.2 %reduce-scatter.51.cloned.1.call-done = bf16[288,1152]{1,0:T(8,128)(2,1)} async-done(((bf16[4608,1152]{1,0:T(8,128)(2,1)}), bf16[288,1152]{1,0:T(8,128)(2,1)}) %reduce-scatter.51.cloned.1.call-update) | async-done | bytes 663568 | tf_op jit(solution)/shard_map/reduce_scatter | solution.py:90
  1568.4 122.2 %reduce-scatter.59.cloned.1.call-done = bf16[288,1152]{1,0:T(8,128)(2,1)} async-done(((bf16[4608,1152]{1,0:T(8,128)(2,1)}), bf16[288,1152]{1,0:T(8,128)(2,1)}) %reduce-scatter.59.cloned.1.call-update) | async-done | bytes 663568 | tf_op jit(solution)/shard_map/reduce_scatter | solution.py:90
  1693.0 122.1 %reduce-scatter.47.cloned.1.call-done = bf16[72,4608]{1,0:T(8,128)(2,1)} async-done(((bf16[1152,4608]{1,0:T(8,128)(2,1)}), bf16[72,4608]{1,0:T(8,128)(2,1)}) %reduce-scatter.47.cloned.1.call-update) | async-done | bytes 663568 | tf_op jit(solution)/shard_map/reduce_scatter | solution.py:87
  1815.2 124.5 %reduce-scatter.55.cloned.1.call-done = bf16[72,4608]{1,0:T(8,128)(2,1)} async-done(((bf16[1152,4608]{1,0:T(8,128)(2,1)}), bf16[72,4608]{1,0:T(8,128)(2,1)}) %reduce-scatter.55.cloned.1.call-update) | async-done | bytes 663568 | tf_op jit(solution)/shard_map/reduce_scatter | solution.py:87
  1939.8 105.2 %reduce-scatter.77.cloned.1.call-done = bf16[72,3456]{1,0:T(8,128)(2,1)} async-done(((bf16[1152,3456]{1,0:T(8,128)(2,1)}), bf16[72,3456]{1,0:T(8,128)(2,1)}) %reduce-scatter.77.cloned.1.call-update) | async-done | bytes 497680
  2047.3 173.5 %reduce-scatter.45.cloned.1.call-done = bf16[72,6912]{1,0:T(8,128)(2,1)} async-done(((bf16[1152,6912]{1,0:T(8,128)(2,1)}), bf16[72,6912]{1,0:T(8,128)(2,1)}) %reduce-scatter.45.cloned.1.call-update) | async-done | bytes 995344 | tf_op jit(solution)/shard_map/reduce_scatter | solution.py:78
  2223.5 172.3 %reduce-scatter.53.cloned.1.call-done = bf16[72,6912]{1,0:T(8,128)(2,1)} async-done(((bf16[1152,6912]{1,0:T(8,128)(2,1)}), bf16[72,6912]{1,0:T(8,128)(2,1)}) %reduce-scatter.53.cloned.1.call-update) | async-done | bytes 995344 | tf_op jit(solution)/shard_map/reduce_scatter | solution.py:78
  2398.7 15.2 convolution_reduce_fusion.2
  2447.3 19.4 reduce-scatter.67.cloned.1.call-done
  2468.8 18.7 reduce-scatter.75.cloned.1.call-done
  2489.6 16.1 reduce-scatter.49.cloned.1.call-done
  2507.5 16.6 reduce-scatter.57.cloned.1.call-done
  2526.0 19.6 reduce-scatter.63.cloned.1.call-done
  2547.6 28.3 %reduce-scatter.61.cloned.1.call-done = bf16[3456,72]{1,0:T(8,128)(2,1)} async-done(((bf16[6912,72]{1,0:T(8,128)(2,1)}), bf16[3456,72]{1,0:T(8,128)(2,1)}) %reduce-scatter.61.cloned.1.call-update) | async-done | bytes 497680
  2578.5 28.1 %reduce-scatter.69.cloned.1.call-done = bf16[3456,72]{1,0:T(8,128)(2,1)} async-done(((bf16[6912,72]{1,0:T(8,128)(2,1)}), bf16[3456,72]{1,0:T(8,128)(2,1)}) %reduce-scatter.69.cloned.1.call-update) | async-done | bytes 497680
  2609.1 130.1 %all-reduce.6.cloned.1.call-done = f32[101,1152]{1,0:T(8,128)} async-done(((f32[101,1152]{1,0:T(8,128)}), f32[101,1152]{1,0:T(8,128)}) %all-reduce.6.cloned.1.call-update) | async-done | bytes 465424 | tf_op jit(solution)/shard_map/psum | solution.py:445
  (426 shorter events, 598.6 us)
Async XLA Ops:
  35.2 307.4 %all-gather.35.cloned.1.call-start = ((), (), s32[]{:S(2)}) async-start(), calls=%async_computation.27 | async-start | bytes 16920576 | tf_op jit(solution)/shard_map/all_gather | solution.py:68
  47.7 384.5 %all-gather.43.cloned.1.call-start = ((), (), s32[]{:S(2)}) async-start(), calls=%async_computation.31 | async-start | bytes 11280384 | tf_op jit(solution)/shard_map/all_gather | solution.py:72
  58.3 456.0 %all-gather.27.cloned.1.call-start = ((), (), s32[]{:S(2)}) async-start(), calls=%async_computation.23 | async-start | bytes 10027008 | tf_op jit(solution)/shard_map/all_gather | solution.py:233
  227.5 369.0 %all-gather.25.cloned.1.call-start = ((), (), s32[]{:S(2)}) async-start(), calls=%async_computation.22 | async-start | bytes 10027008 | tf_op jit(solution)/shard_map/all_gather | solution.py:234
  228.1 412.8 %all-gather.29.cloned.1.call-start = ((), (), s32[]{:S(2)}) async-start(), calls=%async_computation.24 | async-start | bytes 2820096 | tf_op jit(solution)/shard_map/all_gather | solution.py:70
  234.7 495.9 %all-gather.31.cloned.1.call-start = ((), (), s32[]{:S(2)}) async-start(), calls=%async_computation.25 | async-start | bytes 11280384 | tf_op jit(solution)/shard_map/all_gather | solution.py:71
  244.8 575.6 %all-gather.33.cloned.1.call-start = ((), (), s32[]{:S(2)}) async-start(), calls=%async_computation.26 | async-start | bytes 11280384 | tf_op jit(solution)/shard_map/all_gather | solution.py:72
  256.7 636.6 %all-gather.37.cloned.1.call-start = ((), (), s32[]{:S(2)}) async-start(), calls=%async_computation.28 | async-start | bytes 8460288 | tf_op jit(solution)/shard_map/all_gather | solution.py:69
  265.5 672.3 %all-gather.39.cloned.1.call-start = ((), (), s32[]{:S(2)}) async-start(), calls=%async_computation.29 | async-start | bytes 2820096 | tf_op jit(solution)/shard_map/all_gather | solution.py:70
  271.8 755.5 %all-gather.41.cloned.1.call-start = ((), (), s32[]{:S(2)}) async-start(), calls=%async_computation.30 | async-start | bytes 11280384 | tf_op jit(solution)/shard_map/all_gather | solution.py:71
  279.8 1001.4 %all-gather.45.cloned.1.call-start = ((), (), s32[]{:S(2)}) async-start(), calls=%async_computation.32 | async-start | bytes 10027008 | tf_op jit(solution)/shard_map/all_gather | solution.py:286
  350.3 952.0 %all-gather.47.cloned.1.call-start = ((), (), s32[]{:S(2)}) async-start(), calls=%async_computation.33 | async-start | bytes 10027008 | tf_op jit(solution)/shard_map/all_gather | solution.py:287
  1111.7 294.5 %reduce-scatter.79.cloned.1.call-start = ((), (), s32[]{:S(2)}) async-start(), calls=%async_computation.52 | async-start | bytes 2820096
  1120.5 321.0 %reduce-scatter.81.cloned.1.call-start = ((), (), s32[]{:S(2)}) async-start(), calls=%async_computation.53 | async-start | bytes 8460288
  1127.8 438.2 %reduce-scatter.51.cloned.1.call-start = ((), (), s32[]{:S(2)}) async-start(), calls=%async_computation.38 | async-start | bytes 11280384 | tf_op jit(solution)/shard_map/reduce_scatter | solution.py:90
  1139.8 550.9 %reduce-scatter.59.cloned.1.call-start = ((), (), s32[]{:S(2)}) async-start(), calls=%async_computation.42 | async-start | bytes 11280384 | tf_op jit(solution)/shard_map/reduce_scatter | solution.py:90
  1151.3 663.8 %reduce-scatter.47.cloned.1.call-start = ((), (), s32[]{:S(2)}) async-start(), calls=%async_computation.36 | async-start | bytes 11280384 | tf_op jit(solution)/shard_map/reduce_scatter | solution.py:87
  1160.2 779.6 %reduce-scatter.55.cloned.1.call-start = ((), (), s32[]{:S(2)}) async-start(), calls=%async_computation.40 | async-start | bytes 11280384 | tf_op jit(solution)/shard_map/reduce_scatter | solution.py:87
  1170.2 874.8 %reduce-scatter.77.cloned.1.call-start = ((), (), s32[]{:S(2)}) async-start(), calls=%async_computation.51 | async-start | bytes 8460288
  1355.2 865.6 %reduce-scatter.45.cloned.1.call-start = ((), (), s32[]{:S(2)}) async-start(), calls=%async_computation.35 | async-start | bytes 16920576 | tf_op jit(solution)/shard_map/reduce_scatter | solution.py:78
  1405.6 990.3 %reduce-scatter.53.cloned.1.call-start = ((), (), s32[]{:S(2)}) async-start(), calls=%async_computation.39 | async-start | bytes 16920576 | tf_op jit(solution)/shard_map/reduce_scatter | solution.py:78
  1406.2 1024.1 %reduce-scatter.65.cloned.1.call-start = ((), (), s32[]{:S(2)}) async-start(), calls=%async_computation.45 | async-start | bytes 442368
  1408.1 1024.0 %reduce-scatter.73.cloned.1.call-start = ((), (), s32[]{:S(2)}) async-start(), calls=%async_computation.49 | async-start | bytes 442368
  1410.0 1035.2 %reduce-scatter.71.cloned.1.call-start = ((), (), s32[]{:S(2)}) async-start(), calls=%async_computation.48 | async-start | bytes 1327104
  1443.8 1022.8 %reduce-scatter.67.cloned.1.call-start = ((), (), s32[]{:S(2)}) async-start(), calls=%async_computation.46 | async-start | bytes 1327104
  1568.4 919.1 %reduce-scatter.75.cloned.1.call-start = ((), (), s32[]{:S(2)}) async-start(), calls=%async_computation.50 | async-start | bytes 1327104
  1693.0 812.7 %reduce-scatter.49.cloned.1.call-start = ((), (), s32[]{:S(2)}) async-start(), calls=%async_computation.37 | async-start | bytes 995328 | tf_op jit(solution)/shard_map/reduce_scatter | solution.py:104
  1815.1 709.0 %reduce-scatter.57.cloned.1.call-start = ((), (), s32[]{:S(2)}) async-start(), calls=%async_computation.41 | async-start | bytes 995328 | tf_op jit(solution)/shard_map/reduce_scatter | solution.py:104
  1939.8 605.8 %reduce-scatter.63.cloned.1.call-start = ((), (), s32[]{:S(2)}) async-start(), calls=%async_computation.44 | async-start | bytes 1327104
  2047.2 528.7 %reduce-scatter.61.cloned.1.call-start = ((), (), s32[]{:S(2)}) async-start(), calls=%async_computation.43 | async-start | bytes 2654208
  2223.4 383.1 %reduce-scatter.69.cloned.1.call-start = ((), (), s32[]{:S(2)}) async-start(), calls=%async_computation.47 | async-start | bytes 2654208
  2398.4 340.7 %all-reduce.6.cloned.1.call-start = ((), (), s32[]{:S(2)}) async-start(), calls=%async_computation.34 | async-start | bytes 958464 | tf_op jit(solution)/shard_map/psum | solution.py:445
  (83 other events, 2100.7 us)
Sparse Core Ops, SparseCore 0:
  25.5 121.8 all-gather.20
  150.1 70.3 all-gather.22
  222.7 119.8 all-gather.34
  345.3 86.8 all-gather.42
  434.8 79.4 all-gather.26
  516.9 79.5 all-gather.24
  599.2 41.6 all-gather.28
  643.2 87.3 all-gather.30
  733.5 86.8 all-gather.32
  823.0 70.3 all-gather.36
  896.1 41.6 all-gather.38
  939.9 87.3 all-gather.40
  1030.1 79.4 all-gather.44
  1112.2 79.5 all-gather.46
  1195.5 75.2 reduce-scatter.78
  1275.1 62.6 reduce-scatter.82
  1341.8 99.7 reduce-scatter.80
  1446.0 119.9 reduce-scatter.50
  1570.6 119.9 reduce-scatter.58
  1695.1 119.9 reduce-scatter.46
  1819.7 119.9 reduce-scatter.54
  1944.4 100.5 reduce-scatter.76
  2049.1 171.6 reduce-scatter.44
  2224.8 170.9 reduce-scatter.52
  2426.7 18.5 reduce-scatter.70
  2448.1 18.5 reduce-scatter.66
  2468.9 18.5 reduce-scatter.74
  2508.0 16.0 reduce-scatter.56
  2527.0 18.5 reduce-scatter.62
  2547.7 28.2 reduce-scatter.60
  2578.3 28.2 reduce-scatter.68
  2612.4 126.6 all-reduce.5
  (3 shorter events, 39.1 us)
where the time goes:
time: 2760 us; the launch traced here: 2750 us
  waiting for transfers between devices  2040 us (74%)
  matrix products  296 us (11%)
  local copies, waits for them, and re-layouts  180 us (7%)
  blocking collectives  162 us (6%)
  other arithmetic  46.7 us (2%)
    reduce_scatter x2, waiting for transfers between devices, reduce_grads(): lax.psum_scatter(grad_mod.astype(jnp.bfloat16), 'patch', scatter_dimensio...  346 us
    unnamed x47, waiting for transfers between devices  264 us
    reduce_scatter x2, waiting for transfers between devices, reduce_grads(): lax.psum_scatter(grad_up.astype(jnp.bfloat16), 'patch', scatter_dimension...  247 us
    reduce_scatter x2, waiting for transfers between devices, reduce_grads(): lax.psum_scatter(grad_down.astype(jnp.bfloat16), 'patch', scatter_dimensi...  244 us
    dot_general x27, matrix products, matmul(): return jnp.dot(left, right, preferred_element_type=jnp.float32)  193 us
    all_gather x2, waiting for transfers between devices, fetch_weights(): lax.all_gather(wide[3], 'patch', axis=0, tiled=True)  170 us
    all_gather x2, waiting for transfers between devices, fetch_weights(): lax.all_gather(wide[4], 'patch', axis=0, tiled=True)  162 us
    all_gather x2, waiting for transfers between devices, fetch_weights(): lax.all_gather(wide[0], 'patch', axis=0, tiled=True)  146 us
  transfers between devices with their start and end apart: 35, of which 29 were waited for; matrix products, arithmetic and copies ran while one was open for 18% of the time, Pallas kernels for 0%

commit v1 on v0

v1 whole, which is shorter than its diff:
```python
import math
from functools import partial

import jax
import jax.numpy as jnp
from jax import lax
from jax.experimental import pallas as pl
from jax.experimental.pallas import tpu as pltpu
from jax.sharding import Mesh
from jax.sharding import PartitionSpec as P

HEADS = 16
EPSILON = 1e-06
PRECISE = lax.Precision.HIGHEST
LOW = jnp.bfloat16
FULL = jnp.float32


def time_features(step_ids, features):
    half_width = features // 2
    frequency = jnp.exp(-math.log(10000.0) * jnp.arange(half_width, dtype=FULL) / half_width)
    angles = step_ids.astype(FULL)[:, None] * frequency[None, :]
    return jnp.concatenate([jnp.cos(angles), jnp.sin(angles)], axis=-1)


def normalize(values):
    centred = values - jnp.mean(values, axis=-1, keepdims=True)
    inverse = lax.rsqrt(jnp.mean(centred * centred, axis=-1, keepdims=True) + EPSILON)
    return centred * inverse, inverse


def normalize_back(grad_norm, normed, inverse):
    return inverse * (
        grad_norm
        - jnp.mean(grad_norm, axis=-1, keepdims=True)
        - normed * jnp.mean(grad_norm * normed, axis=-1, keepdims=True)
    )


def matmul(left, right):
    return jnp.dot(left, right, preferred_element_type=FULL)


def matmul_nt(left, right):
    return lax.dot_general(left, right, (((1,), (1,)), ((), ())), preferred_element_type=FULL)


def matmul_tn(left, right):
    return lax.dot_general(left, right, (((0,), (0,)), ((), ())), preferred_element_type=FULL)


def in_order(pieces, first):
    count = len(pieces)
    return [lax.select_n((k - first) % count, *pieces) for k in range(count)]


def pick(array, axis, index):
    return lax.dynamic_index_in_dim(array, index, axis, keepdims=False)


LIMIT = 60 * 2**20
CHIPS_Y = 2


def at_rows(index, rows):
    return pl.ds(pl.multiple_of(index * rows, 16), rows)


class Weight:
    def __init__(self, depth, rows, cols, strips):
        self.depth, self.rows, self.cols, self.strips = depth, rows, cols, strips
        self.width = -(-cols // 128) * 128 if strips[0][1] is None else cols
        self.arrays = []
        for strip in strips:
            for array in strip[0]:
                if not any(array is other for other in self.arrays):
                    self.arrays.append(array)

    def scratch(self):
        return [
            pltpu.VMEM((2, 2, 2 * self.depth * self.rows, self.width), LOW),
            pltpu.SemaphoreType.DMA((2, 2, 2, self.depth * len(self.strips))),
        ]

    def copies(self, where, refs, held, sems):
        found = []
        for half in range(2):
            for side in range(2):
                group = []
                x = lax.rem(where[3] + side, 2)
                for turn in range(2):
                    y = lax.rem(where[1] + turn, 2)
                    for ahead in range(self.depth):
                        z = lax.rem(where[0] + ahead, self.depth)
                        at = (z * CHIPS_Y + y) * self.rows
                        base = 0
                        for number, strip in enumerate(self.strips):
                            arrays, x_first, source_lane, row, rows, lane, lanes = strip
                            if x_first is None:
                                core = lax.rem(where[2] + half, 2)
                                source = refs[0].at[
                                    z, y, core, x, :, source_lane : source_lane + lanes
                                ]
                            else:
                                first, second = (side, turn) if x_first else (turn, side)
                                source = refs[base + 2 * half + second].at[first, ahead]
                                base += 4
                            start = pl.multiple_of(at + row, 16)
                            target = held.at[half, x, pl.ds(start, rows), lane : lane + lanes]
                            sem = sems.at[half, side, turn, ahead * len(self.strips) + number]
                            group.append(pltpu.make_async_copy(source, target, sem))
                found.append(group)
        return found


def start_all(copies):
    for copy in copies:
        copy.start()


def wait_all(copies):
    for copy in copies:
        copy.wait()


def dot(left, right):
    return lax.dot_general(left, right, (((1,), (0,)), ((), ())), preferred_element_type=FULL)


def dot_nt(left, right):
    return lax.dot_general(left, right, (((1,), (1,)), ((), ())), preferred_element_type=FULL)


def dot_tn(left, right):
    return lax.dot_general(left, right, (((0,), (0,)), ((), ())), preferred_element_type=FULL)


def call(body, where, ins, outs, scratch, flops, name, after=()):
    count = len(ins)

    def kernel(where_ref, *refs):
        body(where_ref, *refs[:count], *refs[count + len(after) :])

    vmem = pl.BlockSpec(memory_space=pltpu.VMEM)
    hbm = pl.BlockSpec(memory_space=pl.ANY)
    size = sum(a.size * a.dtype.itemsize for a, _ in ins)
    size += sum(math.prod(o.shape) * o.dtype.itemsize for o in outs)
    return pl.pallas_call(
        kernel,
        out_shape=outs,
        in_specs=[pl.BlockSpec(memory_space=pltpu.SMEM)]
        + [vmem if inside else hbm for _, inside in ins]
        + [hbm] * len(after),
        out_specs=[vmem] * len(outs),
        scratch_shapes=scratch,
        compiler_params=pltpu.CompilerParams(vmem_limit_bytes=LIMIT),
        cost_estimate=pl.CostEstimate(flops=flops, bytes_accessed=size, transcendentals=0),
        name=name,
    )(where, *[a for a, _ in ins], *after)


def shape(dims, dtype):
    return jax.ShapeDtypeStruct(dims, dtype)


def norm_qkv(where, rows, mods, weight, cols):
    count, features = rows.shape
    many = len(weight.arrays)
    thin = weight.cols - cols
    chips = 2 * weight.depth
    part = weight.rows // 2

    def body(where, rows, mods, *refs):
        sources, (hidden, out_weight, out, held, sems) = refs[:many], refs[many:]
        copies = weight.copies(where, sources, held, sems)
        for group in copies:
            start_all(group)
        normed, _ = normalize(rows[...].astype(FULL))
        value = (normed * (1.0 + mods[1:2]) + mods[0:1]).astype(LOW)
        hidden[...] = value
        for half in range(2):
            for side in range(2):
                x = lax.rem(where[3] + side, 2)
                wait_all(copies[2 * half + side])
                out[2 * half + x] = dot(value, held[half, x, :, :cols]).astype(LOW)
                strips = held[half, x, :, cols:].astype(FULL).reshape(chips, 2, part, thin)
                both = [strips[:, k].reshape(chips * part, thin) for k in range(2)]
                out_weight[2 * half + x] = jnp.concatenate(both, axis=1).astype(LOW)

    return call(
        body,
        where,
        [(rows, True), (mods, True)] + [(w, False) for w in weight.arrays],
        [
            shape((count, features), LOW),
            shape((4, chips * part, 2 * thin), LOW),
            shape((4, count, cols), LOW),
        ],
        weight.scratch(),
        8 * count * features * cols,
        "norm_qkv",
    )


def head_slices(qkv, half, number, heads, head):
    def column(slot):
        per = 3 * heads // 2
        x, at = divmod(slot, per)
        return qkv[2 * half + x, :, at * head : (at + 1) * head]

    return column(number), column(heads + number), column(2 * heads + number)


def probabilities(query, key, mask, factor):
    scores = dot_nt(key, query) * factor
    if mask is not None:
        scores = jnp.where(mask, scores, -1e30)
    weights = jnp.exp(scores - jnp.max(scores, axis=0, keepdims=True))
    return weights * (1.0 / jnp.sum(weights, axis=0, keepdims=True))


def attend_kernel(where, qkv, marks, head):
    _, count, cols = qkv.shape
    heads = 2 * cols // (3 * head)

    def body(where, qkv, *refs):
        mask = None
        if marks is not None:
            mask = refs[0][...] == refs[1][...]
        out = refs[-1]
        for half in range(2):
            mixed = []
            for number in range(heads):
                query, key, value = head_slices(qkv, half, number, heads, head)
                probs = probabilities(query, key, mask, head ** (-0.5)).astype(LOW)
                mixed.append(dot_tn(value, probs))
            out[half] = jnp.concatenate(mixed, axis=0).T.astype(LOW)

    ins = [(qkv, True)] + ([] if marks is None else [(m, True) for m in marks])
    return call(
        body,
        where,
        ins,
        [shape((2, count, heads * head), LOW)],
        [],
        8 * heads * count * count * head,
        "attend",
    )[0]


def out_norm(where, rows, mods, attended, weight):
    count, features = rows.shape

    def body(where, rows, mods, attended, weight, branch, middle, hidden):
        value = jnp.concatenate(
            [dot(attended[0], weight[x]) + dot(attended[1], weight[2 + x]) for x in range(2)],
            axis=1,
        )
        branch[...] = value
        total = rows[...].astype(FULL) + mods[2:3] * value
        middle[...] = total
        normed, _ = normalize(total)
        hidden[...] = (normed * (1.0 + mods[4:5]) + mods[3:4]).astype(LOW)

    dims = (count, features)
    return call(
        body,
        where,
        [(rows, True), (mods, True), (attended, True), (weight, True)],
        [shape(dims, FULL), shape(dims, FULL), shape(dims, LOW)],
        [],
        2 * count * features * features,
        "out_norm",
    )


GELU_A = math.sqrt(2.0 / math.pi)
GELU_B = 0.044715


def gelu(value):
    inner = GELU_A * (value + GELU_B * value * value * value)
    return 0.5 * value * (1.0 + jnp.tanh(inner))


def gelu_slope(value):
    square = value * value
    bend = jnp.tanh(GELU_A * (value + GELU_B * square * value))
    return 0.5 * (1.0 + bend) + 0.5 * value * (1.0 - bend * bend) * GELU_A * (
        1.0 + 3.0 * GELU_B * square
    )


def up_gelu(where, hidden, weight):
    count, features = hidden.shape
    cols, many = weight.cols, len(weight.arrays)

    def body(where, hidden, *refs):
        sources, (pre, act, held, sems) = refs[:many], refs[many:]
        copies = weight.copies(where, sources, held, sems)
        for group in copies:
            start_all(group)
        value = hidden[...]
        for half in range(2):
            for side in range(2):
                x = lax.rem(where[3] + side, 2)
                wait_all(copies[2 * half + side])
                before = dot(value, held[half, x])
                pre[2 * half + x] = before.astype(LOW)
                act[2 * half + x] = gelu(before).astype(LOW)

    return call(
        body,
        where,
        [(hidden, True)] + [(w, False) for w in weight.arrays],
        [shape((4, count, cols), LOW), shape((4, count, cols), LOW)],
        weight.scratch(),
        8 * count * features * cols,
        "up_gelu",
    )


def by_place(first, pair):
    return [jnp.where(first, pair[0], pair[1]), jnp.where(first, pair[1], pair[0])]


def down_add(where, act, weight, middle, mods):
    count, features = middle.shape
    wide, many = act.shape[-1], len(weight.arrays)

    def body(where, act, middle, mods, *refs):
        sources, (mlp, out, held, sems) = refs[:many], refs[many:]
        copies = weight.copies(where, sources, held, sems)
        for group in copies:
            start_all(group)
        totals = [None, None]
        for half in range(2):
            for side in range(2):
                place = lax.rem(where[3] + side, 2)
                wait_all(copies[2 * half + side])
                for x in range(2):
                    part = dot(act[2 * half + x], held[half, place, x * wide : (x + 1) * wide])
                    totals[side] = part if totals[side] is None else totals[side] + part
        sides = by_place(where[3] == 0, [t[:, : weight.cols] for t in totals])
        total = jnp.concatenate(sides, axis=1)
        mlp[...] = total
        out[...] = (middle[...] + mods[5:6] * total).astype(LOW)

    return call(
        body,
        where,
        [(act, True), (middle, True), (mods, True)] + [(w, False) for w in weight.arrays],
        [shape((count, features), FULL), shape((count, features), LOW)],
        weight.scratch(),
        8 * count * features * wide,
        "down_add",
    )


def column_sums(*values):
    sums = [jnp.sum(v, axis=0, keepdims=True) for v in values]
    fill = jnp.zeros((8 - len(sums), sums[0].shape[1]), FULL)
    return jnp.concatenate(sums + [fill], axis=0)


def mlp_back(where, grad, mods, pre, middle, branch, mlp, up, down):
    count, features = grad.shape
    wide = pre.shape[-1]
    cols = down.cols
    many_up, many_down = len(up.arrays), len(down.arrays)
    shared = up.arrays[0] is down.arrays[0]

    def body(where, grad, mods, pre, middle, branch, mlp, *refs):
        ups = refs[:many_up]
        refs = refs[many_up:]
        downs = ups
        if not shared:
            downs, refs = refs[:many_down], refs[many_down:]
        grad_mid, grad_pre, grad_branch, sums, up_held, up_sems, down_held, down_sems = refs
        down_copies = down.copies(where, downs, down_held, down_sems)
        up_copies = up.copies(where, ups, up_held, up_sems)
        for half in range(2):
            start_all(down_copies[2 * half])
            start_all(down_copies[2 * half + 1])
            start_all(up_copies[2 * half])
            start_all(up_copies[2 * half + 1])
        incoming = grad[...].astype(FULL)
        grad_mlp = (mods[5:6] * incoming).astype(LOW)
        sides = [grad_mlp[:, s * cols : (s + 1) * cols] for s in range(2)]
        total = None
        for half in range(2):
            wait_all(down_copies[2 * half] + down_copies[2 * half + 1])
            for side in range(2):
                x = lax.rem(where[3] + side, 2)
                rows = pl.ds(pl.multiple_of(x * wide, 16), wide)
                grad_act = dot_nt(sides[0], down_held[half, 0, rows, :cols]) + dot_nt(
                    sides[1], down_held[half, 1, rows, :cols]
                )
                slope = gelu_slope(pre[2 * half + x].astype(FULL))
                value = (slope * grad_act).astype(LOW)
                grad_pre[2 * half + x] = value
                wait_all(up_copies[2 * half + side])
                part = dot_nt(value, up_held[half, x])
                total = part if total is None else total + part
        normed, inverse = normalize(middle[...])
        result = incoming + normalize_back(total * (1.0 + mods[4:5]), normed, inverse)
        grad_mid[...] = result
        scaled = (mods[2:3] * result).astype(LOW)
        for s in range(2):
            grad_branch[s] = scaled[:, s * cols : (s + 1) * cols]
        sums[...] = column_sums(result * branch[...], total, total * normed, incoming * mlp[...])

    arrays = up.arrays + ([] if shared else down.arrays)
    return call(
        body,
        where,
        [(a, True) for a in (grad, mods, pre, middle, branch, mlp)] + [(w, False) for w in arrays],
        [
            shape((count, features), FULL),
            shape(pre.shape, LOW),
            shape((2, count, cols), LOW),
            shape((8, features), FULL),
        ],
        up.scratch() + down.scratch(),
        16 * count * features * wide,
        "mlp_back",
    )


def scale_halves(where, grad, mods):
    count, features = grad.shape

    def body(where, grad, mods, out):
        value = (mods[5:6] * grad[...].astype(FULL)).astype(LOW)
        for side in range(2):
            out[side] = value[:, side * features // 2 : (side + 1) * features // 2]

    return call(
        body,
        where,
        [(grad, True), (mods, True)],
        [shape((2, count, features // 2), LOW)],
        [],
        0,
        "scale_halves",
    )[0]


def attend_back_kernel(where, grad_branch, weight, qkv, marks, head):
    _, count, cols = qkv.shape
    heads = 2 * cols // (3 * head)
    factor = head ** (-0.5)

    def body(where, grad_branch, weight, qkv, *refs):
        mask = None
        if marks is not None:
            mask = refs[0][...] == refs[1][...]
        out = refs[-1]
        pieces = [[None] * (3 * heads) for _ in range(2)]
        for half in range(2):
            grads = dot_nt(grad_branch[0], weight[2 * half]) + dot_nt(
                grad_branch[1], weight[2 * half + 1]
            )
            grads = grads.astype(LOW)
            for number in range(heads):
                grad = grads[:, number * head : (number + 1) * head]
                query, key, value = head_slices(qkv, half, number, heads, head)
                probs = probabilities(query, key, mask, factor)
                grad_probs = dot_nt(value, grad)
                delta = jnp.sum(grad_probs * probs, axis=0, keepdims=True)
                grad_scores = (probs * (grad_probs - delta)).astype(LOW)
                pieces[half][number] = (dot_tn(key, grad_scores).T * factor).astype(LOW)
                pieces[half][heads + number] = (dot(grad_scores, query) * factor).astype(LOW)
                pieces[half][2 * heads + number] = dot(probs.astype(LOW), grad).astype(LOW)
        per = 3 * heads // 2
        for half in range(2):
            for x in range(2):
                out[2 * half + x] = jnp.concatenate(
                    pieces[half][x * per : (x + 1) * per], axis=1
                )

    ins = [(grad_branch, True), (weight, True), (qkv, True)]
    ins += [] if marks is None else [(m, True) for m in marks]
    return call(
        body,
        where,
        ins,
        [shape(qkv.shape, LOW)],
        [],
        20 * heads * count * count * head,
        "attend_back",
    )[0]


def qkv_back(where, grad_qkv, weight, rows, mods, grad_mid):
    count, features = rows.shape
    cols, many = grad_qkv.shape[-1], len(weight.arrays)

    def body(where, grad_qkv, rows, mods, grad_mid, *refs):
        sources, (out, sums, held, sems) = refs[:many], refs[many:]
        copies = weight.copies(where, sources, held, sems)
        for group in copies:
            start_all(group)
        total = None
        for half in range(2):
            for side in range(2):
                x = lax.rem(where[3] + side, 2)
                wait_all(copies[2 * half + side])
                part = dot_nt(grad_qkv[2 * half + x], held[half, x, :, :cols])
                total = part if total is None else total + part
        normed, inverse = normalize(rows[...].astype(FULL))
        result = grad_mid[...] + normalize_back(total * (1.0 + mods[1:2]), normed, inverse)
        out[...] = result.astype(LOW)
        sums[...] = column_sums(total, total * normed)

    return call(
        body,
        where,
        [(grad_qkv, True), (rows, True), (mods, True), (grad_mid, True)]
        + [(w, False) for w in weight.arrays],
        [shape((count, features), LOW), shape((8, features), FULL)],
        weight.scratch(),
        8 * count * features * cols,
        "qkv_back",
    )


def weight_grad(where, left, right, tail, depth, x_first, half, added):
    blocks, count, wide = left.shape
    blocks = min(blocks, 2)
    rows = blocks * wide // (2 * depth)
    cols = right.shape[-1]
    pairs = [(left, right)]
    if tail is not None:
        pairs.append(tail)
        cols += tail[1].shape[-1] // 2

    def kernel(where, *refs):
        lefts, rights = refs[0 : 2 * len(pairs) : 2], refs[1 : 2 * len(pairs) : 2]
        refs = refs[2 * len(pairs) :]
        far_in, near_in = refs[:2] if added else (None, None)
        refs = refs[2 * (added is not None) :]
        far, near, *flips = refs
        step = pl.program_id(0)

        @pl.when(step == 0)
        def _():
            for source, flipped in zip(lefts, flips):
                size = source.shape[-1]
                for block in range(source.shape[0]):
                    flipped[block * size : (block + 1) * size] = source[block].T

        z = lax.rem(where[0] + step, depth)
        chosen = []
        for flipped in flips:
            size = flipped.shape[0] // depth
            chosen.append(flipped[pl.ds(pl.multiple_of(z * size, 16), size)])

        def product(x):
            value = dot(chosen[0], rights[0][x]).reshape(2, rows, -1)
            if tail is None:
                return [value[0], value[1]]
            more = dot(chosen[1], rights[1][x])
            size, thin = more.shape[0] // 2, more.shape[1] // 2
            found = []
            for y in range(2):
                part = more[y * size : (y + 1) * size]
                strips = jnp.concatenate([part[:, :thin], part[:, thin:]], axis=0)
                found.append(jnp.concatenate([value[y], strips], axis=1))
            return found

        def put(to, place, value, extra):
            if extra is not None:
                value = value + extra[place, 0].astype(FULL)
            to[place, 0] = value.astype(LOW)

        if x_first:
            for to, x, extra in ((far, 1 - where[3], far_in), (near, where[3], near_in)):
                value = product(x)
                for y in range(2):
                    put(to, y, value[y], extra)
        else:
            for x in range(2):
                value = by_place(where[1] == 0, product(x))
                put(near, x, value[0], near_in)
                put(far, x, value[1], far_in)

    def whole(a):
        place = half if a.shape[0] == 4 or (a.shape[0] == 2 and tail is not None and a is tail[0]) else 0
        size = 1 if tail is not None and a is tail[0] else min(a.shape[0], 2)
        return pl.BlockSpec((size,) + a.shape[1:], lambda i, s: (place, 0, 0))

    moving = pl.BlockSpec((2, 1, rows, cols), lambda i, s: (0, i, 0, 0))
    out = shape((2, depth, rows, cols), LOW)
    extra = list(added) if added else []
    operands = [a for pair in pairs for a in pair]
    scratch = [pltpu.VMEM((blocks * wide, count), LOW)]
    if tail is not None:
        scratch.append(pltpu.VMEM((tail[0].shape[-1], count), LOW))
    return pl.pallas_call(
        kernel,
        out_shape=[out, out],
        grid_spec=pltpu.PrefetchScalarGridSpec(
            num_scalar_prefetch=1,
            grid=(depth,),
            in_specs=[whole(a) for a in operands] + [moving] * len(extra),
            out_specs=[moving, moving],
            scratch_shapes=scratch,
        ),
        compiler_params=pltpu.CompilerParams(vmem_limit_bytes=LIMIT),
        cost_estimate=pl.CostEstimate(
            flops=4 * count * blocks * wide * cols,
            bytes_accessed=4 * depth * rows * cols * (4 if added else 2),
            transcendentals=0,
        ),
        name="weight_grad",
    )(where, *operands, *extra)


def add_split(where, near, came, mine):
    _, depth, rows, cols = near.shape

    def kernel(where, near_far, came_far, near_own, came_own, far, own):
        far[...] = (near_far[...].astype(FULL) + came_far[...].astype(FULL)).astype(LOW)
        own[...] = (near_own[...].astype(FULL) + came_own[...].astype(FULL)).astype(LOW)

    def block(other):
        return pl.BlockSpec(
            (pl.squeezed, 1, rows, cols),
            lambda i, s: (1 - s[mine] if other else s[mine], i, 0, 0),
        )

    moving = pl.BlockSpec((1, rows, cols), lambda i, s: (i, 0, 0))
    out = shape((depth, rows, cols), LOW)
    return pl.pallas_call(
        kernel,
        out_shape=[out, out],
        grid_spec=pltpu.PrefetchScalarGridSpec(
            num_scalar_prefetch=1,
            grid=(depth,),
            in_specs=[block(True), block(True), block(False), block(False)],
            out_specs=[moving, moving],
        ),
        compiler_params=pltpu.CompilerParams(vmem_limit_bytes=LIMIT),
        cost_estimate=pl.CostEstimate(
            flops=0, bytes_accessed=12 * depth * rows * cols, transcendentals=0
        ),
        name="add_split",
    )(where, near, came, near, came)


def add_planes(where, near, came):
    depth, rows, cols = near.shape

    def body(where, near, came, own, *others):
        own[...] = near[0].astype(FULL) + came[0].astype(FULL)
        for ahead, out in enumerate(others):
            total = near[ahead + 1].astype(FULL) + came[ahead + 1].astype(FULL)
            out[...] = total.astype(LOW)

    return call(
        body,
        where,
        [(near, True), (came, True)],
        [shape((rows, cols), FULL)] + [shape((rows, cols), LOW)] * (depth - 1),
        [],
        0,
        "add_planes",
    )


def add_last(where, own, came, cols):
    rows, wide = own.shape
    part, thin = rows // 2, wide - cols

    def body(where, own, *refs):
        total = own[...]
        came, outs = refs[: -3 if thin else -2], refs[-3 if thin else -2 :]
        for ref in came:
            total = total + ref[...].astype(FULL)
        first = where[2] == 0
        mine, theirs = by_place(first, [total[:part, :cols], total[part:, :cols]])
        if thin:
            outs[0][...] = jnp.concatenate([total[:part, cols:], total[part:, cols:]], axis=1)
        outs[-2][...] = mine
        outs[-1][...] = theirs.astype(LOW)

    outs = [shape((part, cols), FULL), shape((part, cols), LOW)]
    if thin:
        outs.insert(0, shape((part, 2 * thin), FULL))
    return call(
        body,
        where,
        [(own, True)] + [(c, True) for c in came],
        outs,
        [],
        0,
        "add_last",
    )


def interleave(where, mine, theirs, width):
    rows, cols = mine.shape

    def body(where, mine, theirs, out):
        both = by_place(where[2] == 0, [mine[...], theirs[...].astype(FULL)])
        groups = []
        for at in range(0, cols, width):
            groups += [b[:, at : at + width] for b in both]
        out[...] = jnp.concatenate(groups, axis=1)

    return call(
        body,
        where,
        [(mine, True), (theirs, True)],
        [shape((rows, 2 * cols), FULL)],
        [],
        0,
        "interleave",
    )[0]


def deal(where, shards, widths):
    rows = shards[0].shape[0]
    cols = sum(a.shape[1] for a in shards) // 2

    def body(where, *refs):
        own, other = refs[-2:]
        halves = [[], []]
        for ref, width in zip(refs, widths):
            value = ref[...]
            for number in range(value.shape[1] // width):
                halves[number % 2].append(value[:, number * width : (number + 1) * width])
        pair = [jnp.concatenate(h, axis=1) for h in halves]
        own[...], other[...] = by_place(where[2] == 0, pair)

    return call(
        body,
        where,
        [(a, True) for a in shards],
        [shape((rows, cols), LOW)] * 2,
        [],
        0,
        "deal",
    )


def pack(where, own, got, outs, down, cols):
    part = own.shape[0]
    rows = 2 * part
    thin = outs[0].shape[1] // 2
    wide = down.shape[1]
    padded = -(-wide // 128) * 128
    first = cols[0] + thin

    def body(where, own, got, out_s, out_t, down, qkv_s, up_s, packed):
        pair = by_place(where[2] == 0, [own[...].astype(FULL), got[...].astype(FULL)])
        both = jnp.concatenate(pair, axis=0)

        def strips(ref):
            value = ref[...].astype(FULL)
            return jnp.concatenate([value[:, :thin], value[:, thin:]], axis=0)

        at = cols[0] + cols[1]
        qkv_s[...] = jnp.concatenate([both[:, : cols[0]], strips(out_s)], axis=1).astype(LOW)
        up_s[...] = both[:, cols[0] : at].astype(LOW)
        qkv_t = jnp.concatenate([both[:, at : at + cols[0]], strips(out_t)], axis=1)
        packed[:, :first] = qkv_t.astype(LOW)
        packed[:, first : first + cols[1]] = both[:, at + cols[0] :].astype(LOW)
        for k in range(down.shape[0] // rows):
            lane = first + cols[1] + k * padded
            packed[:, lane : lane + wide] = down[k * rows : (k + 1) * rows]
            if padded > wide:
                packed[:, lane + wide : lane + padded] = jnp.zeros((rows, padded - wide), LOW)

    total = first + cols[1] + down.shape[0] // rows * padded
    return call(
        body,
        where,
        [(a, True) for a in (own, got, *outs, down)],
        [shape((rows, first), LOW), shape((rows, cols[1]), LOW), shape((rows, total), LOW)],
        [],
        0,
        "pack",
    )


def down_grad(where, act, grad_mlp, depth):
    _, count, wide = act.shape
    cols = grad_mlp.shape[-1]
    rows = wide // depth

    def kernel(where, act, grad_mlp, out, flipped):
        step = pl.program_id(0)

        @pl.when(step == 0)
        def _():
            for half in range(2):
                for block in range(2):
                    flipped[half, block * wide : (block + 1) * wide] = act[2 * half + block].T

        for half in range(2):
            core = lax.rem(where[2] + half, 2)
            chosen = flipped[half, at_rows(step, 2 * rows)]
            for x in range(2):
                value = dot(chosen, grad_mlp[x]).astype(LOW)
                for y in range(2):
                    out[0, y, core, x] = value[y * rows : (y + 1) * rows]

    def whole(a):
        return pl.BlockSpec(a.shape, lambda i, s: (0,) * len(a.shape))

    dims = (depth, 2, 2, 2, rows, cols)
    return pl.pallas_call(
        kernel,
        out_shape=shape(dims, LOW),
        grid_spec=pltpu.PrefetchScalarGridSpec(
            num_scalar_prefetch=1,
            grid=(depth,),
            in_specs=[whole(act), whole(grad_mlp)],
            out_specs=pl.BlockSpec((1,) + dims[1:], lambda i, s: (i, 0, 0, 0, 0, 0)),
            scratch_shapes=[pltpu.VMEM((2, 2 * wide, count), LOW)],
        ),
        compiler_params=pltpu.CompilerParams(vmem_limit_bytes=LIMIT),
        cost_estimate=pl.CostEstimate(
            flops=16 * count * wide * cols,
            bytes_accessed=16 * depth * rows * cols,
            transcendentals=0,
        ),
        name="down_grad",
    )(where, act, grad_mlp)


class Grid:
    def __init__(self, patch, seq, patch_axes, seq_axis):
        self.patch_axes, self.seq_axis = patch_axes, seq_axis
        self.every = (patch_axes if isinstance(patch_axes, tuple) else (patch_axes,)) + (seq_axis,)
        self.patch, self.seq = patch, seq
        self.depth = patch // 4
        where = lax.axis_index(patch_axes)
        self.place = where
        self.core = where % 2
        self.y = (where // 2) % 2
        self.z = where // 4
        self.x = lax.axis_index(seq_axis)

    def moves(self, step):
        pairs = []
        for p in range(self.patch):
            for x in range(self.seq):
                z, y, c = p // 4, (p // 2) % 2, p % 2
                z2, y2, c2, x2 = step(z, y, c, x)
                pairs.append((p * self.seq + x, ((z2 * 2 + y2) * 2 + c2) * self.seq + x2))
        return pairs

    def send(self, array, step):
        return lax.ppermute(array, self.every, self.moves(step))

    def flip_core(self, array):
        return self.send(array, lambda z, y, c, x: (z, y, 1 - c, x))

    def flip_y(self, array):
        return self.send(array, lambda z, y, c, x: (z, 1 - y, c, x))

    def shift_x(self, array, by):
        return self.send(array, lambda z, y, c, x: (z, y, c, (x + by) % self.seq))

    def shift_z(self, array, by):
        return self.send(array, lambda z, y, c, x: ((z + by) % self.depth, y, c, x))

    def xor_patch(self, array, bit):
        pairs = [
            (p * self.seq + x, (p ^ bit) * self.seq + x)
            for p in range(self.patch)
            for x in range(self.seq)
        ]
        return lax.ppermute(array, self.every, pairs)

    def bits(self):
        bit = self.patch // 2
        while bit:
            yield bit
            bit //= 2

    def sum_patch(self, array):
        for bit in self.bits():
            array = array + self.xor_patch(array, bit)
        return array

    def join_patch(self, array, bit):
        other = self.xor_patch(array, bit)
        mine_first = (self.place // bit) % 2 == 0
        return jnp.where(
            mine_first, jnp.concatenate([array, other]), jnp.concatenate([other, array])
        )

    def all_seq(self, array):
        return [array] + [self.shift_x(array, -j) for j in range(1, self.seq)]


class Split:
    def __init__(self, grid, head, group):
        self.grid = grid
        self.head, self.group = head, group
        self.last = None
        self.where = jnp.stack([grid.z, grid.y, grid.core, grid.x]).astype(jnp.int32)

    @staticmethod
    def fits(patch, seq, frames, features, hidden):
        return (
            patch == HEADS
            and patch == frames
            and seq == 2
            and features % (2 * patch) == 0
            and hidden % patch == 0
            and (2 * features // patch) % 16 == 0
            and hidden == 2 * 2 * features
            and (hidden // patch) % 32 == 0
        )


    def tie(self, *arrays):
        if self.last is not None:
            *arrays, self.last = lax.optimization_barrier((*arrays, self.last))
        return arrays[0] if len(arrays) == 1 else arrays

    def done(self, array):
        self.last = array
        return array

    def run(self, kernel, first, *rest):
        result = kernel(self.where, self.tie(first), *rest)
        self.last = result[-1] if isinstance(result, (list, tuple)) else result
        return result

    def first(self, array, x_first):
        return self.grid.shift_x(array, 1) if x_first else self.grid.flip_y(array)

    def prepare(self, spatial, temporal):
        own, other = deal(
            self.where,
            [spatial[0], spatial[2], temporal[0], temporal[2]],
            [self.head, self.group] * 2,
        )
        got = self.grid.flip_core(other)
        cols = (spatial[0].shape[1] // 2, spatial[2].shape[1] // 2)
        return pack(self.where, own, got, [spatial[1], temporal[1]], temporal[3], cols)

    def gather(self, piece, by_rows):
        grid = self.grid
        rows, cols = piece.shape
        cut = rows // 2 if by_rows else (cols // 256 + 1) * 128
        piece = self.tie(piece)
        pieces = [piece] + [grid.shift_z(piece, -j) for j in range(1, grid.depth)]
        yield
        if by_rows:
            strips = [[p[:cut] for p in pieces], [p[cut:] for p in pieces]]
            places = [(0, cut, 0, cols), (cut, rows - cut, 0, cols)]
        else:
            strips = [[p[:, :cut] for p in pieces], [p[:, cut:] for p in pieces]]
            places = [(0, rows, 0, cut), (0, rows, cut, cols - cut)]
        held = self.tie(*[jnp.stack(s) for s in strips])
        self.done(held[1])
        came = [self.first(h, order) for h, order in zip(held, (True, False))]
        yield
        held = self.tie(*[jnp.stack([h, c]) for h, c in zip(held, came)])
        self.done(held[1])
        came = [self.first(h, order) for h, order in zip(held, (False, True))]
        found = []
        for h, c, order, place in zip(held, came, (True, False), places):
            arrays = [h, c, grid.flip_core(h), grid.flip_core(c)]
            found.append((arrays, order, 0) + place)
        yield Weight(grid.depth, rows, cols, found)

    def gather_packed(self, packed, cols, down):
        grid = self.grid
        rows, lanes = packed.shape
        whole = lax.all_gather(self.tie(packed), grid.every, axis=0)
        arrays = [whole.reshape(grid.depth, 2, 2, 2, rows, lanes)]
        at, found = 0, []
        for c in cols:
            found.append(Weight(grid.depth, rows, c, [(arrays, None, at, 0, rows, 0, c)]))
            at += c
        count = down[0] // rows
        padded = (lanes - at) // count
        strips = [
            (arrays, None, at + k * padded, k * rows, rows, 0, padded) for k in range(count)
        ]
        found.append(Weight(grid.depth, down[0], down[1], strips))
        return found

    def reduce(self, left, right, tail, x_first, width):
        grid = self.grid
        depth = grid.depth
        cols = right.shape[-1]
        far, near = self.run(weight_grad, left, right, tail, depth, x_first, 1, None)
        came = grid.flip_core(far), grid.flip_core(near)
        yield
        far, near = self.run(weight_grad, left, right, tail, depth, x_first, 0, came)
        came = self.first(far, x_first)
        yield
        far, near = self.run(add_split, near, came, 1 if x_first else 3)
        came = self.first(far, not x_first)
        yield
        own, *others = self.run(add_planes, near, came)
        came = [grid.shift_z(plane, j + 1) for j, plane in enumerate(others)]
        yield
        *rest, mine, theirs = self.run(add_last, own, came, cols)
        theirs = grid.flip_core(theirs)
        yield
        whole = self.run(interleave, mine, theirs, width)
        yield [whole] + rest

    def scatter(self, grads):
        dims = grads.shape[-2:]
        mine = lax.psum_scatter(
            grads.reshape((-1,) + dims), self.grid.every, scatter_dimension=0, tiled=False
        )
        return mine.reshape(dims).astype(FULL)

    def qkv_part(self, rows, mods, weight, marks):
        cols = 3 * rows.shape[1] // 4
        hidden_one, out_w, qkv = self.run(norm_qkv, rows, mods, weight, cols)
        attended = self.run(attend_kernel, qkv, marks, self.head)
        branch, middle, hidden_two = self.run(out_norm, rows, mods, attended, out_w)
        return rows, hidden_one, out_w, qkv, attended, branch, middle, hidden_two

    def forward(self, tokens, mods, shards, marks, to_patches):
        (qkv_s, up_s, down_s), packed = shards
        cols = (qkv_s.shape[1], up_s.shape[1])
        qkv_g = self.gather(qkv_s, False)
        next(qkv_g)
        next(qkv_g)
        up_g = self.gather(up_s, False)
        next(up_g)
        next(up_g)
        qkv_w = next(qkv_g)
        down_g = self.gather(down_s, True)
        next(down_g)
        next(down_g)
        up_w = next(up_g)
        temporal = self.gather_packed(packed, cols, down_s.shape)
        saved = self.qkv_part(tokens, mods[0], qkv_w, None)
        down_w = next(down_g)
        pre, act = self.run(up_gelu, saved[-1], up_w)
        mlp, result = self.run(down_add, act, down_w, saved[-2], mods[0])
        spatial = (mods[0], (qkv_w, up_w, down_w), saved + (pre, act, mlp), None)

        saved = self.qkv_part(to_patches(result), mods[1], temporal[0], marks)
        pre, act = self.run(up_gelu, saved[-1], temporal[1])
        mlp, result = self.run(down_add, act, temporal[2], saved[-2], mods[1])
        return result, spatial, (mods[1], temporal, saved + (pre, act, mlp), marks)

    def backward(self, spatial, temporal, grad, move, condition_steps):
        depth, head = self.grid.depth, self.head
        mods, (qkv_w, up_w, down_w), saved, marks = temporal
        rows, hidden_one, out_w, qkv, attended, branch, middle, hidden_two, pre, act, mlp = saved
        grad_mlp = self.run(scale_halves, grad, mods)
        down_t = self.scatter(self.run(down_grad, act, grad_mlp, depth))
        grad_mid, grad_pre, grad_branch, sums_two = self.run(
            mlp_back, grad, mods, pre, middle, branch, mlp, up_w, down_w
        )
        up_t = self.reduce(hidden_two[None], grad_pre, None, True, self.group)
        next(up_t)
        grad_rows = self.run(attend_back_kernel, grad_branch, out_w, qkv, marks, head)
        next(up_t)
        qkv_t = self.reduce(hidden_one[None], grad_rows, (attended, grad_branch), False, head)
        next(qkv_t)
        grad, sums_one = self.run(qkv_back, grad_rows, qkv_w, rows, mods, grad_mid)
        mods_t = jnp.concatenate([sums_one[:2], sums_two[:4]], axis=0).reshape(1, -1)
        grad = move(grad)
        next(qkv_t)

        mods, (qkv_w, up_w, down_w), saved, marks = spatial
        rows, hidden_one, out_w, qkv, attended, branch, middle, hidden_two, pre, act, mlp = saved
        grad_mlp = self.run(scale_halves, grad, mods)
        down_s = self.scatter(self.run(down_grad, act, grad_mlp, depth))
        next(up_t)
        grad_mid, grad_pre, grad_branch, sums_two = self.run(
            mlp_back, grad, mods, pre, middle, branch, mlp, up_w, down_w
        )
        up_s = self.reduce(hidden_two[None], grad_pre, None, True, self.group)
        next(up_s)
        next(qkv_t)
        grad_rows = self.run(attend_back_kernel, grad_branch, out_w, qkv, marks, head)
        next(up_s)
        next(up_t)
        qkv_s = self.reduce(hidden_one[None], grad_rows, (attended, grad_branch), False, head)
        next(qkv_s)
        next(qkv_t)
        grad, sums_one = self.run(qkv_back, grad_rows, qkv_w, rows, mods, grad_mid)
        mods_s = jnp.concatenate([sums_one[:2], sums_two[:4]], axis=0).reshape(1, -1)
        next(qkv_s)
        next(up_t)
        steps = condition_steps(mods_s, mods_t)
        for _ in range(2):
            next(steps)
        next(up_s)
        for _ in range(3):
            next(steps)
        next(qkv_t)
        next(qkv_s)
        (up_t,) = next(up_t)
        next(up_s)
        qkv_t, out_t = next(qkv_t)
        for _ in range(3):
            next(steps)
        next(qkv_s)
        next(up_s)
        conditions = list(steps)[-1]
        (up_s,) = next(up_s)
        next(qkv_s)
        qkv_s, out_s = next(qkv_s)
        return grad, conditions, (qkv_s, out_s, up_s, down_s), (qkv_t, out_t, up_t, down_t)


class WholeWeights:
    def __init__(self, grid, features, hidden):
        self.features, self.hidden = features, hidden

    def gather(self, local):
        wide = lax.all_gather(local, "seq", axis=1, tiled=True)
        return lax.all_gather(wide, "patch", axis=0, tiled=True)

    def fetch(self, spatial, temporal):
        return [[tuple(self.gather(w) for w in block)] for block in (spatial, temporal)]

    def scatter(self, grad):
        rows = lax.psum_scatter(grad.astype(LOW), "patch", scatter_dimension=0, tiled=True)
        return lax.psum_scatter(rows, "seq", scatter_dimension=1, tiled=True).astype(FULL)

    def reduce_mlp(self, hidden, grad_pre, activated, grad_mlp, flip):
        return (
            self.scatter(matmul_tn(hidden, grad_pre[0])),
            self.scatter(matmul_tn(activated[0], grad_mlp)),
        )

    def reduce_out(self, attended, grad_branch, flip):
        return self.scatter(matmul_tn(attended[0], grad_branch))

    def reduce_qkv(self, hidden, grad_qkv, flip):
        return self.scatter(matmul_tn(hidden, grad_qkv[0]))


def attention(queries, keys, mask, factor):
    scores = jnp.einsum("bphd,bkhd->bhpk", queries, keys, preferred_element_type=FULL) * factor
    if mask is not None:
        scores = jnp.where(mask, scores, -1e30)
    top = jnp.max(scores, axis=-1, keepdims=True)
    weights = jnp.exp(scores - top)
    return weights / jnp.sum(weights, axis=-1, keepdims=True)


def attend(qkv, batch, mask, head, share):
    rows = qkv.reshape(batch, -1, 3, qkv.shape[-1] // (3 * head), head)
    keys, values = share(rows[:, :, 1]), share(rows[:, :, 2])
    probs = attention(rows[:, :, 0], keys, mask, head ** (-0.5)).astype(LOW)
    mixed = jnp.einsum("bhpk,bkhd->bphd", probs, values, preferred_element_type=FULL)
    return mixed.reshape(qkv.shape[0], -1).astype(LOW)


def attend_back(grad, qkv, batch, mask, head, share, share_back):
    factor = head ** (-0.5)
    heads = qkv.shape[-1] // (3 * head)
    rows = qkv.reshape(batch, -1, 3, heads, head)
    grad_rows = grad.reshape(batch, -1, heads, head)
    queries, keys, values = rows[:, :, 0], share(rows[:, :, 1]), share(rows[:, :, 2])
    probs = attention(queries, keys, mask, factor)
    grad_probs = jnp.einsum("bphd,bkhd->bhpk", grad_rows, values, preferred_element_type=FULL)
    delta = jnp.sum(grad_probs * probs, axis=-1, keepdims=True)
    grad_scores = (probs * (grad_probs - delta)).astype(LOW)
    grad_queries = (
        jnp.einsum("bhpk,bkhd->bphd", grad_scores, keys, preferred_element_type=FULL) * factor
    )
    grad_keys = (
        jnp.einsum("bhpk,bphd->bkhd", grad_scores, queries, preferred_element_type=FULL) * factor
    )
    grad_values = jnp.einsum(
        "bhpk,bphd->bkhd", probs.astype(LOW), grad_rows, preferred_element_type=FULL
    )
    joined = jnp.stack(
        [grad_queries, share_back(grad_keys), share_back(grad_values)], axis=2
    )
    return joined.reshape(qkv.shape[0], -1).astype(LOW)


def total_parts(parts):
    total = parts[0]
    for part in parts[1:]:
        total = total + part
    return total


def block_forward(residual, pieces, parts, mix):
    normed_one, inverse_one = normalize(residual)
    hidden_one = (normed_one * (1.0 + pieces[1]) + pieces[0]).astype(LOW)
    qkv = [matmul(hidden_one, part[0]).astype(LOW) for part in parts]
    attended = [mix(rows) for rows in qkv]
    branch = total_parts([matmul(a, part[1]) for a, part in zip(attended, parts)])
    middle = residual + pieces[2] * branch
    normed_two, inverse_two = normalize(middle)
    hidden_two = (normed_two * (1.0 + pieces[4]) + pieces[3]).astype(LOW)
    pre = [matmul(hidden_two, part[2]) for part in parts]
    activated = [jax.nn.gelu(v, approximate=True).astype(LOW) for v in pre]
    mlp = total_parts([matmul(a, part[3]) for a, part in zip(activated, parts)])
    result = middle + pieces[5] * mlp
    saved = (
        normed_one,
        inverse_one,
        hidden_one,
        qkv,
        attended,
        branch,
        normed_two,
        inverse_two,
        hidden_two,
        pre,
        activated,
        mlp,
    )
    return result, saved


def block_backward(incoming, pieces, parts, saved, mix_back, weights, groups, flip):
    (
        normed_one,
        inverse_one,
        hidden_one,
        qkv,
        attended,
        branch,
        normed_two,
        inverse_two,
        hidden_two,
        pre,
        activated,
        mlp,
    ) = saved
    grad_mlp = (pieces[5] * incoming).astype(LOW)
    grad_pre = []
    for part, v in zip(parts, pre):
        _, back = jax.vjp(partial(jax.nn.gelu, approximate=True), v)
        grad_pre.append(back(matmul_nt(grad_mlp, part[3]))[0].astype(LOW))
    grad_up, grad_down = weights.reduce_mlp(hidden_two, grad_pre, activated, grad_mlp, flip)
    grad_hidden_two = total_parts([matmul_nt(g, part[2]) for g, part in zip(grad_pre, parts)])
    grad_middle = incoming + normalize_back(
        grad_hidden_two * (1.0 + pieces[4]), normed_two, inverse_two
    )
    grad_branch = (pieces[2] * grad_middle).astype(LOW)
    grad_out = weights.reduce_out(attended, grad_branch, flip)
    grad_attended = [matmul_nt(grad_branch, part[1]).astype(LOW) for part in parts]
    grad_qkv_rows = [mix_back(g, rows) for g, rows in zip(grad_attended, qkv)]
    grad_qkv = weights.reduce_qkv(hidden_one, grad_qkv_rows, flip)
    grad_hidden_one = total_parts(
        [matmul_nt(g, part[0]) for g, part in zip(grad_qkv_rows, parts)]
    )
    grad_residual = grad_middle + normalize_back(
        grad_hidden_one * (1.0 + pieces[1]), normed_one, inverse_one
    )
    sums = [
        jnp.sum(v.reshape(groups, -1, v.shape[-1]), axis=1)
        for v in (
            grad_hidden_one,
            grad_hidden_one * normed_one,
            grad_middle * branch,
            grad_hidden_two,
            grad_hidden_two * normed_two,
            incoming * mlp,
        )
    ]
    grad_mods = jnp.concatenate(sums, axis=-1)
    return grad_residual, grad_mods, (grad_qkv, grad_out, grad_up, grad_down)


def per_device(
    patch,
    seq,
    patch_axes,
    seq_axis,
    tokens,
    cotangent,
    class_ids,
    timesteps,
    segments,
    class_table,
    mod_spatial,
    qkv_spatial,
    out_spatial,
    up_spatial,
    down_spatial,
    mod_temporal,
    qkv_temporal,
    out_temporal,
    up_temporal,
    down_temporal,
):
    groups, frames, patch_rows, features = tokens.shape
    row_count = groups * frames * patch_rows
    head = features // HEADS
    hidden = up_spatial.shape[1] * seq
    grid = Grid(patch, seq, patch_axes, seq_axis)
    split = groups == 1 and Split.fits(patch, seq, frames, features, hidden)

    ways = max(1, patch // frames)
    subgroups = None
    if ways > 1:
        subgroups = [[a * ways + b for a in range(frames)] for b in range(ways)]

    def to_frames(array):
        moved = lax.all_to_all(
            array.reshape(groups, frames, patch_rows, features),
            patch_axes,
            split_axis=1,
            concat_axis=2,
            tiled=True,
            axis_index_groups=subgroups,
        )
        return moved.reshape(row_count, features)

    own_frames = max(1, frames // patch)

    def to_patches(array):
        moved = lax.all_to_all(
            array.reshape(groups, own_frames, -1, features),
            patch_axes,
            split_axis=2,
            concat_axis=1,
            tiled=True,
            axis_index_groups=subgroups,
        )
        return moved.reshape(row_count, features)

    def sharers(by):
        return [
            (a * ways + b, a * ways + (b + by) % ways)
            for a in range(patch // ways)
            for b in range(ways)
        ]

    def share_frame(array):
        if ways == 1:
            return array
        return jnp.concatenate(
            [array] + [lax.ppermute(array, patch_axes, sharers(j)) for j in range(1, ways)], axis=1
        )

    def share_frame_back(array):
        if ways == 1:
            return array
        cut = jnp.split(array, ways, axis=1)
        total = cut[0]
        for j in range(1, ways):
            total = total + lax.ppermute(cut[j], patch_axes, sharers(-j))
        return total

    one_hot = (
        class_ids[:, None] == jnp.arange(class_table.shape[0], dtype=jnp.int32)[None, :]
    ).astype(LOW)
    condition = matmul(one_hot, class_table) + time_features(timesteps, features)
    conditions = grid.all_seq(condition)
    every_class = grid.all_seq(class_ids)
    cond_low = [jax.nn.silu(c).astype(LOW) for c in conditions]
    mod_rows = features // patch
    first_row = grid.place * mod_rows
    cond_own = [lax.dynamic_slice_in_dim(c, first_row, mod_rows, axis=1) for c in cond_low]
    partial_mods = [
        jnp.stack([matmul(c, mod_spatial), matmul(c, mod_temporal)]) for c in cond_own
    ]
    mods = grid.sum_patch(jnp.stack(partial_mods))
    received = [mods[0]] + [grid.shift_x(mods[j], j) for j in range(1, seq)]
    ordered = in_order(received[:1] + received[:0:-1], grid.x)
    modulation = jnp.concatenate(ordered, axis=-1)

    width = mod_spatial.shape[1]

    def outer(columns):
        return lax.dot_general(
            jnp.concatenate(cond_own).astype(FULL),
            columns,
            (((0,), (0,)), ((), ())),
            precision=PRECISE,
            preferred_element_type=FULL,
        )

    def condition_part(columns, mod):
        return lax.dot_general(
            columns,
            mod.astype(FULL),
            (((1,), (1,)), ((), ())),
            precision=PRECISE,
            preferred_element_type=FULL,
        )

    def condition_steps(spatial_sums, temporal_sums, hold):
        sums = jnp.stack([spatial_sums, temporal_sums])
        for bit in grid.bits():
            sums = hold(sums + grid.xor_patch(sums, bit))
            yield None
        sums = sums.reshape(2, groups, seq, width)
        columns = [pick(sums, 2, grid.x)] + [
            grid.shift_x(pick(sums, 2, (grid.x - j) % seq), -j) for j in range(1, seq)
        ]
        columns = hold(jnp.concatenate(columns, axis=1))
        yield None
        parts = condition_part(columns[0], mod_spatial) + condition_part(columns[1], mod_temporal)
        parts = parts.reshape(seq, groups, mod_rows)
        total = parts
        for j in range(1, seq):
            total = total + jnp.roll(grid.shift_x(parts, j), j, axis=0)
        total = hold(total[None])
        yield None
        bit = 1
        while bit < patch:
            total = hold(grid.join_patch(total, bit))
            bit *= 2
            yield None
        grad_condition = total.transpose(1, 2, 0, 3).reshape(seq * groups, features)
        _, silu_back = jax.vjp(jax.nn.silu, jnp.concatenate(conditions))
        every_hot = (
            jnp.concatenate(every_class)[:, None]
            == jnp.arange(class_table.shape[0], dtype=jnp.int32)[None, :]
        ).astype(FULL)
        grad_class_table = lax.dot_general(
            every_hot,
            silu_back(grad_condition)[0],
            (((0,), (0,)), ((), ())),
            precision=PRECISE,
            preferred_element_type=FULL,
        )
        yield grad_class_table, outer(columns[0]), outer(columns[1])


    spatial_shards = (qkv_spatial, out_spatial, up_spatial, down_spatial)
    temporal_shards = (qkv_temporal, out_temporal, up_temporal, down_temporal)
    span = frames * patch_rows
    patch_of = jnp.arange(span, dtype=jnp.int32) % patch_rows
    place_of = jnp.repeat(segments, patch_rows, axis=1) * patch_rows + patch_of[None, :]

    if split:
        plan = Split(grid, head, hidden // patch)
        mods_of = [
            jnp.pad(modulation[block].reshape(6, features), ((0, 2), (0, 0))) for block in range(2)
        ]
        marks = (place_of.reshape(-1, 1), place_of.reshape(1, -1))
        qkv_s, up_s, packed = plan.prepare(spatial_shards, temporal_shards)
        frame_tokens = to_frames(tokens)
        plan.done(mods_of[0])
        frame_tokens = plan.done(plan.tie(frame_tokens))
        result, spatial_state, temporal_state = plan.forward(
            frame_tokens,
            mods_of,
            ((qkv_s, up_s, down_spatial), packed),
            marks,
            to_patches,
        )
        out_tokens = result.reshape(tokens.shape)
        grad_spatial_in, condition_grads, spatial_grads, temporal_grads = plan.backward(
            spatial_state,
            temporal_state,
            cotangent.reshape(row_count, features),
            to_frames,
            lambda s, t: condition_steps(s, t, lambda v: plan.done(plan.tie(v))),
        )
        grad_tokens = to_patches(grad_spatial_in).astype(FULL).reshape(tokens.shape)
    else:
        weights = WholeWeights(grid, features, hidden)

        def pieces_of(block):
            rows = modulation[block]
            if groups > 1:
                rows = jnp.repeat(rows, row_count // groups, axis=0)
            return [rows[:, k * features : (k + 1) * features] for k in range(6)]

        spatial_pieces, temporal_pieces = pieces_of(0), pieces_of(1)
        spatial_parts, temporal_parts = weights.fetch(spatial_shards, temporal_shards)
        same = (place_of[:, :, None] == place_of[:, None, :])[:, None, :, :]
        itself = lambda array: array
        spatial_batch = groups * own_frames
        spatial_mix = lambda rows: attend(rows, spatial_batch, None, head, share_frame)
        spatial_mix_back = lambda g, rows: attend_back(
            g, rows, spatial_batch, None, head, share_frame, share_frame_back
        )
        temporal_mix = lambda rows: attend(rows, groups, same, head, itself)
        temporal_mix_back = lambda g, rows: attend_back(
            g, rows, groups, same, head, itself, itself
        )
        spatial_in = to_frames(tokens).astype(FULL)
        spatial_out, spatial_saved = block_forward(
            spatial_in, spatial_pieces, spatial_parts, spatial_mix
        )
        temporal_in = to_patches(spatial_out.astype(LOW)).astype(FULL)
        result, temporal_saved = block_forward(
            temporal_in, temporal_pieces, temporal_parts, temporal_mix
        )
        out_tokens = result.astype(LOW).reshape(tokens.shape)
        incoming = cotangent.astype(FULL).reshape(row_count, features)
        grad_temporal_in, temporal_sums, temporal_grads = block_backward(
            incoming,
            temporal_pieces,
            temporal_parts,
            temporal_saved,
            temporal_mix_back,
            weights,
            groups,
            True,
        )
        grad_spatial_out = to_frames(grad_temporal_in.astype(LOW)).astype(FULL)
        grad_spatial_in, spatial_sums, spatial_grads = block_backward(
            grad_spatial_out,
            spatial_pieces,
            spatial_parts,
            spatial_saved,
            spatial_mix_back,
            weights,
            groups,
            False,
        )
        grad_tokens = to_patches(grad_spatial_in.astype(LOW)).astype(FULL).reshape(tokens.shape)
        condition_grads = list(condition_steps(spatial_sums, temporal_sums, itself))[-1]

    grad_class_table, grad_mod_spatial, grad_mod_temporal = condition_grads

    return (
        out_tokens,
        grad_tokens,
        grad_class_table,
        grad_mod_spatial,
        *spatial_grads,
        grad_mod_temporal,
        *temporal_grads,
    )


def solution(mesh):
    patch, seq = mesh.shape["patch"], mesh.shape["seq"]
    patch_axes, seq_axis = "patch", "seq"
    if seq == 2 and patch % 4 == 0:
        patch_axes, seq_axis = ("z", "y", "core"), "x"
        mesh = Mesh(mesh.devices.reshape(patch // 4, 2, 2, seq), patch_axes + (seq_axis,))
    rows = P(seq_axis, None, patch_axes, None)
    both = P(patch_axes, seq_axis)
    return jax.shard_map(
        partial(per_device, patch, seq, patch_axes, seq_axis),
        mesh=mesh,
        in_specs=(rows, rows, P(seq_axis), P(seq_axis), P(seq_axis, None), P()) + (both,) * 10,
        out_specs=(rows, rows, P()) + (both,) * 10,
        check_vma=False,
    )
```

time: 2760 us -> 1020 us (0.37)
  waiting for transfers between devices: 2040 us -> 457 us
  Pallas kernels: 0 us -> 314 us
  matrix products: 296 us -> 10.5 us
  blocking collectives: 162 us -> 0 us
  starting transfers between devices: 2.92 us -> 149 us
  local copies, waits for them, and re-layouts: 180 us -> 39.8 us
    reduce_scatter x8 -> x2, waiting for transfers between devices: 870 us -> 0.01 us  [scatter(): lax.psum_scatter(grads.reshape((-1,) + dims), self.grid.every, scatter_di...]
    all_gather x14 -> x1, waiting for transfers between devices: 780 us -> 7.63 us  [gather_packed(): whole = lax.all_gather(self.tie(packed), grid.every, axis=0)]
    ppermute x0 -> x83, waiting for transfers between devices: none -> 404 us  [the longest x71 376 us: send(): return lax.ppermute(array, self.every, self.moves(step))]
    pallas_call x0 -> x46, Pallas kernels: none -> 314 us  [the longest x32 212 us: call(): pl.pallas_call(kernel, out_shape=outs, in_specs=[pl.BlockSpec(memory_spac...]
    dot_general x42 -> x10, matrix products: 296 us -> 10.5 us  [the longest x5 4.08 us: matmul(): return jnp.dot(left, right, preferred_element_type=FULL)]
    unnamed x47 -> x3, waiting for transfers between devices: 264 us -> 0.05 us
    all_gather x12 -> x0, blocking collectives: 162 us -> none  [the longest x1 36.1 us: spatial_back(): lax.all_gather(jnp.moveaxis(row_delta[..., 0], 2, 3), 'patch', axis=2, ti...]
    psum x1 -> x0, waiting for transfers between devices: 130 us -> none  [per_device(): grad_class_table = lax.psum(table_part, ('patch', 'seq'))]
  transfers between devices with their start and end apart: 35 -> 90, of which waited for: 29 -> 34; matrix products, arithmetic and copies ran while one was open for 18% -> 5% of each run, Pallas kernels for 0% -> 26%
where the time goes in v1:
time: 1020 us; the launch traced here: 1010 us
  waiting for transfers between devices  457 us (45%)
  Pallas kernels  314 us (31%)
  starting transfers between devices  149 us (15%)
  local copies, waits for them, and re-layouts  39.8 us (4%)
  other arithmetic  27.7 us (3%)
  between operations  16.5 us (2%)
  matrix products  10.5 us (1%)
    ppermute x71, waiting for transfers between devices, send(): return lax.ppermute(array, self.every, self.moves(step))  376 us
    pallas_call x32, Pallas kernels, call(): pl.pallas_call(kernel, out_shape=outs, in_specs=[pl.BlockSpec(memory_spac...  212 us
    ppermute x71, starting transfers between devices, send(): return lax.ppermute(array, self.every, self.moves(step))  101 us
    pallas_call x8, Pallas kernels, weight_grad(): pl.pallas_call(kernel, out_shape=[out, out], grid_spec=pltpu.PrefetchScal...  60.8 us
    unnamed x98, local copies, waits for them, and re-layouts  28.6 us
    ppermute x12, waiting for transfers between devices, xor_patch(): return lax.ppermute(array, self.every, pairs)  28.4 us
    ppermute x12, starting transfers between devices, xor_patch(): return lax.ppermute(array, self.every, pairs)  25.2 us
    all_to_all x2, waiting for transfers between devices, to_patches(): lax.all_to_all(array.reshape(groups, own_frames, -1, features), patch_axe...  24 us
  transfers between devices with their start and end apart: 90, of which 34 were waited for; matrix products, arithmetic and copies ran while one was open for 5% of the time, Pallas kernels for 26%

profile of v1, /device:TPU:0, one launch (start us, length us, event | category | flops | bytes accessed | tf_op | source)
XLA Modules:
  0.0 1014.3 jit_solution(2990489653908784348)
XLA Ops:
  65.3 13.2 %collective-permute-done.8 = bf16[144,1152]{1,0:T(8,128)(2,1)S(1)} collective-permute-done((bf16[144,1152]{1,0:T(8,128)(2,1)}, bf16[144,1152]{1,0:T(8,128)(2,1)S(1)}, u32[]{:S(2)}, u32[]{:S(2)}) %collective-permute-start.8) | collective-permute-done | bytes 331808 | tf_op jit(solution)/shard_map/ppermute | solution.py:857
  96.5 11.9 %collective-permute-done.13 = bf16[144,1152]{1,0:T(8,128)(2,1)S(1)} collective-permute-done((bf16[144,1152]{1,0:T(8,128)(2,1)S(1)}, bf16[144,1152]{1,0:T(8,128)(2,1)S(1)}, u32[]{:S(2)}, u32[]{:S(2)}) %collective-permute-start.13) | collective-permute-done | bytes 331808 | tf_op jit(solution)/shard_map/ppermute | solution.py:857
  133.8 13.9 %collective-permute-done.22 = bf16[288,576]{1,0:T(8,128)(2,1)S(1)} collective-permute-done((bf16[288,576]{1,0:T(8,128)(2,1)S(1)}, bf16[288,576]{1,0:T(8,128)(2,1)S(1)}, u32[]{:S(2)}, u32[]{:S(2)}) %collective-permute-start.22) | collective-permute-done | bytes 331808 | tf_op jit(solution)/shard_map/ppermute | solution.py:857
  153.4 51.1 %collective-permute-done.24 = bf16[4,144,576]{2,1,0:T(8,128)(2,1)S(1)} collective-permute-done((bf16[4,144,576]{2,1,0:T(8,128)(2,1)}, bf16[4,144,576]{2,1,0:T(8,128)(2,1)S(1)}, u32[]{:S(2)}, u32[]{:S(2)}) %collective-permute-start.24) | collective-permute-done | bytes 663584 | tf_op jit(solution)/shard_map/ppermute | solution.py:857
  205.9 24.9 %collective-permute-done.25 = bf16[4,144,576]{2,1,0:T(8,128)(2,1)S(1)} collective-permute-done((bf16[4,144,576]{2,1,0:T(8,128)(2,1)}, bf16[4,144,576]{2,1,0:T(8,128)(2,1)S(1)}, u32[]{:S(2)}, u32[]{:S(2)}) %collective-permute-start.25) | collective-permute-done | bytes 663584 | tf_op jit(solution)/shard_map/ppermute | solution.py:857
  237.5 9.0 norm_qkv.2
  261.3 10.2 %collective-permute-done.28.refs_2_.refs_7_ = bf16[2,4,144,640]{3,2,1,0:T(8,128)(2,1)} collective-permute-done((bf16[2,4,144,640]{3,2,1,0:T(8,128)(2,1)S(1)}, bf16[2,4,144,640]{3,2,1,0:T(8,128)(2,1)}, u32[]{:S(2)}, u32[]{:S(2)}) %collective-permute-start.28) | collective-permute-done | bytes 1474592 | tf_op jit(solution)/shard_map/ppermute | solution.py:857
  272.1 61.8 %collective-permute-done.34.refs_4_.refs_15_ = bf16[2,4,144,576]{3,2,1,0:T(8,128)(2,1)} collective-permute-done((bf16[2,4,144,576]{3,2,1,0:T(8,128)(2,1)S(1)}, bf16[2,4,144,576]{3,2,1,0:T(8,128)(2,1)}, u32[]{:S(2)}, u32[]{:S(2)}) %collective-permute-start.34) | collective-permute-done | bytes 1327136 | tf_op jit(solution)/shard_map/ppermute | solution.py:857
  334.9 10.2 %up_gelu.2 = (bf16[4,256,1152]{2,1,0:T(8,128)(2,1)}, bf16[4,256,1152]{2,1,0:T(8,128)(2,1)}) custom-call(s32[4]{0:T(128)} %pad_add_fusion.where_ref.where, bf16[256,1152]{1,0:T(8,128)(2,1)} %get-tuple-element.191.refs_0_, bf16[2,4,144,640]{3,2,1,0:T(8,128)(2,1)} %copy-done.2, bf16[2,4,144,640]{3,2,1,0:T(8,128)(2,1)} %collective-permute-done.28.refs_2_.refs_7_, ...), custom_call_target="tpu_custom_call" | custom-call | flops 2717908992 | bytes 15925248 | tf_op jit(solution)/shard_map/up_gelu/pallas_call | solution.py:148
  346.3 10.6 %down_add.2 = (f32[256,1152]{1,0:T(8,128)}, bf16[256,1152]{1,0:T(8,128)(2,1)}) custom-call(s32[4]{0:T(128)} %pad_add_fusion.where_ref.where, bf16[4,256,1152]{2,1,0:T(8,128)(2,1)} %get-tuple-element.239.refs_0_.act, f32[256,1152]{1,0:T(8,128)} %get-tuple-element.197.refs_1_.refs_3_, f32[8,1152]{1,0:T(8,128)} %pad.7.refs_1_.refs_2_, ...), custom_call_target="tpu_custom_call" | custom-call | flops 2717908992 | bytes 15962112 | tf_op jit(solution)/shard_map/down_add/pallas_call | solution.py:148
  374.1 24.0 %all-to-all-done.1 = bf16[16,2,9216]{2,1,0:T(2,128)(2,1)S(1)} async-done(((bf16[16,2,9216]{2,1,0:T(2,128)(2,1)}), bf16[16,2,9216]{2,1,0:T(2,128)(2,1)S(1)}, u32[]{:S(2)}, u32[]{:S(2)}) %all-to-all-start.1) | async-done | bytes 589856 | tf_op jit(solution)/shard_map/all_to_all | solution.py:1323
  429.1 10.0 up_gelu.3
  439.1 10.6 %down_add.3 = (f32[256,1152]{1,0:T(8,128)}, bf16[256,1152]{1,0:T(8,128)(2,1)}) custom-call(s32[4]{0:T(128)} %pad_add_fusion.where_ref.where, bf16[4,256,1152]{2,1,0:T(8,128)(2,1)} %get-tuple-element.214.refs_0_.act, f32[256,1152]{1,0:T(8,128)} %get-tuple-element.211.refs_1_.refs_3_, f32[8,1152]{1,0:T(8,128)} %pad.8.refs_1_.refs_2_, ...), custom_call_target="tpu_custom_call" | custom-call | flops 2717908992 | bytes 38375424 | tf_op jit(solution)/shard_map/down_add/pallas_call | solution.py:148
  451.8 10.1 down_grad.2
  462.0 20.5 %mlp_back.2 = (f32[256,1152]{1,0:T(8,128)}, bf16[4,256,1152]{2,1,0:T(8,128)(2,1)}, bf16[2,256,576]{2,1,0:T(8,128)(2,1)}, f32[8,1152]{1,0:T(8,128)}) custom-call(s32[4]{0:T(128)} %pad_add_fusion.where_ref.where, bf16[256,1152]{1,0:T(8,128)(2,1)} %bitcast.208, f32[8,1152]{1,0:T(8,128)} %pad.8.refs_1_.refs_2_, ...), custom_call_target="tpu_custom_call" | custom-call | flops 5435817984 | bytes 43720704 | tf_op jit(solution)/shard_map/mlp_back/pallas_call | solution.py:148
  489.7 12.3 %attend_back.2.refs_1_.refs_0_ = bf16[4,256,864]{2,1,0:T(8,128)(2,1)} custom-call(s32[4]{0:T(128)} %pad_add_fusion.where_ref.where, bf16[2,256,576]{2,1,0:T(8,128)(2,1)} %get-tuple-element.224.refs_0_.refs_3_, bf16[4,576,576]{2,1,0:T(8,128)(2,1)} %get-tuple-element.206.refs_3_.refs_1_, bf16[4,256,864]{2,1,0:T(8,128)(2,1)} %get-tuple-element.204.refs_0_.refs_2_, ...), custom_call_target="tpu_custom_call" | custom-call | flops 754974720 | bytes 6785024 | tf_op jit(solution)/shard_map/attend_back/pallas_call | solution.py:148
  519.4 9.5 qkv_back.2
  532.6 8.7 weight_grad.11
  541.3 16.5 %all-to-all-done.2 = bf16[1,16,16,1152]{3,2,0,1:T(8,128)(2,1)S(1)} async-done(((bf16[1,16,16,1152]{3,2,0,1:T(8,128)(2,1)}), bf16[1,16,16,1152]{3,2,0,1:T(8,128)(2,1)S(1)}, u32[]{:S(2)}, u32[]{:S(2)}) %all-to-all-start.2) | async-done | bytes 589856 | tf_op jit(solution)/shard_map/all_to_all | solution.py:1310
  560.7 9.7 down_grad.3
  573.2 64.7 %collective-permute-done.44.came_far.came_own = bf16[2,4,144,1152]{3,2,1,0:T(8,128)(2,1)} collective-permute-done((bf16[2,4,144,1152]{3,2,1,0:T(8,128)(2,1)}, bf16[2,4,144,1152]{3,2,1,0:T(8,128)(2,1)}, u32[]{:S(2)}, u32[]{:S(2)}) %collective-permute-start.44) | collective-permute-done | bytes 2654240 | tf_op jit(solution)/shard_map/ppermute | solution.py:857
  643.5 21.4 %mlp_back.3 = (f32[256,1152]{1,0:T(8,128)}, bf16[4,256,1152]{2,1,0:T(8,128)(2,1)}, bf16[2,256,576]{2,1,0:T(8,128)(2,1)}, f32[8,1152]{1,0:T(8,128)}) custom-call(s32[4]{0:T(128)} %pad_add_fusion.where_ref.where, bf16[256,1152]{1,0:T(8,128)(2,1)} %bitcast.192, f32[8,1152]{1,0:T(8,128)} %pad.7.refs_1_.refs_2_, ...), custom_call_target="tpu_custom_call" | custom-call | flops 5435817984 | bytes 31924224 | tf_op jit(solution)/shard_map/mlp_back/pallas_call | solution.py:148
  683.0 12.2 %attend_back.3.refs_1_.refs_0_ = bf16[4,256,864]{2,1,0:T(8,128)(2,1)} custom-call(s32[4]{0:T(128)} %pad_add_fusion.where_ref.where, bf16[2,256,576]{2,1,0:T(8,128)(2,1)} %get-tuple-element.255.refs_0_.refs_3_, bf16[4,576,576]{2,1,0:T(8,128)(2,1)} %get-tuple-element.185.refs_3_.refs_1_, bf16[4,256,864]{2,1,0:T(8,128)(2,1)} %get-tuple-element.183.refs_0_.refs_2_), custom_call_target="tpu_custom_call" | custom-call | flops 754974720 | bytes 6782976 | tf_op jit(solution)/shard_map/attend_back/pallas_call | solution.py:148
  720.9 40.0 %collective-permute-done.49.refs_1_ = bf16[4,144,1152]{2,1,0:T(8,128)(2,1)} collective-permute-done((bf16[4,144,1152]{2,1,0:T(8,128)(2,1)}, bf16[4,144,1152]{2,1,0:T(8,128)(2,1)}, u32[]{:S(2)}, u32[]{:S(2)}) %collective-permute-start.49) | collective-permute-done | bytes 1327136 | tf_op jit(solution)/shard_map/ppermute | solution.py:857
  763.8 10.0 qkv_back.3
  776.2 8.7 weight_grad.15
  803.6 11.6 %collective-permute-done.54.refs_1_ = bf16[144,1152]{1,0:T(8,128)(2,1)S(1)} collective-permute-done((bf16[144,1152]{1,0:T(8,128)(2,1)}, bf16[144,1152]{1,0:T(8,128)(2,1)S(1)}, u32[]{:S(2)}, u32[]{:S(2)}) %collective-permute-start.54) | collective-permute-done | bytes 331808 | tf_op jit(solution)/shard_map/ppermute | solution.py:857
  815.2 12.7 %collective-permute-done.55.refs_2_ = bf16[144,1152]{1,0:T(8,128)(2,1)S(1)} collective-permute-done((bf16[144,1152]{1,0:T(8,128)(2,1)}, bf16[144,1152]{1,0:T(8,128)(2,1)S(1)}, u32[]{:S(2)}, u32[]{:S(2)}) %collective-permute-start.55) | collective-permute-done | bytes 331808 | tf_op jit(solution)/shard_map/ppermute | solution.py:857
  884.8 12.9 %collective-permute-done.64.refs_2_ = bf16[144,1152]{1,0:T(8,128)(2,1)} collective-permute-done((bf16[144,1152]{1,0:T(8,128)(2,1)}, bf16[144,1152]{1,0:T(8,128)(2,1)}, u32[]{:S(2)}, u32[]{:S(2)}) %collective-permute-start.64) | collective-permute-done | bytes 331808 | tf_op jit(solution)/shard_map/ppermute | solution.py:857
  937.8 15.9 %collective-permute-done.72 = f32[4,2,1,72]{3,1,2,0:T(2,128)S(1)} collective-permute-done((f32[4,2,1,72]{3,1,2,0:T(2,128)S(1)}, f32[4,2,1,72]{3,1,2,0:T(2,128)S(1)}, u32[]{:S(2)}, u32[]{:S(2)}) %collective-permute-start.72) | collective-permute-done | bytes 2336 | tf_op jit(solution)/shard_map/ppermute | solution.py:877
  965.5 9.5 collective-permute-start.79
  983.4 13.9 %collective-permute-done.80.refs_2_ = bf16[144,1152]{1,0:T(8,128)(2,1)S(1)} collective-permute-done((bf16[144,1152]{1,0:T(8,128)(2,1)S(1)}, bf16[144,1152]{1,0:T(8,128)(2,1)S(1)}, u32[]{:S(2)}, u32[]{:S(2)}) %collective-permute-start.80) | collective-permute-done | bytes 331808 | tf_op jit(solution)/shard_map/ppermute | solution.py:857
  (395 shorter events, 415.5 us)
Async XLA Ops:
  36.9 370.2 %all-gather.3.cloned.1.call-start = ((), (), s32[]{:S(2)}) async-start(), calls=%async_computation.8 | async-start | bytes 34062336 | tf_op jit(solution)/shard_map/all_gather | solution.py:978
  110.7 39.1 %collective-permute-start.26 = (bf16[4,144,640]{2,1,0:T(8,128)(2,1)S(1)}, bf16[4,144,640]{2,1,0:T(8,128)(2,1)S(1)}, u32[]{:S(2)}, u32[]{:S(2)}) collective-permute-start(bf16[4,144,640]{2,1,0:T(8,128)(2,1)S(1)} %pad_maximum_fusion.7), channel_id=1, source_target_pairs={{0,1},{1,0},{2,3},{3,2},{4,5},{5,4},{6,7},{7,6},{8,9},{9,8},{10,11... | collective-permute-start | bytes 2211848 | tf_op jit(solution)/shard_map/ppermute | solution.py:857
  150.0 55.4 %collective-permute-start.15 = (bf16[2,4,144,640]{3,2,1,0:T(8,128)(2,1)S(1)}, bf16[2,4,144,640]{3,2,1,0:T(8,128)(2,1)S(1)}, u32[]{:S(2)}, u32[]{:S(2)}) collective-permute-start(bf16[2,4,144,640]{3,2,1,0:T(8,128)(2,1)S(1)} %pad_maximum_fusion.refs_2_.refs_4_), channel_id=1, source_target_pairs={{0,4},{1,5},{2,6},{3,7},{4,0},{5,1},{6,2},{7,3},{8,12},{9,13},{10,... | collective-permute-start | bytes 4423688 | tf_op jit(solution)/shard_map/ppermute | solution.py:857
  150.9 54.5 %collective-permute-start.18 = (bf16[2,4,144,512]{3,2,1,0:T(8,128)(2,1)}, bf16[2,4,144,512]{3,2,1,0:T(8,128)(2,1)S(1)}, u32[]{:S(2)}, u32[]{:S(2)}) collective-permute-start(bf16[2,4,144,512]{3,2,1,0:T(8,128)(2,1)} %pad_maximum_fusion.4.refs_6_.refs_8_), channel_id=1, source_target_pairs={{0,1},{1,0},{2,3},{3,2},{4,5},{5,4},{6,7},{7,6},{8,9},{9,8},{10,11... | collective-permute-start | bytes 3538952 | tf_op jit(solution)/shard_map/ppermute | solution.py:857
  151.4 53.1 %collective-permute-start.24 = (bf16[4,144,576]{2,1,0:T(8,128)(2,1)}, bf16[4,144,576]{2,1,0:T(8,128)(2,1)S(1)}, u32[]{:S(2)}, u32[]{:S(2)}) collective-permute-start(bf16[4,144,576]{2,1,0:T(8,128)(2,1)} %pad_maximum_fusion.8), channel_id=1, source_target_pairs={{0,1},{1,0},{2,3},{3,2},{4,5},{5,4},{6,7},{7,6},{8,9},{9,8},{10,11... | collective-permute-start | bytes 1990664 | tf_op jit(solution)/shard_map/ppermute | solution.py:857
  152.9 77.9 %collective-permute-start.19 = (bf16[2,4,144,512]{3,2,1,0:T(8,128)(2,1)}, bf16[2,4,144,512]{3,2,1,0:T(8,128)(2,1)S(1)}, u32[]{:S(2)}, u32[]{:S(2)}) collective-permute-start(bf16[2,4,144,512]{3,2,1,0:T(8,128)(2,1)} %pad_maximum_fusion.4.refs_6_.refs_8_), channel_id=1, source_target_pairs={{0,2},{1,3},{2,0},{3,1},{4,6},{5,7},{6,4},{7,5},{8,10},{9,11},{10,... | collective-permute-start | bytes 3538952 | tf_op jit(solution)/shard_map/ppermute | solution.py:857
  152.9 79.4 %collective-permute-start.16 = (bf16[2,4,144,640]{3,2,1,0:T(8,128)(2,1)S(1)}, bf16[2,4,144,640]{3,2,1,0:T(8,128)(2,1)S(1)}, u32[]{:S(2)}, u32[]{:S(2)}) collective-permute-start(bf16[2,4,144,640]{3,2,1,0:T(8,128)(2,1)S(1)} %pad_maximum_fusion.refs_2_.refs_4_), channel_id=1, source_target_pairs={{0,2},{1,3},{2,0},{3,1},{4,6},{5,7},{6,4},{7,5},{8,10},{9,11},{10,... | collective-permute-start | bytes 4423688 | tf_op jit(solution)/shard_map/ppermute | solution.py:857
  232.4 39.2 %collective-permute-start.28 = (bf16[2,4,144,640]{3,2,1,0:T(8,128)(2,1)S(1)}, bf16[2,4,144,640]{3,2,1,0:T(8,128)(2,1)}, u32[]{:S(2)}, u32[]{:S(2)}) collective-permute-start(bf16[2,4,144,640]{3,2,1,0:T(8,128)(2,1)S(1)} %pad_maximum_fusion.3.refs_1_.refs_6_), channel_id=1, source_target_pairs={{0,4},{1,5},{2,6},{3,7},{4,0},{5,1},{6,2},{7,3},{8,12},{9,13},{10,... | collective-permute-start | bytes 4423688 | tf_op jit(solution)/shard_map/ppermute | solution.py:857
  236.5 35.0 %collective-permute-start.29 = (bf16[2,4,144,640]{3,2,1,0:T(8,128)(2,1)S(1)}, bf16[2,4,144,640]{3,2,1,0:T(8,128)(2,1)}, u32[]{:S(2)}, u32[]{:S(2)}) collective-permute-start(bf16[2,4,144,640]{3,2,1,0:T(8,128)(2,1)S(1)} %pad_maximum_fusion.3.refs_1_.refs_6_), channel_id=1, source_target_pairs={{0,2},{1,3},{2,0},{3,1},{4,6},{5,7},{6,4},{7,5},{8,10},{9,11},{10,... | collective-permute-start | bytes 4423688 | tf_op jit(solution)/shard_map/ppermute | solution.py:857
  259.8 74.1 %collective-permute-start.34 = (bf16[2,4,144,576]{3,2,1,0:T(8,128)(2,1)S(1)}, bf16[2,4,144,576]{3,2,1,0:T(8,128)(2,1)}, u32[]{:S(2)}, u32[]{:S(2)}) collective-permute-start(bf16[2,4,144,576]{3,2,1,0:T(8,128)(2,1)S(1)} %pad_maximum_fusion.1.refs_3_.refs_14_), channel_id=1, source_target_pairs={{0,4},{1,5},{2,6},{3,7},{4,0},{5,1},{6,2},{7,3},{8,12},{9,13},{10,... | collective-permute-start | bytes 3981320 | tf_op jit(solution)/shard_map/ppermute | solution.py:857
  260.7 73.6 %collective-permute-start.37 = (bf16[2,4,144,576]{3,2,1,0:T(8,128)(2,1)}, bf16[2,4,144,576]{3,2,1,0:T(8,128)(2,1)}, u32[]{:S(2)}, u32[]{:S(2)}) collective-permute-start(bf16[2,4,144,576]{3,2,1,0:T(8,128)(2,1)} %pad_maximum_fusion.2.refs_7_.refs_18_), channel_id=1, source_target_pairs={{0,1},{1,0},{2,3},{3,2},{4,5},{5,4},{6,7},{7,6},{8,9},{9,8},{10,11... | collective-permute-start | bytes 3981320 | tf_op jit(solution)/shard_map/ppermute | solution.py:857
  271.5 63.3 %collective-permute-start.30 = (bf16[2,4,144,640]{3,2,1,0:T(8,128)(2,1)}, bf16[2,4,144,640]{3,2,1,0:T(8,128)(2,1)}, u32[]{:S(2)}, u32[]{:S(2)}) collective-permute-start(bf16[2,4,144,640]{3,2,1,0:T(8,128)(2,1)} %collective-permute-done.28.refs_2_.refs_7_), channel_id=1, source_target_pairs={{0,2},{1,3},{2,0},{3,1},{4,6},{5,7},{6,4},{7,5},{8,10},{9,11},{10,... | collective-permute-start | bytes 4423688 | tf_op jit(solution)/shard_map/ppermute | solution.py:857
  271.5 73.6 %collective-permute-start.35 = (bf16[2,4,144,576]{3,2,1,0:T(8,128)(2,1)S(1)}, bf16[2,4,144,576]{3,2,1,0:T(8,128)(2,1)S(1)}, u32[]{:S(2)}, u32[]{:S(2)}) collective-permute-start(bf16[2,4,144,576]{3,2,1,0:T(8,128)(2,1)S(1)} %pad_maximum_fusion.1.refs_3_.refs_14_), channel_id=1, source_target_pairs={{0,2},{1,3},{2,0},{3,1},{4,6},{5,7},{6,4},{7,5},{8,10},{9,11},{10,... | collective-permute-start | bytes 3981320 | tf_op jit(solution)/shard_map/ppermute | solution.py:857
  272.0 73.1 %collective-permute-start.38 = (bf16[2,4,144,576]{3,2,1,0:T(8,128)(2,1)}, bf16[2,4,144,576]{3,2,1,0:T(8,128)(2,1)}, u32[]{:S(2)}, u32[]{:S(2)}) collective-permute-start(bf16[2,4,144,576]{3,2,1,0:T(8,128)(2,1)} %pad_maximum_fusion.2.refs_7_.refs_18_), channel_id=1, source_target_pairs={{0,2},{1,3},{2,0},{3,1},{4,6},{5,7},{6,4},{7,5},{8,10},{9,11},{10,... | collective-permute-start | bytes 3981320 | tf_op jit(solution)/shard_map/ppermute | solution.py:857
  365.0 33.1 %all-to-all-start.1 = ((bf16[16,2,9216]{2,1,0:T(2,128)(2,1)}), bf16[16,2,9216]{2,1,0:T(2,128)(2,1)S(1)}, u32[]{:S(2)}, u32[]{:S(2)}) async-start(bf16[16,2,9216]{2,1,0:T(2,128)(2,1)} %reshape.485), calls=%async_computation.1 | async-start | bytes 1179648 | tf_op jit(solution)/shard_map/all_to_all | solution.py:1323
  371.8 603.2 %reduce-scatter.5.cloned.1.call-start = ((), (), s32[]{:S(2)}) async-start(), calls=%async_computation.7 | async-start | bytes 12165120 | tf_op jit(solution)/shard_map/reduce_scatter | solution.py:1016
  532.6 473.0 %reduce-scatter.3.cloned.1.call-start = ((), (), s32[]{:S(2)}) async-start(), calls=%async_computation.6 | async-start | bytes 12165120 | tf_op jit(solution)/shard_map/reduce_scatter | solution.py:1016
  570.4 67.5 %collective-permute-start.44 = (bf16[2,4,144,1152]{3,2,1,0:T(8,128)(2,1)}, bf16[2,4,144,1152]{3,2,1,0:T(8,128)(2,1)}, u32[]{:S(2)}, u32[]{:S(2)}) collective-permute-start(bf16[2,4,144,1152]{3,2,1,0:T(8,128)(2,1)} %get-tuple-element.241), channel_id=1, source_target_pairs={{0,1},{1,0},{2,3},{3,2},{4,5},{5,4},{6,7},{7,6},{8,9},{9,8},{10,11... | collective-permute-start | bytes 7962632 | tf_op jit(solution)/shard_map/ppermute | solution.py:857
  571.1 104.8 %collective-permute-start.45 = (bf16[2,4,144,1152]{3,2,1,0:T(8,128)(2,1)}, bf16[2,4,144,1152]{3,2,1,0:T(8,128)(2,1)S(1)}, u32[]{:S(2)}, u32[]{:S(2)}) collective-permute-start(bf16[2,4,144,1152]{3,2,1,0:T(8,128)(2,1)} %get-tuple-element.253), channel_id=1, source_target_pairs={{0,4},{1,5},{2,6},{3,7},{4,0},{5,1},{6,2},{7,3},{8,12},{9,13},{10,... | collective-permute-start | bytes 7962632 | tf_op jit(solution)/shard_map/ppermute | solution.py:857
  671.7 35.3 %collective-permute-start.48 = (bf16[4,144,1152]{2,1,0:T(8,128)(2,1)}, bf16[4,144,1152]{2,1,0:T(8,128)(2,1)}, u32[]{:S(2)}, u32[]{:S(2)}) collective-permute-start(bf16[4,144,1152]{2,1,0:T(8,128)(2,1)} %get-tuple-element.261), channel_id=1, source_target_pairs={{0,4},{1,5},{2,6},{3,7},{4,0},{5,1},{6,2},{7,3},{8,12},{9,13},{10,... | collective-permute-start | bytes 3981320 | tf_op jit(solution)/shard_map/ppermute | solution.py:857
  717.5 57.2 %collective-permute-start.52 = (bf16[2,4,144,1152]{3,2,1,0:T(8,128)(2,1)}, bf16[2,4,144,1152]{3,2,1,0:T(8,128)(2,1)S(1)}, u32[]{:S(2)}, u32[]{:S(2)}) collective-permute-start(bf16[2,4,144,1152]{3,2,1,0:T(8,128)(2,1)} %get-tuple-element.274), channel_id=1, source_target_pairs={{0,2},{1,3},{2,0},{3,1},{4,6},{5,7},{6,4},{7,5},{8,10},{9,11},{10,... | collective-permute-start | bytes 7962632 | tf_op jit(solution)/shard_map/ppermute | solution.py:857
  717.5 57.2 %collective-permute-start.53 = (bf16[2,4,144,1152]{3,2,1,0:T(8,128)(2,1)}, bf16[2,4,144,1152]{3,2,1,0:T(8,128)(2,1)}, u32[]{:S(2)}, u32[]{:S(2)}) collective-permute-start(bf16[2,4,144,1152]{3,2,1,0:T(8,128)(2,1)} %get-tuple-element.264), channel_id=1, source_target_pairs={{0,2},{1,3},{2,0},{3,1},{4,6},{5,7},{6,4},{7,5},{8,10},{9,11},{10,... | collective-permute-start | bytes 7962632 | tf_op jit(solution)/shard_map/ppermute | solution.py:857
  718.0 42.8 %collective-permute-start.49 = (bf16[4,144,1152]{2,1,0:T(8,128)(2,1)}, bf16[4,144,1152]{2,1,0:T(8,128)(2,1)}, u32[]{:S(2)}, u32[]{:S(2)}) collective-permute-start(bf16[4,144,1152]{2,1,0:T(8,128)(2,1)} %get-tuple-element.266), channel_id=1, source_target_pairs={{0,1},{1,0},{2,3},{3,2},{4,5},{5,4},{6,7},{7,6},{8,9},{9,8},{10,11... | collective-permute-start | bytes 3981320 | tf_op jit(solution)/shard_map/ppermute | solution.py:857
  718.8 121.6 %collective-permute-start.59 = (bf16[2,4,144,1152]{3,2,1,0:T(8,128)(2,1)}, bf16[2,4,144,1152]{3,2,1,0:T(8,128)(2,1)}, u32[]{:S(2)}, u32[]{:S(2)}) collective-permute-start(bf16[2,4,144,1152]{3,2,1,0:T(8,128)(2,1)} %get-tuple-element.283), channel_id=1, source_target_pairs={{0,1},{1,0},{2,3},{3,2},{4,5},{5,4},{6,7},{7,6},{8,9},{9,8},{10,11... | collective-permute-start | bytes 7962632 | tf_op jit(solution)/shard_map/ppermute | solution.py:857
  784.9 117.5 %collective-permute-start.66 = (bf16[2,4,144,1152]{3,2,1,0:T(8,128)(2,1)}, bf16[2,4,144,1152]{3,2,1,0:T(8,128)(2,1)S(1)}, u32[]{:S(2)}, u32[]{:S(2)}) collective-permute-start(bf16[2,4,144,1152]{3,2,1,0:T(8,128)(2,1)} %get-tuple-element.296), channel_id=1, source_target_pairs={{0,4},{1,5},{2,6},{3,7},{4,0},{5,1},{6,2},{7,3},{8,12},{9,13},{10,... | collective-permute-start | bytes 7962632 | tf_op jit(solution)/shard_map/ppermute | solution.py:857
  851.5 47.8 %collective-permute-start.65 = (bf16[144,1152]{1,0:T(8,128)(2,1)}, bf16[144,1152]{1,0:T(8,128)(2,1)S(1)}, u32[]{:S(2)}, u32[]{:S(2)}) collective-permute-start(bf16[144,1152]{1,0:T(8,128)(2,1)} %get-tuple-element.267), channel_id=1, source_target_pairs={{0,24},{1,25},{2,26},{3,27},{4,28},{5,29},{6,30},{7,31},{8,0},{9,1... | collective-permute-start | bytes 995336 | tf_op jit(solution)/shard_map/ppermute | solution.py:857
  859.7 38.1 %collective-permute-start.64 = (bf16[144,1152]{1,0:T(8,128)(2,1)}, bf16[144,1152]{1,0:T(8,128)(2,1)}, u32[]{:S(2)}, u32[]{:S(2)}) collective-permute-start(bf16[144,1152]{1,0:T(8,128)(2,1)} %get-tuple-element.291), channel_id=1, source_target_pairs={{0,16},{1,17},{2,18},{3,19},{4,20},{5,21},{6,22},{7,23},{8,24},{9,... | collective-permute-start | bytes 995336 | tf_op jit(solution)/shard_map/ppermute | solution.py:857
  872.8 50.1 %all-to-all-start.3 = ((bf16[16,2,9216]{2,1,0:T(2,128)(2,1)}), bf16[16,2,9216]{2,1,0:T(2,128)(2,1)}, u32[]{:S(2)}, u32[]{:S(2)}) async-start(bf16[16,2,9216]{2,1,0:T(2,128)(2,1)} %reshape.487), calls=%async_computation.3 | async-start | bytes 1179648 | tf_op jit(solution)/shard_map/all_to_all | solution.py:1323
  878.4 37.9 %collective-permute-start.68 = (bf16[4,144,1152]{2,1,0:T(8,128)(2,1)}, bf16[4,144,1152]{2,1,0:T(8,128)(2,1)}, u32[]{:S(2)}, u32[]{:S(2)}) collective-permute-start(bf16[4,144,1152]{2,1,0:T(8,128)(2,1)} %get-tuple-element.300), channel_id=1, source_target_pairs={{0,4},{1,5},{2,6},{3,7},{4,0},{5,1},{6,2},{7,3},{8,12},{9,13},{10,... | collective-permute-start | bytes 3981320 | tf_op jit(solution)/shard_map/ppermute | solution.py:857
  883.2 38.9 %collective-permute-start.50 = (s32[1]{0:T(128)}, s32[1]{0:T(128)}, u32[]{:S(2)}, u32[]{:S(2)}) collective-permute-start(s32[1]{0:T(128)} %param.18), channel_id=1, source_target_pairs={{0,1},{1,0},{2,3},{3,2},{4,5},{5,4},{6,7},{7,6},{8,9},{9,8},{10,11... | collective-permute-start | bytes 20 | tf_op jit(solution)/shard_map/ppermute | solution.py:857
  909.1 44.6 %collective-permute-start.73 = (bf16[4,144,1152]{2,1,0:T(8,128)(2,1)}, bf16[4,144,1152]{2,1,0:T(8,128)(2,1)S(1)}, u32[]{:S(2)}, u32[]{:S(2)}) collective-permute-start(bf16[4,144,1152]{2,1,0:T(8,128)(2,1)} %get-tuple-element.308), channel_id=1, source_target_pairs={{0,1},{1,0},{2,3},{3,2},{4,5},{5,4},{6,7},{7,6},{8,9},{9,8},{10,11... | collective-permute-start | bytes 3981320 | tf_op jit(solution)/shard_map/ppermute | solution.py:857
  957.7 39.6 %collective-permute-start.81 = (bf16[144,1152]{1,0:T(8,128)(2,1)}, bf16[144,1152]{1,0:T(8,128)(2,1)S(1)}, u32[]{:S(2)}, u32[]{:S(2)}) collective-permute-start(bf16[144,1152]{1,0:T(8,128)(2,1)} %get-tuple-element.309), channel_id=1, source_target_pairs={{0,24},{1,25},{2,26},{3,27},{4,28},{5,29},{6,30},{7,31},{8,0},{9,1... | collective-permute-start | bytes 995336 | tf_op jit(solution)/shard_map/ppermute | solution.py:857
  (103 other events, 1477.4 us)
Sparse Core Ops, SparseCore 0:
  150.1 256.8 all-gather.2
  462.1 177.1 reduce-scatter.4
  646.5 178.3 reduce-scatter.2

commit v2 on v1

v2 whole, which is shorter than its diff:
```python
import math
from functools import partial

import jax
import jax.numpy as jnp
from jax import lax
from jax.experimental import pallas as pl
from jax.experimental.pallas import tpu as pltpu
from jax.sharding import Mesh
from jax.sharding import PartitionSpec as P

HEADS = 16
EPSILON = 1e-06
PRECISE = lax.Precision.HIGHEST
LOW = jnp.bfloat16
FULL = jnp.float32


def time_features(step_ids, features):
    half_width = features // 2
    frequency = jnp.exp(-math.log(10000.0) * jnp.arange(half_width, dtype=FULL) / half_width)
    angles = step_ids.astype(FULL)[:, None] * frequency[None, :]
    return jnp.concatenate([jnp.cos(angles), jnp.sin(angles)], axis=-1)


def normalize(values):
    centred = values - jnp.mean(values, axis=-1, keepdims=True)
    inverse = lax.rsqrt(jnp.mean(centred * centred, axis=-1, keepdims=True) + EPSILON)
    return centred * inverse, inverse


def normalize_back(grad_norm, normed, inverse):
    return inverse * (
        grad_norm
        - jnp.mean(grad_norm, axis=-1, keepdims=True)
        - normed * jnp.mean(grad_norm * normed, axis=-1, keepdims=True)
    )


def matmul(left, right):
    return jnp.dot(left, right, preferred_element_type=FULL)


def matmul_nt(left, right):
    return lax.dot_general(left, right, (((1,), (1,)), ((), ())), preferred_element_type=FULL)


def matmul_tn(left, right):
    return lax.dot_general(left, right, (((0,), (0,)), ((), ())), preferred_element_type=FULL)


def in_order(pieces, first):
    count = len(pieces)
    return [lax.select_n((k - first) % count, *pieces) for k in range(count)]


def pick(array, axis, index):
    return lax.dynamic_index_in_dim(array, index, axis, keepdims=False)


LIMIT = 60 * 2**20
TINY = pl.CostEstimate(flops=1, bytes_accessed=1, transcendentals=0)
CHIPS_Y = 2


def at_rows(index, rows):
    return pl.ds(pl.multiple_of(index * rows, 16), rows)


class Weight:
    def __init__(self, depth, rows, cols, strips):
        self.depth, self.rows, self.cols, self.strips = depth, rows, cols, strips
        self.width = max(strip[6] + strip[7] for strip in strips)
        self.arrays = []
        for strip in strips:
            if not any(strip[0][0] is array for array in self.arrays):
                self.arrays += strip[0]

    def scratch(self):
        return [
            pltpu.VMEM((2, 2 * self.depth * self.rows, self.width), LOW),
            pltpu.SemaphoreType.DMA((2, 2, self.depth * len(self.strips))),
        ]

    def copies(self, where, refs, held, sems):
        found = []
        for side in range(2):
            group = []
            x = lax.rem(where[3] + side, 2)
            for turn in range(2):
                y = lax.rem(where[1] + turn, 2)
                for ahead in range(self.depth):
                    z = lax.rem(where[0] + ahead, self.depth)
                    at = (z * CHIPS_Y + y) * self.rows
                    for number, strip in enumerate(self.strips):
                        arrays, x_first, z_placed, source_lane, row, rows, lane, lanes = strip
                        base = [k for k, a in enumerate(self.arrays) if a is arrays[0]][0]
                        first, second = (side, turn) if x_first else (turn, side)
                        source = refs[base + second].at[
                            first,
                            z if z_placed else ahead,
                            :,
                            source_lane : source_lane + lanes,
                        ]
                        start = pl.multiple_of(at + row, 16)
                        target = held.at[x, pl.ds(start, rows), lane : lane + lanes]
                        sem = sems.at[side, turn, ahead * len(self.strips) + number]
                        group.append(pltpu.make_async_copy(source, target, sem))
            found.append(group)
        return found


def start_all(copies):
    for copy in copies:
        copy.start()


def wait_all(copies):
    for copy in copies:
        copy.wait()


def dot(left, right):
    return lax.dot_general(left, right, (((1,), (0,)), ((), ())), preferred_element_type=FULL)


def dot_nt(left, right):
    return lax.dot_general(left, right, (((1,), (1,)), ((), ())), preferred_element_type=FULL)


def dot_tn(left, right):
    return lax.dot_general(left, right, (((0,), (0,)), ((), ())), preferred_element_type=FULL)


def call(body, where, ins, outs, scratch, flops, name, after=()):
    count = len(ins)

    def kernel(where_ref, *refs):
        body(where_ref, *refs[:count], *refs[count + len(after) :])

    vmem = pl.BlockSpec(memory_space=pltpu.VMEM)
    hbm = pl.BlockSpec(memory_space=pl.ANY)
    size = sum(a.size * a.dtype.itemsize for a, _ in ins)
    size += sum(math.prod(o.shape) * o.dtype.itemsize for o in outs)
    return pl.pallas_call(
        kernel,
        out_shape=outs,
        in_specs=[pl.BlockSpec(memory_space=pltpu.SMEM)]
        + [vmem if inside else hbm for _, inside in ins]
        + [hbm] * len(after),
        out_specs=[vmem] * len(outs),
        scratch_shapes=scratch,
        compiler_params=pltpu.CompilerParams(vmem_limit_bytes=LIMIT),
        cost_estimate=TINY,
        name=name,
    )(where, *[a for a, _ in ins], *after)


def shape(dims, dtype):
    return jax.ShapeDtypeStruct(dims, dtype)


def by_place(first, pair):
    return [jnp.where(first, pair[0], pair[1]), jnp.where(first, pair[1], pair[0])]


def two_cores(refs):
    return jnp.concatenate([ref[...].astype(FULL) for ref in refs], axis=0)


def add_core(part, came):
    count = part.shape[0] // 2
    part, came = part[...].astype(FULL), came[...].astype(FULL)
    return jnp.concatenate([part[:count] + came[count:], part[count:] + came[:count]], axis=0)


def norm_qkv(where, rows, mods, weight, cols):
    count, features = rows[0].shape
    count *= 2
    many = len(weight.arrays)
    thin = weight.cols - cols
    chips = 2 * weight.depth
    part = weight.rows // 2

    def body(where, own, other, mods, *refs):
        sources, (hidden, out_weight, out, held, sems) = refs[:many], refs[many:]
        copies = weight.copies(where, sources, held, sems)
        for group in copies:
            start_all(group)
        normed, _ = normalize(two_cores((own, other)))
        value = (normed * (1.0 + mods[1:2]) + mods[0:1]).astype(LOW)
        hidden[0] = value
        for side in range(2):
            x = lax.rem(where[3] + side, 2)
            wait_all(copies[side])
            out[x] = dot(value, held[x, :, :cols]).astype(LOW)
            strips = held[x, :, cols:].astype(FULL).reshape(chips, 2, part, thin)
            both = [strips[:, k].reshape(chips * part, thin) for k in range(2)]
            out_weight[x] = jnp.concatenate(both, axis=1).astype(LOW)

    return call(
        body,
        where,
        [(a, True) for a in (*rows, mods)] + [(w, False) for w in weight.arrays],
        [
            shape((1, count, features), LOW),
            shape((2, chips * part, 2 * thin), LOW),
            shape((2, count, cols), LOW),
        ],
        weight.scratch(),
        4 * count * features * cols,
        "norm_qkv",
    )


def head_slices(qkv, rows, number, heads, head):
    def column(slot):
        per = 3 * heads // 2
        x, at = divmod(slot, per)
        return qkv[x, rows, at * head : (at + 1) * head]

    return column(number), column(heads + number), column(2 * heads + number)


def probabilities(query, key, mask, factor):
    scores = dot_nt(key, query) * factor
    if mask is not None:
        scores = jnp.where(mask, scores, -1e30)
    weights = jnp.exp(scores - jnp.max(scores, axis=0, keepdims=True))
    return weights * (1.0 / jnp.sum(weights, axis=0, keepdims=True))


def attend_out(where, qkv, out_weight, marks, head):
    _, count, cols = qkv.shape
    heads = 2 * cols // (3 * head)
    size = count // 2

    def body(where, qkv, out_weight, *refs):
        mask = None
        if marks is not None:
            mask = refs[0][...] == refs[1][...]
        attended, part = refs[-2:]
        for block in range(2):
            rows = slice(block * size, (block + 1) * size)
            mixed = []
            for number in range(heads):
                query, key, value = head_slices(qkv, rows, number, heads, head)
                probs = probabilities(query, key, mask, head ** (-0.5)).astype(LOW)
                mixed.append(dot_tn(value, probs))
            result = jnp.concatenate(mixed, axis=0).T.astype(LOW)
            attended[0, rows] = result
            sides = [dot(result, out_weight[x]) for x in range(2)]
            part[rows] = jnp.concatenate(sides, axis=1).astype(LOW)

    ins = [(qkv, True), (out_weight, True)] + ([] if marks is None else [(m, True) for m in marks])
    return call(
        body,
        where,
        ins,
        [shape((1, count, heads * head), LOW), shape((count, 2 * out_weight.shape[2]), LOW)],
        [],
        8 * heads * count * size * head,
        "attend_out",
    )


GELU_A = math.sqrt(2.0 / math.pi)
GELU_B = 0.044715


def gelu(value):
    inner = GELU_A * (value + GELU_B * value * value * value)
    return 0.5 * value * (1.0 + jnp.tanh(inner))


def gelu_slope(value):
    square = value * value
    bend = jnp.tanh(GELU_A * (value + GELU_B * square * value))
    return 0.5 * (1.0 + bend) + 0.5 * value * (1.0 - bend * bend) * GELU_A * (
        1.0 + 3.0 * GELU_B * square
    )


def norm_up(where, part, came, rows, mods, weight):
    count, features = part.shape
    cols, many = weight.cols, len(weight.arrays)

    def body(where, part, came, own, other, mods, *refs):
        sources, (branch, middle, hidden, pre, act, held, sems) = refs[:many], refs[many:]
        copies = weight.copies(where, sources, held, sems)
        for group in copies:
            start_all(group)
        value = add_core(part, came)
        branch[...] = value
        total = two_cores((own, other)) + mods[2:3] * value
        middle[...] = total
        normed, _ = normalize(total)
        value = (normed * (1.0 + mods[4:5]) + mods[3:4]).astype(LOW)
        hidden[0] = value
        for side in range(2):
            x = lax.rem(where[3] + side, 2)
            wait_all(copies[side])
            before = dot(value, held[x])
            pre[x] = before.astype(LOW)
            act[x] = gelu(before).astype(LOW)

    dims = (count, features)
    return call(
        body,
        where,
        [(a, True) for a in (part, came, *rows, mods)] + [(w, False) for w in weight.arrays],
        [shape(dims, FULL), shape(dims, FULL), shape((1,) + dims, LOW)]
        + [shape((2, count, cols), LOW)] * 2,
        weight.scratch(),
        4 * count * features * cols,
        "norm_up",
    )


def down_part(where, act, weight):
    _, count, wide = act.shape
    many = len(weight.arrays)

    def body(where, act, *refs):
        sources, (out, held, sems) = refs[:many], refs[many:]
        copies = weight.copies(where, sources, held, sems)
        for group in copies:
            start_all(group)
        totals = []
        for side in range(2):
            place = lax.rem(where[3] + side, 2)
            wait_all(copies[side])
            total = dot(act[0], held[place, :wide]) + dot(act[1], held[place, wide:])
            totals.append(total[:, : weight.cols].astype(LOW))
        out[...] = jnp.concatenate(by_place(where[3] == 0, totals), axis=1)

    return call(
        body,
        where,
        [(act, True)] + [(w, False) for w in weight.arrays],
        [shape((count, 2 * weight.cols), LOW)],
        weight.scratch(),
        8 * count * wide * weight.cols,
        "down_part",
    )[0]


def finish(where, part, came, middle, mods):
    count, features = part.shape

    def body(where, part, came, middle, mods, mlp, out):
        total = add_core(part, came)
        mlp[...] = total
        size = count // 2
        out[...] = (middle[:size] + mods[5:6] * total[:size]).astype(LOW)

    return call(
        body,
        where,
        [(a, True) for a in (part, came, middle, mods)],
        [shape((count, features), FULL), shape((count // 2, features), LOW)],
        [],
        0,
        "finish",
    )


def column_sums(*values):
    sums = [jnp.sum(v, axis=0, keepdims=True) for v in values]
    fill = jnp.zeros((8 - len(sums), sums[0].shape[1]), FULL)
    return jnp.concatenate(sums + [fill], axis=0)


def mlp_back(where, grads, mods, pre, up, down):
    count, features = grads[0].shape
    count *= 2
    wide = pre.shape[-1]
    cols = down.cols
    many_up, many_down = len(up.arrays), len(down.arrays)

    def body(where, own, other, mods, pre, *refs):
        ups, downs = refs[:many_up], refs[many_up : many_up + many_down]
        grad_mlp, grad_pre, part, up_held, up_sems, down_held, down_sems = refs[many_up + many_down :]
        down_copies = down.copies(where, downs, down_held, down_sems)
        up_copies = up.copies(where, ups, up_held, up_sems)
        for group in down_copies + up_copies:
            start_all(group)
        scaled = (mods[5:6] * two_cores((own, other))).astype(LOW)
        sides = [scaled[:, s * cols : (s + 1) * cols] for s in range(2)]
        for s in range(2):
            grad_mlp[s] = sides[s]
        wait_all(down_copies[0] + down_copies[1])
        total = None
        for side in range(2):
            x = lax.rem(where[3] + side, 2)
            rows = pl.ds(pl.multiple_of(x * wide, 16), wide)
            grad_act = dot_nt(sides[0], down_held[0, rows, :cols]) + dot_nt(
                sides[1], down_held[1, rows, :cols]
            )
            value = (gelu_slope(pre[x].astype(FULL)) * grad_act).astype(LOW)
            grad_pre[x] = value
            wait_all(up_copies[side])
            piece = dot_nt(value, up_held[x])
            total = piece if total is None else total + piece
        part[...] = total.astype(LOW)

    return call(
        body,
        where,
        [(a, True) for a in (*grads, mods, pre)] + [(w, False) for w in up.arrays + down.arrays],
        [
            shape((2, count, cols), LOW),
            shape((2, count, wide), LOW),
            shape((count, features), LOW),
        ],
        up.scratch() + down.scratch(),
        8 * count * features * wide,
        "mlp_back",
    )


def attend_grad(
    where, part, came, grads, mods, middle, branch, mlp, out_weight, qkv, marks, head
):
    _, count, cols = qkv.shape
    heads = 2 * cols // (3 * head)
    factor = head ** (-0.5)
    features = part.shape[1]
    wide = features // 2
    size = count // 2

    def body(where, part, came, own, other, mods, middle, branch, mlp, out_weight, qkv, *refs):
        mask = None
        if marks is not None:
            mask = refs[0][...] == refs[1][...]
        grad_mid, grad_branch, sums, out = refs[-4:]
        incoming = two_cores((own, other))
        total = add_core(part, came)
        normed, inverse = normalize(middle[...])
        result = incoming + normalize_back(total * (1.0 + mods[4:5]), normed, inverse)
        grad_mid[...] = result
        sums[...] = column_sums(result * branch[...], total, total * normed, incoming * mlp[...])
        scaled = (mods[2:3] * result).astype(LOW)
        sides = [scaled[:, s * wide : (s + 1) * wide] for s in range(2)]
        for s in range(2):
            grad_branch[s] = sides[s]
        attended = dot_nt(sides[0], out_weight[0]) + dot_nt(sides[1], out_weight[1])
        attended = attended.astype(LOW)
        for block in range(2):
            rows = slice(block * size, (block + 1) * size)
            pieces = [None] * (3 * heads)
            for number in range(heads):
                grad = attended[rows, number * head : (number + 1) * head]
                query, key, value = head_slices(qkv, rows, number, heads, head)
                probs = probabilities(query, key, mask, factor)
                grad_probs = dot_nt(value, grad)
                delta = jnp.sum(grad_probs * probs, axis=0, keepdims=True)
                grad_scores = (probs * (grad_probs - delta)).astype(LOW)
                pieces[number] = (dot_tn(key, grad_scores).T * factor).astype(LOW)
                pieces[heads + number] = (dot(grad_scores, query) * factor).astype(LOW)
                pieces[2 * heads + number] = dot(probs.astype(LOW), grad).astype(LOW)
            per = 3 * heads // 2
            for x in range(2):
                out[x, rows] = jnp.concatenate(pieces[x * per : (x + 1) * per], axis=1)

    ins = [(a, True) for a in (part, came, *grads, mods, middle, branch, mlp, out_weight, qkv)]
    ins += [] if marks is None else [(m, True) for m in marks]
    return call(
        body,
        where,
        ins,
        [
            shape((count, features), FULL),
            shape((2, count, wide), LOW),
            shape((8, features), FULL),
            shape((2, count, cols), LOW),
        ],
        [],
        20 * heads * count * size * head,
        "attend_grad",
    )


def qkv_part(where, grad_qkv, weight, features):
    _, count, cols = grad_qkv.shape
    many = len(weight.arrays)

    def body(where, grad_qkv, *refs):
        sources, (out, held, sems) = refs[:many], refs[many:]
        copies = weight.copies(where, sources, held, sems)
        for group in copies:
            start_all(group)
        total = None
        for side in range(2):
            x = lax.rem(where[3] + side, 2)
            wait_all(copies[side])
            piece = dot_nt(grad_qkv[x], held[x, :, :cols])
            total = piece if total is None else total + piece
        out[...] = total.astype(LOW)

    return call(
        body,
        where,
        [(grad_qkv, True)] + [(w, False) for w in weight.arrays],
        [shape((count, features), LOW)],
        weight.scratch(),
        4 * count * features * cols,
        "qkv_part",
    )[0]


def finish_back(where, part, came, rows, mods, grad_mid):
    count, features = part.shape

    def body(where, part, came, own, other, mods, grad_mid, out, sums):
        total = add_core(part, came)
        normed, inverse = normalize(two_cores((own, other)))
        back = normalize_back(total * (1.0 + mods[1:2]), normed, inverse)
        sums[...] = column_sums(total, total * normed)
        size = count // 2
        out[...] = (grad_mid[:size] + back[:size]).astype(LOW)

    return call(
        body,
        where,
        [(a, True) for a in (part, came, *rows, mods, grad_mid)],
        [shape((count // 2, features), LOW), shape((8, features), FULL)],
        [],
        0,
        "finish_back",
    )


def weight_grad(where, left, right, tail, depth, cut):
    blocks, count, wide = left.shape
    rows = blocks * wide // (2 * depth)
    cols = right.shape[-1]
    operands = [left, right]
    scratch = [pltpu.VMEM((blocks * wide, count), LOW)]
    if tail is not None:
        size, thin = tail[0].shape[-1], tail[1].shape[-1] // 2
        operands += tail
        scratch.append(pltpu.VMEM((size, count), LOW))
        cols += thin
    many = len(operands)
    cuts = [(at, to) for at, to in ((0, cut), (cut, cols)) if to > at]

    def kernel(where, *refs):
        ins, outs, held = refs[:many], refs[many : -len(scratch)], refs[-len(scratch) :]
        z = pl.program_id(0)

        @pl.when(z == 0)
        def _():
            for source, flipped in zip(ins[::2], held):
                size = source.shape[-1]
                for block in range(source.shape[0]):
                    flipped[block * size : (block + 1) * size] = source[block].T

        chosen = []
        for flipped in held:
            size = flipped.shape[0] // depth
            chosen.append(flipped[pl.ds(pl.multiple_of(z * size, 16), size)])

        for turn, x in enumerate((1 - where[3], where[3])):
            value = dot(chosen[0], ins[1][x])
            value = [value[:rows], value[rows:]]
            if tail is not None:
                more = dot(chosen[1], ins[3][x])
                size = more.shape[0] // 2
                for y in range(2):
                    part = more[y * size : (y + 1) * size]
                    strips = jnp.concatenate([part[:, :thin], part[:, thin:]], axis=0)
                    value[y] = jnp.concatenate([value[y], strips], axis=1)
            own, other = by_place(where[1] == 0, value)
            for number, (at, to) in enumerate(cuts):
                outs[4 * number + 2 * turn][0] = other[:, at:to].astype(LOW)
                outs[4 * number + 2 * turn + 1][0] = own[:, at:to].astype(LOW)

    def whole(a):
        return pl.BlockSpec(a.shape, lambda i, s: (0,) * len(a.shape))

    widths = [to - at for at, to in cuts for _ in range(4)]
    return pl.pallas_call(
        kernel,
        out_shape=[shape((depth, rows, w), LOW) for w in widths],
        grid_spec=pltpu.PrefetchScalarGridSpec(
            num_scalar_prefetch=1,
            grid=(depth,),
            in_specs=[whole(a) for a in operands],
            out_specs=[pl.BlockSpec((1, rows, w), lambda i, s: (i, 0, 0)) for w in widths],
            scratch_shapes=scratch,
        ),
        compiler_params=pltpu.CompilerParams(vmem_limit_bytes=LIMIT),
        cost_estimate=TINY,
        name="weight_grad",
    )(where, *operands)


def add_all(where, *arrays):
    depth, rows, cols = arrays[0].shape

    def kernel(where, *refs):
        total = refs[0][...].astype(FULL)
        for ref in refs[1:-1]:
            total = total + ref[...].astype(FULL)
        refs[-1][...] = total.astype(LOW)

    moving = pl.BlockSpec((1, rows, cols), lambda i, s: (i, 0, 0))
    return pl.pallas_call(
        kernel,
        out_shape=shape((depth, rows, cols), LOW),
        grid_spec=pltpu.PrefetchScalarGridSpec(
            num_scalar_prefetch=1,
            grid=(depth,),
            in_specs=[moving] * len(arrays),
            out_specs=moving,
        ),
        compiler_params=pltpu.CompilerParams(vmem_limit_bytes=LIMIT),
        cost_estimate=TINY,
        name="add_all",
    )(where, *arrays)


def add_planes(where, *strips):
    depth, rows, _ = strips[0][0].shape
    count = len(strips[0])
    cols = sum(a.shape[-1] for a in strips[0])

    def body(where, *refs):
        ins, outs = refs[: count * len(strips)], refs[count * len(strips) :]
        for ahead, out in enumerate(outs):
            z = lax.rem(where[0] + ahead, depth)
            at = 0
            for number in range(count):
                total = ins[number][z].astype(FULL)
                for ref in ins[number + count :: count]:
                    total = total + ref[z].astype(FULL)
                wide = total.shape[-1]
                out[:, at : at + wide] = total.astype(out.dtype)
                at += wide

    return call(
        body,
        where,
        [(a, True) for group in strips for a in group],
        [shape((rows, cols), FULL)] + [shape((rows, cols), LOW)] * (depth - 1),
        [],
        0,
        "add_planes",
    )


def add_planes_last(where, *planes):
    def body(where, *refs):
        total = refs[0][...]
        for ref in refs[1:-1]:
            total = total + ref[...].astype(FULL)
        refs[-1][...] = total

    outs = [shape(planes[0].shape, FULL)]
    return call(body, where, [(p, True) for p in planes], outs, [], 0, "add_planes_last")[0]


def part_rows(where, totals, cols):
    rows = totals[0].shape[0]
    wide = sum(t.shape[1] for t in totals)
    part, thin = rows // 2, wide - cols

    def body(where, *refs):
        ins, outs = refs[: len(totals)], refs[len(totals) :]
        total = jnp.concatenate([ref[...].astype(FULL) for ref in ins], axis=1)
        mine, theirs = by_place(where[2] == 0, [total[:part, :cols], total[part:, :cols]])
        if thin:
            outs[0][...] = jnp.concatenate([total[:part, cols:], total[part:, cols:]], axis=1)
        outs[-2][...] = mine
        outs[-1][...] = theirs.astype(LOW)

    outs = [shape((part, cols), FULL), shape((part, cols), LOW)]
    if thin:
        outs.insert(0, shape((part, 2 * thin), FULL))
    return call(body, where, [(t, True) for t in totals], outs, [], 0, "part_rows")


def interleave(where, mine, theirs, width):
    rows, cols = mine.shape

    def body(where, mine, theirs, out):
        both = by_place(where[2] == 0, [mine[...], theirs[...].astype(FULL)])
        groups = []
        for at in range(0, cols, width):
            groups += [b[:, at : at + width] for b in both]
        out[...] = jnp.concatenate(groups, axis=1)

    return call(
        body,
        where,
        [(mine, True), (theirs, True)],
        [shape((rows, 2 * cols), FULL)],
        [],
        0,
        "interleave",
    )[0]


def deal(where, shards, widths):
    rows = shards[0].shape[0]
    cols = sum(a.shape[1] for a in shards) // 2

    def body(where, *refs):
        own, other = refs[-2:]
        halves = [[], []]
        for ref, width in zip(refs, widths):
            value = ref[...]
            for number in range(value.shape[1] // width):
                halves[number % 2].append(value[:, number * width : (number + 1) * width])
        pair = [jnp.concatenate(h, axis=1) for h in halves]
        own[...], other[...] = by_place(where[2] == 0, pair)

    return call(
        body,
        where,
        [(a, True) for a in shards],
        [shape((rows, cols), LOW)] * 2,
        [],
        0,
        "deal",
    )


def pack(where, own, got, outs, downs, cols):
    part = own.shape[0]
    rows = 2 * part
    thin = outs[0].shape[1] // 2
    wide = downs[0].shape[1]
    padded = -(-wide // 128) * 128
    count = downs[0].shape[0] // rows
    first = cols[0] + thin

    def body(where, own, got, out_s, out_t, down_s, down_t, qkv_s, mlp_s, packed):
        pair = by_place(where[2] == 0, [own[...].astype(FULL), got[...].astype(FULL)])
        both = jnp.concatenate(pair, axis=0)

        def strips(ref):
            value = ref[...].astype(FULL)
            return jnp.concatenate([value[:, :thin], value[:, thin:]], axis=0)

        def put_down(to, lane, down):
            for k in range(count):
                to[:, lane : lane + wide] = down[k * rows : (k + 1) * rows]
                if padded > wide:
                    to[:, lane + wide : lane + padded] = jnp.zeros((rows, padded - wide), LOW)
                lane += padded

        at = cols[0] + cols[1]
        qkv_s[...] = jnp.concatenate([both[:, : cols[0]], strips(out_s)], axis=1).astype(LOW)
        mlp_s[:, : cols[1]] = both[:, cols[0] : at].astype(LOW)
        put_down(mlp_s, cols[1], down_s)
        qkv_t = jnp.concatenate([both[:, at : at + cols[0]], strips(out_t)], axis=1)
        packed[:, :first] = qkv_t.astype(LOW)
        packed[:, first : first + cols[1]] = both[:, at + cols[0] :].astype(LOW)
        put_down(packed, first + cols[1], down_t)

    mlp = cols[1] + count * padded
    return call(
        body,
        where,
        [(a, True) for a in (own, got, *outs, *downs)],
        [shape((rows, first), LOW), shape((rows, mlp), LOW), shape((rows, first + mlp), LOW)],
        [],
        0,
        "pack",
    )


class Grid:
    def __init__(self, patch, seq, patch_axes, seq_axis):
        self.patch_axes, self.seq_axis = patch_axes, seq_axis
        self.every = (patch_axes if isinstance(patch_axes, tuple) else (patch_axes,)) + (seq_axis,)
        self.chips = self.every[:2] + (seq_axis,)
        self.patch, self.seq = patch, seq
        self.depth = patch // 4
        where = lax.axis_index(patch_axes)
        self.place = where
        self.core = where % 2
        self.y = (where // 2) % 2
        self.z = where // 4
        self.x = lax.axis_index(seq_axis)

    def moves(self, step):
        pairs = []
        for p in range(self.patch):
            for x in range(self.seq):
                z, y, c = p // 4, (p // 2) % 2, p % 2
                z2, y2, c2, x2 = step(z, y, c, x)
                pairs.append((p * self.seq + x, ((z2 * 2 + y2) * 2 + c2) * self.seq + x2))
        return pairs

    def send(self, array, step):
        return lax.ppermute(array, self.every, self.moves(step))

    def flip_core(self, array):
        return self.send(array, lambda z, y, c, x: (z, y, 1 - c, x))

    def flip_y(self, array):
        return self.send(array, lambda z, y, c, x: (z, 1 - y, c, x))

    def shift_x(self, array, by):
        return self.send(array, lambda z, y, c, x: (z, y, c, (x + by) % self.seq))

    def shift_z(self, array, by):
        return self.send(array, lambda z, y, c, x: ((z + by) % self.depth, y, c, x))

    def xor_patch(self, array, bit):
        pairs = [
            (p * self.seq + x, (p ^ bit) * self.seq + x)
            for p in range(self.patch)
            for x in range(self.seq)
        ]
        return lax.ppermute(array, self.every, pairs)

    def bits(self):
        bit = self.patch // 2
        while bit:
            yield bit
            bit //= 2

    def sum_patch(self, array):
        for bit in self.bits():
            array = array + self.xor_patch(array, bit)
        return array

    def join_patch(self, array, other, bit):
        mine_first = (self.place // bit) % 2 == 0
        return jnp.where(
            mine_first, jnp.concatenate([array, other]), jnp.concatenate([other, array])
        )

    def all_seq(self, array):
        return [array] + [self.shift_x(array, -j) for j in range(1, self.seq)]


class Flight:
    pass


class Split:
    def __init__(self, grid, head, group, token):
        self.grid = grid
        self.head, self.group = head, group
        self.up_cols = group * grid.patch // 4
        self.split_cut = 5 * 128
        self.token = token
        self.strict = True
        self.flights = []
        self.strict = True
        self.where = jnp.stack([grid.z, grid.y, grid.core, grid.x]).astype(jnp.int32)

    @staticmethod
    def fits(patch, seq, frames, features, hidden):
        return (
            patch == HEADS
            and patch == frames
            and seq == 2
            and features % (2 * patch) == 0
            and hidden % patch == 0
            and (2 * features // patch) % 16 == 0
            and hidden == 2 * 2 * features
            and (hidden // patch) % 32 == 0
        )


    def tie(self, *arrays):
        *arrays, self.token = lax.optimization_barrier((*arrays, self.token))
        return arrays[0] if len(arrays) == 1 else arrays

    def run(self, kernel, first, *rest):
        if isinstance(first, (list, tuple)):
            head, *tail = first
            if isinstance(head, tuple):
                first = [(self.tie(head[0]), *head[1:]), *tail]
            else:
                first = [self.tie(head), *tail]
        else:
            first = self.tie(first)
        result = kernel(self.where, first, *rest)
        if not self.strict:
            self.token = result[-1] if isinstance(result, (list, tuple)) else result
            return result
        if isinstance(result, (list, tuple)):
            return self.tie(*result) if len(result) > 1 else [self.tie(result[0])]
        return self.tie(result)

    def first(self, array, x_first):
        return self.grid.shift_x(array, 1) if x_first else self.grid.flip_y(array)

    def prepare(self, spatial, temporal):
        own, other = deal(
            self.where,
            [spatial[0], spatial[2], temporal[0], temporal[2]],
            [self.head, self.group] * 2,
        )
        got = self.grid.flip_core(other)
        cols = (spatial[0].shape[1] // 2, spatial[2].shape[1] // 2)
        outs, downs = [spatial[1], temporal[1]], [spatial[3], temporal[3]]
        return self.run(pack, own, got, outs, downs, cols)

    def gather_z(self, piece):
        piece = self.tie(piece)
        moves = [partial(self.grid.shift_z, by=-j) for j in range(1, self.grid.depth)]
        return piece, [self.fly(piece, move) for move in moves]

    def fly(self, array, move):
        flight = Flight()
        flight.value = move(self.tie(array))
        self.flights.append(flight)
        return flight

    def land(self, *chosen):
        chosen = chosen or tuple(self.flights)
        arrived = self.tie(*[flight.value for flight in chosen], self.token)
        for flight, value in zip(chosen, arrived):
            flight.value = value
        self.flights = [f for f in self.flights if not any(f is c for c in chosen)]

    def move_first(self, x_first):
        return partial(self.first, x_first=x_first)

    def split_rows(self, totals, cols, width):
        *rest, mine, theirs = self.run(part_rows, totals, cols)
        flight = self.fly(theirs, self.grid.flip_core)
        yield
        yield [self.run(interleave, mine, flight.value, width)] + rest

    def across_z(self, array):
        return lax.psum_scatter(array, self.grid.chips[0], scatter_dimension=0, tiled=False)

    def both(self, array):
        return [array, self.grid.flip_core(array)]

    def forward(self, rows, mods, mod_steps, shards, down_shape, marks, to_frames, to_patches):
        grid, head = self.grid, self.head
        qkv_s, mlp_s, packed = shards
        depth, count = grid.depth, qkv_s.shape[0]
        cols = qkv_s.shape[1], self.up_cols
        padded = (mlp_s.shape[1] - cols[1]) * count // down_shape[0]
        cut = self.split_cut
        chunk = 3 * head * HEADS // 4

        def halved(strips, width, placed):
            return [
                (strip.buffers, strip.x_first, placed, 0, 0, count, lane, lanes)
                for strip, lane, lanes in zip(strips, (0, cut), (cut, width - cut))
            ]

        def stacked(pieces, cuts):
            own, flights = pieces
            self.land(*flights)
            pieces = [own] + [flight.value for flight in flights]
            parts = [jnp.stack([p[:, at:to] for p in pieces]) for at, to in zip(cuts, cuts[1:])]
            parts = self.tie(*parts)
            return [Arriving(self, part, k % 2 == 0) for k, part in enumerate(parts)]

        rows = self.fly(rows, to_frames)
        pieces = self.gather_z(qkv_s)
        list(mod_steps)
        mods = mods()
        one = stacked(pieces, [0, cut, cols[0]])
        for strip in one:
            strip.first()
        self.land(rows)
        rows = self.both(rows.value)
        pieces = self.gather_z(mlp_s)
        for strip in one:
            strip.second()
        self.land(*[strip.flight for strip in one])
        two = up, down = stacked(pieces, [0, cols[1], mlp_s.shape[1]])
        held_t = lax.all_gather(self.tie(packed), grid.chips[0], axis=0)
        for strip in two:
            strip.first()
        qkv_w = Weight(depth, count, cols[0], halved(one, cols[0], False))
        hidden_one, out_w, qkv = self.run(norm_qkv, rows, mods[0], qkv_w, chunk)
        attended, part = self.run(attend_out, qkv, out_w, None, head)
        came = self.fly(part, grid.flip_core)
        for strip in two:
            strip.second()
        self.land(came)
        held_t = self.tie(held_t)
        cuts = [0, cols[0], cols[0] + cols[1]]
        cuts += [cuts[-1] + padded, cuts[-1] + 2 * padded]
        strips = [self.tie(held_t[..., at:to]) for at, to in zip(cuts, cuts[1:])]
        strips = [Arriving(self, s, k % 2 == 0) for k, s in enumerate(strips)]
        for strip in strips[:2]:
            strip.first()
        self.land(*[strip.flight for strip in two])
        up_w = Weight(
            depth, count, cols[1], [(up.buffers, True, False, 0, 0, count, 0, cols[1])]
        )
        down_w = Weight(
            depth,
            *down_shape,
            [
                (down.buffers, False, False, k * padded, k * count, count, 0, padded)
                for k in range(down_shape[0] // count)
            ],
        )
        branch, middle, hidden_two, pre, act = self.run(
            norm_up, part, came.value, rows, mods[0], up_w
        )
        part = self.run(down_part, act, down_w)
        came = self.fly(part, grid.flip_core)
        for strip in strips[:2]:
            strip.second()
        for strip in strips[2:]:
            strip.first()
        self.land(came)
        mlp, result = self.run(finish, part, came.value, middle, mods[0])
        spatial = (
            (mods[0], None, rows),
            (qkv_w, out_w, up_w, down_w),
            (hidden_one, qkv, attended, branch, middle, hidden_two, pre, act, mlp),
        )

        for strip in strips[2:]:
            strip.second()
        moved = self.fly(result, to_patches)
        self.land(moved)
        rows = [moved.value, self.fly(moved.value, grid.flip_core)]
        self.land(rows[1])
        rows[1] = rows[1].value
        self.land(*[strip.flight for strip in strips[:2]])
        early, late = strips[:2]
        qkv_w = Weight(
            depth, count, cols[0], [(early.buffers, True, True, 0, 0, count, 0, cols[0])]
        )
        up_w = Weight(
            depth, count, cols[1], [(late.buffers, False, True, 0, 0, count, 0, cols[1])]
        )
        hidden_one, out_w, qkv = self.run(norm_qkv, rows, mods[1], qkv_w, chunk)
        attended, part = self.run(attend_out, qkv, out_w, marks, head)
        came = self.fly(part, grid.flip_core)
        self.land(came)
        branch, middle, hidden_two, pre, act = self.run(
            norm_up, part, came.value, rows, mods[1], up_w
        )
        self.land()
        down_w = Weight(
            depth,
            *down_shape,
            [
                (strip.buffers, strip.x_first, True, 0, k * count, count, 0, padded)
                for k, strip in enumerate(strips[2:])
            ],
        )
        part = self.run(down_part, act, down_w)
        came = self.fly(part, grid.flip_core)
        self.land()
        mlp, result = self.run(finish, part, came.value, middle, mods[1])
        temporal = (
            (mods[1], marks, rows),
            (qkv_w, out_w, up_w, down_w),
            (hidden_one, qkv, attended, branch, middle, hidden_two, pre, act, mlp),
        )
        return result, spatial, temporal

    def grads_of(self, left, right, tail, cut, orders):
        quads = self.run(weight_grad, left, right, tail, self.grid.depth, cut)
        return [Strip(self, quads[4 * k : 4 * k + 4], order) for k, order in enumerate(orders)]

    def backward(self, spatial, temporal, grad, move, move_back, condition_steps):
        start = self.token
        self.strict = False
        head, flip = self.head, self.grid.flip_core
        (mods, marks, rows), (qkv_w, out_w, up_w, down_w), saved = temporal
        hidden_one, qkv, attended, branch, middle, hidden_two, pre, act, mlp = saved
        features = grad.shape[-1]
        wide, half = 2 * features // 2, features // 2
        chunk = 3 * half // 2
        grads = self.both(grad)
        grad_mlp, grad_pre, part = self.run(mlp_back, grads, mods, pre, up_w, down_w)
        came = self.fly(part, flip)
        (up_t,) = self.grads_of(hidden_two, grad_pre, None, wide, [True])
        self.land()

        up_t.first(0)
        (down_t,) = self.grads_of(act, grad_mlp, None, 0, [False])
        grad_mid, grad_branch, sums_two, grad_qkv = self.run(
            attend_grad,
            part,
            came.value,
            grads,
            mods,
            middle,
            branch,
            mlp,
            out_w,
            qkv,
            marks,
            head,
        )
        self.land()

        up_t.first(1)
        down_t.first(0)
        part = self.run(qkv_part, grad_qkv, qkv_w, features)
        came = self.fly(part, flip)
        (qkv_t,) = self.grads_of(hidden_one, grad_qkv, [attended, grad_branch], wide, [True])
        self.land()

        down_t.first(1)
        grad, sums_one = self.run(finish_back, part, came.value, rows, mods, grad_mid)
        mods_t = jnp.concatenate([sums_one[:2], sums_two[:4]], axis=0).reshape(1, -1)
        moved = self.fly(grad, move)
        up_t.second()
        self.land()

        qkv_t.first(0)
        grads = [moved.value, self.fly(moved.value, flip)]
        down_t.add_second()
        self.land()
        grads[1] = grads[1].value

        qkv_t.first(1)
        up_t.fly_second()
        (mods, marks, rows), (qkv_w, out_w, up_w, down_w), saved = spatial
        hidden_one, qkv, attended, branch, middle, hidden_two, pre, act, mlp = saved
        grad_mlp, grad_pre, part = self.run(mlp_back, grads, mods, pre, up_w, down_w)
        self.land()

        came = self.fly(part, flip)
        down_t.fly_second()
        (up_s,) = self.grads_of(hidden_two, grad_pre, None, wide, [False])
        (down_s,) = self.grads_of(act, grad_mlp, None, half, [True])
        up_t.total()
        self.land()

        up_s.first(0)
        down_s.first(0)
        up_z = self.across_z(up_t.sum)
        grad_mid, grad_branch, sums_two, grad_qkv = self.run(
            attend_grad,
            part,
            came.value,
            grads,
            mods,
            middle,
            branch,
            mlp,
            out_w,
            qkv,
            marks,
            head,
        )
        qkv_t.add_second()
        self.land()

        up_s.first(1)
        down_s.first(1)
        (early, late) = self.grads_of(
            hidden_one, grad_qkv, [attended, grad_branch], self.split_cut, [True, False]
        )
        part = self.run(qkv_part, grad_qkv, qkv_w, features)
        came = self.fly(part, flip)
        down_t.total()
        down_z = self.across_z(down_t.sum)
        self.land()

        early.first(0)
        late.first(0)
        qkv_t.fly_second()
        grad, sums_one = self.run(finish_back, part, came.value, rows, mods, grad_mid)
        mods_s = jnp.concatenate([sums_one[:2], sums_two[:4]], axis=0).reshape(1, -1)
        up_s.add_second()
        down_s.add_second()
        self.land()

        early.first(1)
        late.first(1)
        up_s.fly_second()
        down_s.fly_second()
        qkv_t.total()
        qkv_z = self.across_z(qkv_t.sum)
        early.add_second()
        late.add_second()
        self.land()

        early.fly_second()
        late.fly_second()
        up_s.total()
        up_sz = self.across_z(up_s.sum)
        down_s.total()
        down_sz = self.across_z(down_s.sum)
        self.land()
        self.strict = True
        self.token, _ = lax.optimization_barrier((start, self.token))
        chain = Chain(self, condition_steps(mods_s, mods_t))
        own, *planes = self.run(
            add_planes,
            [early.near[1], late.near[1]],
            [early.came[1].value, late.came[1].value],
            [early.last.value, late.last.value],
        )
        planes = [
            self.fly(plane, partial(self.grid.shift_z, by=j + 1)) for j, plane in enumerate(planes)
        ]
        for _ in range(4):
            chain.advance()
        up_t = self.split_rows([up_z], wide, self.group)
        next(up_t)
        self.land(self.flights[-1])
        (up_t,) = next(up_t)
        chain.advance()
        qkv_t = self.split_rows([qkv_z], chunk, head)
        next(qkv_t)
        self.land(self.flights[-1])
        qkv_t, out_t = next(qkv_t)
        chain.advance()
        tokens = self.fly(grad, move_back)
        chain.advance()
        self.land(*planes)
        qkv_sz = self.run(add_planes_last, own, *[plane.value for plane in planes])
        qkv_s = self.split_rows([qkv_sz], chunk, head)
        next(qkv_s)
        chain.advance()
        up_s = self.split_rows([up_sz], wide, self.group)
        next(up_s)
        chain.advance()
        self.land()
        qkv_s, out_s = next(qkv_s)
        (up_s,) = next(up_s)
        down_t, down_s = down_z.astype(FULL), down_sz.astype(FULL)
        grads = (qkv_s, out_s, up_s, down_s), (qkv_t, out_t, up_t, down_t)
        return tokens.value, chain.result, *grads


class Chain:
    def __init__(self, plan, steps):
        self.plan, self.steps = plan, steps
        self.flight = plan.fly(*next(steps))

    def advance(self):
        self.plan.land(self.flight)
        request = self.steps.send(self.flight.value)
        if isinstance(request[1], partial):
            self.flight = self.plan.fly(*request)
        else:
            self.result = request


class Arriving:
    def __init__(self, plan, held, x_first):
        self.plan, self.held, self.x_first = plan, held, x_first

    def first(self):
        self.flight = self.plan.fly(self.held, self.plan.move_first(self.x_first))

    def second(self):
        self.plan.land(self.flight)
        self.held = self.plan.tie(jnp.stack([self.held, self.flight.value]))
        self.flight = self.plan.fly(self.held, self.plan.move_first(not self.x_first))

    @property
    def buffers(self):
        return [self.held, self.flight.value]


class Strip:
    def __init__(self, plan, quads, x_first):
        self.plan, self.x_first = plan, x_first
        far = [quads[0], quads[1] if x_first else quads[2]]
        self.near = [quads[2] if x_first else quads[1], quads[3]]
        self.far, self.came = far, [None, None]

    def first(self, turn):
        self.came[turn] = self.plan.fly(self.far[turn], self.plan.move_first(self.x_first))

    def add_second(self):
        self.send = self.plan.run(add_all, self.near[0], self.came[0].value)

    def fly_second(self):
        self.last = self.plan.fly(self.send, self.plan.move_first(not self.x_first))

    def second(self):
        self.add_second()

    def total(self):
        self.sum = self.plan.run(add_all, self.near[1], self.came[1].value, self.last.value)


class WholeWeights:
    def __init__(self, grid, features, hidden):
        self.features, self.hidden = features, hidden

    def gather(self, local):
        wide = lax.all_gather(local, "seq", axis=1, tiled=True)
        return lax.all_gather(wide, "patch", axis=0, tiled=True)

    def fetch(self, spatial, temporal):
        return [[tuple(self.gather(w) for w in block)] for block in (spatial, temporal)]

    def scatter(self, grad):
        rows = lax.psum_scatter(grad.astype(LOW), "patch", scatter_dimension=0, tiled=True)
        return lax.psum_scatter(rows, "seq", scatter_dimension=1, tiled=True).astype(FULL)

    def reduce_mlp(self, hidden, grad_pre, activated, grad_mlp, flip):
        return (
            self.scatter(matmul_tn(hidden, grad_pre[0])),
            self.scatter(matmul_tn(activated[0], grad_mlp)),
        )

    def reduce_out(self, attended, grad_branch, flip):
        return self.scatter(matmul_tn(attended[0], grad_branch))

    def reduce_qkv(self, hidden, grad_qkv, flip):
        return self.scatter(matmul_tn(hidden, grad_qkv[0]))


def attention(queries, keys, mask, factor):
    scores = jnp.einsum("bphd,bkhd->bhpk", queries, keys, preferred_element_type=FULL) * factor
    if mask is not None:
        scores = jnp.where(mask, scores, -1e30)
    top = jnp.max(scores, axis=-1, keepdims=True)
    weights = jnp.exp(scores - top)
    return weights / jnp.sum(weights, axis=-1, keepdims=True)


def attend(qkv, batch, mask, head, share):
    rows = qkv.reshape(batch, -1, 3, qkv.shape[-1] // (3 * head), head)
    keys, values = share(rows[:, :, 1]), share(rows[:, :, 2])
    probs = attention(rows[:, :, 0], keys, mask, head ** (-0.5)).astype(LOW)
    mixed = jnp.einsum("bhpk,bkhd->bphd", probs, values, preferred_element_type=FULL)
    return mixed.reshape(qkv.shape[0], -1).astype(LOW)


def attend_back(grad, qkv, batch, mask, head, share, share_back):
    factor = head ** (-0.5)
    heads = qkv.shape[-1] // (3 * head)
    rows = qkv.reshape(batch, -1, 3, heads, head)
    grad_rows = grad.reshape(batch, -1, heads, head)
    queries, keys, values = rows[:, :, 0], share(rows[:, :, 1]), share(rows[:, :, 2])
    probs = attention(queries, keys, mask, factor)
    grad_probs = jnp.einsum("bphd,bkhd->bhpk", grad_rows, values, preferred_element_type=FULL)
    delta = jnp.sum(grad_probs * probs, axis=-1, keepdims=True)
    grad_scores = (probs * (grad_probs - delta)).astype(LOW)
    grad_queries = (
        jnp.einsum("bhpk,bkhd->bphd", grad_scores, keys, preferred_element_type=FULL) * factor
    )
    grad_keys = (
        jnp.einsum("bhpk,bphd->bkhd", grad_scores, queries, preferred_element_type=FULL) * factor
    )
    grad_values = jnp.einsum(
        "bhpk,bphd->bkhd", probs.astype(LOW), grad_rows, preferred_element_type=FULL
    )
    joined = jnp.stack(
        [grad_queries, share_back(grad_keys), share_back(grad_values)], axis=2
    )
    return joined.reshape(qkv.shape[0], -1).astype(LOW)


def total_parts(parts):
    total = parts[0]
    for part in parts[1:]:
        total = total + part
    return total


def block_forward(residual, pieces, parts, mix):
    normed_one, inverse_one = normalize(residual)
    hidden_one = (normed_one * (1.0 + pieces[1]) + pieces[0]).astype(LOW)
    qkv = [matmul(hidden_one, part[0]).astype(LOW) for part in parts]
    attended = [mix(rows) for rows in qkv]
    branch = total_parts([matmul(a, part[1]) for a, part in zip(attended, parts)])
    middle = residual + pieces[2] * branch
    normed_two, inverse_two = normalize(middle)
    hidden_two = (normed_two * (1.0 + pieces[4]) + pieces[3]).astype(LOW)
    pre = [matmul(hidden_two, part[2]) for part in parts]
    activated = [jax.nn.gelu(v, approximate=True).astype(LOW) for v in pre]
    mlp = total_parts([matmul(a, part[3]) for a, part in zip(activated, parts)])
    result = middle + pieces[5] * mlp
    saved = (
        normed_one,
        inverse_one,
        hidden_one,
        qkv,
        attended,
        branch,
        normed_two,
        inverse_two,
        hidden_two,
        pre,
        activated,
        mlp,
    )
    return result, saved


def block_backward(incoming, pieces, parts, saved, mix_back, weights, groups, flip):
    (
        normed_one,
        inverse_one,
        hidden_one,
        qkv,
        attended,
        branch,
        normed_two,
        inverse_two,
        hidden_two,
        pre,
        activated,
        mlp,
    ) = saved
    grad_mlp = (pieces[5] * incoming).astype(LOW)
    grad_pre = []
    for part, v in zip(parts, pre):
        _, back = jax.vjp(partial(jax.nn.gelu, approximate=True), v)
        grad_pre.append(back(matmul_nt(grad_mlp, part[3]))[0].astype(LOW))
    grad_up, grad_down = weights.reduce_mlp(hidden_two, grad_pre, activated, grad_mlp, flip)
    grad_hidden_two = total_parts([matmul_nt(g, part[2]) for g, part in zip(grad_pre, parts)])
    grad_middle = incoming + normalize_back(
        grad_hidden_two * (1.0 + pieces[4]), normed_two, inverse_two
    )
    grad_branch = (pieces[2] * grad_middle).astype(LOW)
    grad_out = weights.reduce_out(attended, grad_branch, flip)
    grad_attended = [matmul_nt(grad_branch, part[1]).astype(LOW) for part in parts]
    grad_qkv_rows = [mix_back(g, rows) for g, rows in zip(grad_attended, qkv)]
    grad_qkv = weights.reduce_qkv(hidden_one, grad_qkv_rows, flip)
    grad_hidden_one = total_parts(
        [matmul_nt(g, part[0]) for g, part in zip(grad_qkv_rows, parts)]
    )
    grad_residual = grad_middle + normalize_back(
        grad_hidden_one * (1.0 + pieces[1]), normed_one, inverse_one
    )
    sums = [
        jnp.sum(v.reshape(groups, -1, v.shape[-1]), axis=1)
        for v in (
            grad_hidden_one,
            grad_hidden_one * normed_one,
            grad_middle * branch,
            grad_hidden_two,
            grad_hidden_two * normed_two,
            incoming * mlp,
        )
    ]
    grad_mods = jnp.concatenate(sums, axis=-1)
    return grad_residual, grad_mods, (grad_qkv, grad_out, grad_up, grad_down)


def per_device(
    patch,
    seq,
    patch_axes,
    seq_axis,
    tokens,
    cotangent,
    class_ids,
    timesteps,
    segments,
    class_table,
    mod_spatial,
    qkv_spatial,
    out_spatial,
    up_spatial,
    down_spatial,
    mod_temporal,
    qkv_temporal,
    out_temporal,
    up_temporal,
    down_temporal,
):
    groups, frames, patch_rows, features = tokens.shape
    row_count = groups * frames * patch_rows
    head = features // HEADS
    hidden = up_spatial.shape[1] * seq
    grid = Grid(patch, seq, patch_axes, seq_axis)
    split = groups == 1 and Split.fits(patch, seq, frames, features, hidden)

    ways = max(1, patch // frames)
    subgroups = None
    if ways > 1:
        subgroups = [[a * ways + b for a in range(frames)] for b in range(ways)]

    def to_frames(array):
        moved = lax.all_to_all(
            array.reshape(groups, frames, patch_rows, features),
            patch_axes,
            split_axis=1,
            concat_axis=2,
            tiled=True,
            axis_index_groups=subgroups,
        )
        return moved.reshape(row_count, features)

    own_frames = max(1, frames // patch)

    def to_patches(array):
        moved = lax.all_to_all(
            array.reshape(groups, own_frames, -1, features),
            patch_axes,
            split_axis=2,
            concat_axis=1,
            tiled=True,
            axis_index_groups=subgroups,
        )
        return moved.reshape(row_count, features)

    def sharers(by):
        return [
            (a * ways + b, a * ways + (b + by) % ways)
            for a in range(patch // ways)
            for b in range(ways)
        ]

    def share_frame(array):
        if ways == 1:
            return array
        return jnp.concatenate(
            [array] + [lax.ppermute(array, patch_axes, sharers(j)) for j in range(1, ways)], axis=1
        )

    def share_frame_back(array):
        if ways == 1:
            return array
        cut = jnp.split(array, ways, axis=1)
        total = cut[0]
        for j in range(1, ways):
            total = total + lax.ppermute(cut[j], patch_axes, sharers(-j))
        return total

    whose = [jnp.stack([class_ids, timesteps])]
    whose += [grid.shift_x(whose[0], -j) for j in range(1, seq)]
    every_class = [w[0] for w in whose]
    conditions = []
    for chosen, times in whose:
        one_hot = (
            chosen[:, None] == jnp.arange(class_table.shape[0], dtype=jnp.int32)[None, :]
        ).astype(LOW)
        conditions.append(matmul(one_hot, class_table) + time_features(times, features))
    cond_low = [jax.nn.silu(c).astype(LOW) for c in conditions]
    mod_rows = features // patch
    first_row = grid.place * mod_rows
    cond_own = [lax.dynamic_slice_in_dim(c, first_row, mod_rows, axis=1) for c in cond_low]
    modulation = []

    def mod_steps(hold):
        together = jnp.concatenate(cond_own)
        mods = jnp.stack([matmul(together, mod_spatial), matmul(together, mod_temporal)], axis=1)
        for bit in grid.bits():
            mods = hold(mods + grid.xor_patch(mods, bit))
            yield
        mods = mods.reshape(seq, groups, 2, -1).transpose(0, 2, 1, 3)
        received = [mods[0]] + [grid.shift_x(mods[j], j) for j in range(1, seq)]
        ordered = in_order(received[:1] + received[:0:-1], grid.x)
        modulation.append(hold(jnp.concatenate(ordered, axis=-1)))
        yield

    width = mod_spatial.shape[1]

    def outer(columns):
        return lax.dot_general(
            jnp.concatenate(cond_own).astype(FULL),
            columns,
            (((0,), (0,)), ((), ())),
            precision=PRECISE,
            preferred_element_type=FULL,
        )

    def condition_part(columns, mod):
        return lax.dot_general(
            columns,
            mod.astype(FULL),
            (((1,), (1,)), ((), ())),
            precision=PRECISE,
            preferred_element_type=FULL,
        )

    def condition_steps(spatial_sums, temporal_sums, own_class):
        sums = jnp.stack([spatial_sums, temporal_sums])
        for bit in grid.bits():
            if split and bit == 1:
                continue
            sums = sums + (yield sums, partial(grid.xor_patch, bit=bit))
        sums = sums.reshape(2, groups, seq, width)
        columns = [pick(sums, 2, grid.x)]
        for j in range(1, seq):
            away = pick(sums, 2, (grid.x - j) % seq)
            columns.append((yield away, partial(grid.shift_x, by=-j)))
        columns = jnp.concatenate(columns, axis=1)
        parts = condition_part(columns[0], mod_spatial) + condition_part(columns[1], mod_temporal)
        parts = parts.reshape(seq, groups, mod_rows)
        total = parts
        for j in range(1, seq):
            total = total + jnp.roll((yield parts, partial(grid.shift_x, by=j)), j, axis=0)
        total = total[None]
        bit = 1
        while bit < patch:
            total = grid.join_patch(total, (yield total, partial(grid.xor_patch, bit=bit)), bit)
            bit *= 2
        grad_condition = total.transpose(1, 2, 0, 3).reshape(seq * groups, features)
        _, silu_back = jax.vjp(jax.nn.silu, jnp.concatenate(conditions))
        every_hot = (
            jnp.concatenate([own_class()] + every_class[1:])[:, None]
            == jnp.arange(class_table.shape[0], dtype=jnp.int32)[None, :]
        ).astype(FULL)
        grad_class_table = lax.dot_general(
            every_hot,
            silu_back(grad_condition)[0],
            (((0,), (0,)), ((), ())),
            precision=PRECISE,
            preferred_element_type=FULL,
        )
        yield grad_class_table, outer(columns[0]), outer(columns[1])

    def conditions_at_once(spatial_sums, temporal_sums):
        steps = condition_steps(spatial_sums, temporal_sums, lambda: class_ids)
        request = next(steps)
        while isinstance(request[1], partial):
            request = steps.send(request[1](request[0]))
        return request


    spatial_shards = (qkv_spatial, out_spatial, up_spatial, down_spatial)
    temporal_shards = (qkv_temporal, out_temporal, up_temporal, down_temporal)
    span = frames * patch_rows
    patch_of = jnp.arange(span, dtype=jnp.int32) % patch_rows
    place_of = jnp.repeat(segments, patch_rows, axis=1) * patch_rows + patch_of[None, :]

    if split:
        plan = Split(grid, head, hidden // patch, whose[0])
        hold = plan.tie
        marks = (place_of.reshape(-1, 1), place_of.reshape(1, -1))
        shards = plan.prepare(spatial_shards, temporal_shards)
        steps = mod_steps(hold)
        for _ in range(2):
            next(steps)

        def mods_of():
            return [
                jnp.pad(modulation[-1][block].reshape(6, features), ((0, 2), (0, 0)))
                for block in range(2)
            ]

        result, spatial_state, temporal_state = plan.forward(
            tokens,
            mods_of,
            steps,
            shards,
            down_spatial.shape,
            marks,
            to_frames,
            to_patches,
        )
        out_tokens = result.reshape(tokens.shape)
        grad_spatial_in, condition_grads, spatial_grads, temporal_grads = plan.backward(
            spatial_state,
            temporal_state,
            cotangent.reshape(row_count, features),
            to_frames,
            to_patches,
            lambda s, t: condition_steps(s, t, lambda: plan.token[0]),
        )
        grad_tokens = grad_spatial_in.astype(FULL).reshape(tokens.shape)
    else:
        weights = WholeWeights(grid, features, hidden)
        list(mod_steps(lambda v: v))

        def pieces_of(block):
            rows = modulation[-1][block]
            if groups > 1:
                rows = jnp.repeat(rows, row_count // groups, axis=0)
            return [rows[:, k * features : (k + 1) * features] for k in range(6)]

        spatial_pieces, temporal_pieces = pieces_of(0), pieces_of(1)
        spatial_parts, temporal_parts = weights.fetch(spatial_shards, temporal_shards)
        same = (place_of[:, :, None] == place_of[:, None, :])[:, None, :, :]
        itself = lambda array: array
        spatial_batch = groups * own_frames
        spatial_mix = lambda rows: attend(rows, spatial_batch, None, head, share_frame)
        spatial_mix_back = lambda g, rows: attend_back(
            g, rows, spatial_batch, None, head, share_frame, share_frame_back
        )
        temporal_mix = lambda rows: attend(rows, groups, same, head, itself)
        temporal_mix_back = lambda g, rows: attend_back(
            g, rows, groups, same, head, itself, itself
        )
        spatial_in = to_frames(tokens).astype(FULL)
        spatial_out, spatial_saved = block_forward(
            spatial_in, spatial_pieces, spatial_parts, spatial_mix
        )
        temporal_in = to_patches(spatial_out.astype(LOW)).astype(FULL)
        result, temporal_saved = block_forward(
            temporal_in, temporal_pieces, temporal_parts, temporal_mix
        )
        out_tokens = result.astype(LOW).reshape(tokens.shape)
        incoming = cotangent.astype(FULL).reshape(row_count, features)
        grad_temporal_in, temporal_sums, temporal_grads = block_backward(
            incoming,
            temporal_pieces,
            temporal_parts,
            temporal_saved,
            temporal_mix_back,
            weights,
            groups,
            True,
        )
        grad_spatial_out = to_frames(grad_temporal_in.astype(LOW)).astype(FULL)
        grad_spatial_in, spatial_sums, spatial_grads = block_backward(
            grad_spatial_out,
            spatial_pieces,
            spatial_parts,
            spatial_saved,
            spatial_mix_back,
            weights,
            groups,
            False,
        )
        grad_tokens = to_patches(grad_spatial_in.astype(LOW)).astype(FULL).reshape(tokens.shape)
        condition_grads = conditions_at_once(spatial_sums, temporal_sums)

    grad_class_table, grad_mod_spatial, grad_mod_temporal = condition_grads

    return (
        out_tokens,
        grad_tokens,
        grad_class_table,
        grad_mod_spatial,
        *spatial_grads,
        grad_mod_temporal,
        *temporal_grads,
    )


def solution(mesh):
    patch, seq = mesh.shape["patch"], mesh.shape["seq"]
    patch_axes, seq_axis = "patch", "seq"
    if seq == 2 and patch % 4 == 0:
        patch_axes, seq_axis = ("z", "y", "core"), "x"
        mesh = Mesh(mesh.devices.reshape(patch // 4, 2, 2, seq), patch_axes + (seq_axis,))
    rows = P(seq_axis, None, patch_axes, None)
    both = P(patch_axes, seq_axis)
    return jax.shard_map(
        partial(per_device, patch, seq, patch_axes, seq_axis),
        mesh=mesh,
        in_specs=(rows, rows, P(seq_axis), P(seq_axis), P(seq_axis, None), P()) + (both,) * 10,
        out_specs=(rows, rows, P()) + (both,) * 10,
        check_vma=False,
    )
```

time: 1020 us -> 909 us (0.89)
  waiting for transfers between devices: 457 us -> 314 us
  blocking collectives: 0 us -> 45.6 us
  starting transfers between devices: 149 us -> 125 us
  other arithmetic: 27.7 us -> 38.6 us
    ppermute x71 -> x67, waiting for transfers between devices: 376 us -> 229 us  [send(): return lax.ppermute(array, self.every, self.moves(step))]
    all_gather x1, waiting for transfers between devices: 7.63 us -> 54.5 us  [forward(): held_t = lax.all_gather(self.tie(packed), grid.chips[0], axis=0)]
    all_to_all x0 -> x1, blocking collectives: none -> 45.6 us  [to_patches(): lax.all_to_all(array.reshape(groups, own_frames, -1, features), patch_axe...]
    ppermute x71 -> x67, starting transfers between devices: 101 us -> 69.7 us  [send(): return lax.ppermute(array, self.every, self.moves(step))]
    all_to_all x2 -> x1, waiting for transfers between devices: 24 us -> 0.01 us  [to_patches(): lax.all_to_all(array.reshape(groups, own_frames, -1, features), patch_axe...]
    all_to_all x2, waiting for transfers between devices: 20.8 us -> 7 us  [to_frames(): lax.all_to_all(array.reshape(groups, frames, patch_rows, features), patch...]
    another operation x15 -> x14, other arithmetic: 8.03 us -> 18.8 us  [the longest x8 17.1 us: second(): self.held = self.plan.tie(jnp.stack([self.held, self.flight.value]))]
    unnamed x98 -> x100, local copies, waits for them, and re-layouts: 28.6 us -> 21.5 us
  transfers between devices with their start and end apart: 90 -> 87, of which waited for: 34 -> 30; matrix products, arithmetic and copies ran while one was open for 5% -> 7% of each run, Pallas kernels for 26% -> 31%
where the time goes in v2:
time: 909 us; the launch traced here: 903 us
  Pallas kernels  315 us (35%)
  waiting for transfers between devices  314 us (35%)
  starting transfers between devices  125 us (14%)
  blocking collectives  45.6 us (5%)
  other arithmetic  38.6 us (4%)
  local copies, waits for them, and re-layouts  37.3 us (4%)
  between operations  17.4 us (2%)
  matrix products  9.67 us (1%)
    ppermute x67, waiting for transfers between devices, send(): return lax.ppermute(array, self.every, self.moves(step))  229 us
    pallas_call x30, Pallas kernels, call(): pl.pallas_call(kernel, out_shape=outs, in_specs=[pl.BlockSpec(memory_spac...  208 us
    ppermute x67, starting transfers between devices, send(): return lax.ppermute(array, self.every, self.moves(step))  69.7 us
    pallas_call x12, Pallas kernels, add_all(): pl.pallas_call(kernel, out_shape=shape((depth, rows, cols), LOW), grid_sp...  55.4 us
    all_gather x1, waiting for transfers between devices, forward(): held_t = lax.all_gather(self.tie(packed), grid.chips[0], axis=0)  54.5 us
    pallas_call x6, Pallas kernels, weight_grad(): pl.pallas_call(kernel, out_shape=[shape((depth, rows, w), LOW) for w in w...  52.1 us
    all_to_all x1, blocking collectives, to_patches(): lax.all_to_all(array.reshape(groups, own_frames, -1, features), patch_axe...  45.6 us
    ppermute x11, starting transfers between devices, xor_patch(): return lax.ppermute(array, self.every, pairs)  29.2 us
  transfers between devices with their start and end apart: 87, of which 30 were waited for; matrix products, arithmetic and copies ran while one was open for 7% of the time, Pallas kernels for 31%

profile of v2, /device:TPU:0, one launch (start us, length us, event | category | flops | bytes accessed | tf_op | source)
XLA Modules:
  0.0 902.7 jit_solution(10581434450446335480)
XLA Ops:
  52.9 16.3 %collective-permute-done.6 = bf16[144,1152]{1,0:T(8,128)(2,1)S(1)} collective-permute-done((bf16[144,1152]{1,0:T(8,128)(2,1)S(1)}, bf16[144,1152]{1,0:T(8,128)(2,1)S(1)}, u32[]{:S(2)}, u32[]{:S(2)}) %collective-permute-start.6) | collective-permute-done | bytes 331808 | tf_op jit(solution)/shard_map/ppermute | solution.py:799
  69.2 16.3 %collective-permute-done.5 = bf16[144,1152]{1,0:T(8,128)(2,1)S(1)} collective-permute-done((bf16[144,1152]{1,0:T(8,128)(2,1)S(1)}, bf16[144,1152]{1,0:T(8,128)(2,1)S(1)}, u32[]{:S(2)}, u32[]{:S(2)}) %collective-permute-start.5) | collective-permute-done | bytes 331808 | tf_op jit(solution)/shard_map/ppermute | solution.py:799
  87.9 15.6 %collective-permute-done.13 = bf16[4,144,640]{2,1,0:T(8,128)(2,1)S(1)} collective-permute-done((bf16[4,144,640]{2,1,0:T(8,128)(2,1)S(1)}, bf16[4,144,640]{2,1,0:T(8,128)(2,1)S(1)}, u32[]{:S(2)}, u32[]{:S(2)}) %collective-permute-start.13) | collective-permute-done | bytes 737312 | tf_op jit(solution)/shard_map/ppermute | solution.py:799
  117.2 15.0 %collective-permute-done.16.refs_6_.refs_4_ = bf16[2,4,144,512]{3,2,1,0:T(8,128)(2,1)S(1)} collective-permute-done((bf16[2,4,144,512]{3,2,1,0:T(8,128)(2,1)S(1)}, bf16[2,4,144,512]{3,2,1,0:T(8,128)(2,1)S(1)}, u32[]{:S(2)}, u32[]{:S(2)}) %collective-permute-start.16) | collective-permute-done | bytes 1179680 | tf_op jit(solution)/shard_map/ppermute | solution.py:799
  136.2 23.6 %collective-permute-done.11 = bf16[144,2432]{1,0:T(8,128)(2,1)S(1)} collective-permute-done((bf16[144,2432]{1,0:T(8,128)(2,1)S(1)}, bf16[144,2432]{1,0:T(8,128)(2,1)S(1)}, u32[]{:S(2)}, u32[]{:S(2)}) %collective-permute-start.11) | collective-permute-done | bytes 700448 | tf_op jit(solution)/shard_map/ppermute | solution.py:799
  174.8 10.1 %attend_out.2 = (bf16[1,512,576]{2,1,0:T(8,128)(2,1)}, bf16[512,1152]{1,0:T(8,128)(2,1)}) custom-call(s32[4]{0:T(128)} %pad_add_fusion.1.where_ref.where, bf16[2,512,864]{2,1,0:T(8,128)(2,1)} %get-tuple-element.531.refs_0_.refs_9_, bf16[2,576,576]{2,1,0:T(8,128)(2,1)} %get-tuple-element.532.refs_1_.refs_8_), custom_call_target="tpu_custom_call" | custom-call | flops 1 | bytes 1 | tf_op jit(solution)/shard_map/attend_out/pallas_call | solution.py:145
  200.3 54.5 %all-gather.3.cloned.1.call-done = bf16[576,3584]{1,0:T(8,128)(2,1)} async-done(((bf16[144,3584]{1,0:T(8,128)(2,1)}), bf16[576,3584]{1,0:T(8,128)(2,1)}) %all-gather.3.cloned.1.call-update) | async-done | bytes 4128784 | tf_op jit(solution)/shard_map/all_gather | solution.py:977
  263.8 10.7 %norm_up.2 = (f32[512,1152]{1,0:T(8,128)}, f32[512,1152]{1,0:T(8,128)}, bf16[1,512,1152]{2,1,0:T(8,128)(2,1)}, bf16[2,512,1152]{2,1,0:T(8,128)(2,1)}, bf16[2,512,1152]{2,1,0:T(8,128)(2,1)}) custom-call(s32[4]{0:T(128)} %pad_add_fusion.1.where_ref.where, bf16[512,1152]{1,0:T(8,128)(2,1)} %get-tuple-element.563.refs_0_, ...), custom_call_target="tpu_custom_call" | custom-call | flops 1 | bytes 1 | tf_op jit(solution)/shard_map/norm_up/pallas_call | solution.py:145
  274.6 9.3 %down_part.2.refs_0_ = bf16[512,1152]{1,0:T(8,128)(2,1)} custom-call(s32[4]{0:T(128)} %pad_add_fusion.1.where_ref.where, bf16[2,512,1152]{2,1,0:T(8,128)(2,1)} %get-tuple-element.711.refs_0_, bf16[2,4,144,1280]{3,2,1,0:T(8,128)(2,1)} %copy-done.1, bf16[2,4,144,1280]{3,2,1,0:T(8,128)(2,1)} %collective-permute-done.21.refs_2_.refs_7_), custom_call_target="tpu_custom_call" | custom-call | flops 1 | bytes 1 | tf_op jit(solution)/shard_map/down_part/pallas_call | solution.py:145
  305.9 11.4 %collective-permute-done.27 = bf16[4,144,640]{2,1,0:T(8,128)(2,1)} collective-permute-done((bf16[4,144,640]{2,1,0:T(8,128)(2,1)}, bf16[4,144,640]{2,1,0:T(8,128)(2,1)}, u32[]{:S(2)}, u32[]{:S(2)}) %collective-permute-start.27) | collective-permute-done | bytes 737312 | tf_op jit(solution)/shard_map/ppermute | solution.py:799
  334.0 45.6 %all_to_all.16 = bf16[16,2,9216]{2,1,0:T(2,128)(2,1)} all-to-all(bf16[16,2,9216]{2,1,0:T(2,128)(2,1)} %reshape.682), channel_id=1, replica_groups=mesh['z'=4,'y'=2,'core'=2,'x'=2] {'z','y','core'}, dimensions={0} | all-to-all | bytes 1179648 | tf_op jit(solution)/shard_map/all_to_all | solution.py:1495
  397.2 10.0 %attend_out.3 = (bf16[1,512,576]{2,1,0:T(8,128)(2,1)}, bf16[512,1152]{1,0:T(8,128)(2,1)}) custom-call(s32[4]{0:T(128)} %pad_add_fusion.1.where_ref.where, bf16[2,512,864]{2,1,0:T(8,128)(2,1)} %get-tuple-element.630.refs_0_.refs_9_, bf16[2,576,576]{2,1,0:T(8,128)(2,1)} %get-tuple-element.631.refs_1_.refs_8_, s32[256,1]{1,0:T(8,128)} %fusion.refs_2_.refs_10_, ...), custom_call_target="tpu_custom_call" | custom-call | flops 1 | bytes 1 | tf_op jit(solution)/shard_map/attend_out/pallas_call | solution.py:145
  411.3 11.1 %norm_up.3 = (f32[512,1152]{1,0:T(8,128)}, f32[512,1152]{1,0:T(8,128)}, bf16[1,512,1152]{2,1,0:T(8,128)(2,1)}, bf16[2,512,1152]{2,1,0:T(8,128)(2,1)}, bf16[2,512,1152]{2,1,0:T(8,128)(2,1)}) custom-call(s32[4]{0:T(128)} %pad_add_fusion.1.where_ref.where, bf16[512,1152]{1,0:T(8,128)(2,1)} %get-tuple-element.640.refs_0_, bf16[512,1152]{1,0:T(8,128)(2,1)} %copy-done.26, ...), custom_call_target="tpu_custom_call" | custom-call | flops 1 | bytes 1 | tf_op jit(solution)/shard_map/norm_up/pallas_call | solution.py:145
  422.4 9.3 %down_part.3.refs_0_ = bf16[512,1152]{1,0:T(8,128)(2,1)} custom-call(s32[4]{0:T(128)} %pad_add_fusion.1.where_ref.where, bf16[2,512,1152]{2,1,0:T(8,128)(2,1)} %get-tuple-element.655.refs_0_, bf16[2,4,144,640]{3,2,1,0:T(8,128)(2,1)} %pad_maximum_fusion.6.refs_1_.refs_6_, bf16[2,4,144,640]{3,2,1,0:T(8,128)(2,1)} %collective-permute-done.32.refs_2_.refs_7_, ...), custom_call_target="tpu_custom_call" | custom-call | flops 1 | bytes 1 | tf_op jit(solution)/shard_map/down_part/pallas_call | solution.py:145
  441.3 17.8 %mlp_back.2 = (bf16[2,512,576]{2,1,0:T(8,128)(2,1)}, bf16[2,512,1152]{2,1,0:T(8,128)(2,1)}, bf16[512,1152]{1,0:T(8,128)(2,1)}) custom-call(s32[4]{0:T(128)} %pad_add_fusion.1.where_ref.where, bf16[256,1152]{1,0:T(8,128)(2,1)} %bitcast.177, bf16[256,1152]{1,0:T(8,128)(2,1)} %copy-done.16, f32[8,1152]{1,0:T(8,128)} %pad.8.refs_2_.refs_4_.refs_3_, ...), custom_call_target="tpu_custom_call" | custom-call | flops 1 | bytes 1 | tf_op jit(solution)/shard_map/mlp_back/pallas_call | solution.py:145
  459.3 8.8 weight_grad.6
  479.1 16.1 %attend_grad.2 = (f32[512,1152]{1,0:T(8,128)}, bf16[2,512,576]{2,1,0:T(8,128)(2,1)}, f32[8,1152]{1,0:T(8,128)}, bf16[2,512,864]{2,1,0:T(8,128)(2,1)}) custom-call(s32[4]{0:T(128)} %pad_add_fusion.1.where_ref.where, bf16[512,1152]{1,0:T(8,128)(2,1)} %get-tuple-element.680.refs_0_, bf16[512,1152]{1,0:T(8,128)(2,1)} %copy-done.24, bf16[256,1152]{1,0:T(8,128)(2,1)} %bitcast.178, ...), custom_call_target="tpu_custom_call" | custom-call | flops 1 | bytes 1 | tf_op jit(solution)/shard_map/attend_grad/pallas_call | solution.py:145
  505.6 9.3 %weight_grad.8 = (bf16[4,144,1152]{2,1,0:T(8,128)(2,1)}, bf16[4,144,1152]{2,1,0:T(8,128)(2,1)}, bf16[4,144,1152]{2,1,0:T(8,128)(2,1)}, bf16[4,144,1152]{2,1,0:T(8,128)(2,1)}) custom-call(s32[4]{0:T(128)} %pad_add_fusion.1.where_ref.where, bf16[1,512,1152]{2,1,0:T(8,128)(2,1)} %get-tuple-element.691.refs_0_, ...), custom_call_target="tpu_custom_call" | custom-call | flops 1 | bytes 1 | tf_op jit(solution)/shard_map/weight_grad/pallas_call | solution.py:583
  520.6 16.1 %all-to-all-start.2 = ((bf16[1,16,16,1152]{3,2,0,1:T(8,128)(2,1)}), bf16[1,16,16,1152]{3,2,0,1:T(8,128)(2,1)S(1)}, u32[]{:S(2)}, u32[]{:S(2)}) async-start(bf16[1,16,16,1152]{3,2,0,1:T(8,128)(2,1)} %bitcast.185), calls=%async_computation.2 | async-start | bytes 1179648 | tf_op jit(solution)/shard_map/all_to_all | solution.py:1482
  558.0 11.0 %collective-permute-done.42.refs_1_ = bf16[4,144,1152]{2,1,0:T(8,128)(2,1)} collective-permute-done((bf16[4,144,1152]{2,1,0:T(8,128)(2,1)}, bf16[4,144,1152]{2,1,0:T(8,128)(2,1)}, u32[]{:S(2)}, u32[]{:S(2)}) %collective-permute-start.42) | collective-permute-done | bytes 1327136 | tf_op jit(solution)/shard_map/ppermute | solution.py:799
  569.8 17.6 %mlp_back.3 = (bf16[2,512,576]{2,1,0:T(8,128)(2,1)}, bf16[2,512,1152]{2,1,0:T(8,128)(2,1)}, bf16[512,1152]{1,0:T(8,128)(2,1)}) custom-call(s32[4]{0:T(128)} %pad_add_fusion.1.where_ref.where, bf16[256,1152]{1,0:T(8,128)(2,1)} %bitcast.167, bf16[256,1152]{1,0:T(8,128)(2,1)} %copy-done.15, f32[8,1152]{1,0:T(8,128)} %pad.7.refs_2_.refs_4_.refs_3_, ...), custom_call_target="tpu_custom_call" | custom-call | flops 1 | bytes 1 | tf_op jit(solution)/shard_map/mlp_back/pallas_call | solution.py:145
  595.3 8.9 weight_grad.10
  612.5 16.5 %collective-permute-done.45.refs_2_ = bf16[4,288,576]{2,1,0:T(8,128)(2,1)} collective-permute-done((bf16[4,288,576]{2,1,0:T(8,128)(2,1)}, bf16[4,288,576]{2,1,0:T(8,128)(2,1)}, u32[]{:S(2)}, u32[]{:S(2)}) %collective-permute-start.45) | collective-permute-done | bytes 1327136 | tf_op jit(solution)/shard_map/ppermute | solution.py:799
  630.2 16.1 %attend_grad.3 = (f32[512,1152]{1,0:T(8,128)}, bf16[2,512,576]{2,1,0:T(8,128)(2,1)}, f32[8,1152]{1,0:T(8,128)}, bf16[2,512,864]{2,1,0:T(8,128)(2,1)}) custom-call(s32[4]{0:T(128)} %pad_add_fusion.1.where_ref.where, bf16[512,1152]{1,0:T(8,128)(2,1)} %get-tuple-element.707.refs_0_, bf16[512,1152]{1,0:T(8,128)(2,1)} %collective-permute-done.44.refs_1_, ...), custom_call_target="tpu_custom_call" | custom-call | flops 1 | bytes 1 | tf_op jit(solution)/shard_map/attend_grad/pallas_call | solution.py:145
  652.9 9.4 %weight_grad.11 = (bf16[4,144,640]{2,1,0:T(8,128)(2,1)}, bf16[4,144,640]{2,1,0:T(8,128)(2,1)}, bf16[4,144,640]{2,1,0:T(8,128)(2,1)}, bf16[4,144,640]{2,1,0:T(8,1...) custom-call(s32[4]{0:T(128)} %pad_add_fusion.1.where_ref.where, ...), custom_call_target="tpu_custom_call" | custom-call | flops 1 | bytes 1 | tf_op jit(solution)/shard_map/weight_grad/pallas_call | solution.py:583
  662.3 8.3 qkv_part.3.refs_0_
  678.2 14.0 %collective-permute-done.49.refs_1_ = bf16[4,288,576]{2,1,0:T(8,128)(2,1)S(1)} collective-permute-done((bf16[4,288,576]{2,1,0:T(8,128)(2,1)}, bf16[4,288,576]{2,1,0:T(8,128)(2,1)S(1)}, u32[]{:S(2)}, u32[]{:S(2)}) %collective-permute-start.49) | collective-permute-done | bytes 1327136 | tf_op jit(solution)/shard_map/ppermute | solution.py:799
  727.2 33.8 %collective-permute-done.53.refs_3_ = bf16[4,144,512]{2,1,0:T(8,128)(2,1)} collective-permute-done((bf16[4,144,512]{2,1,0:T(8,128)(2,1)}, bf16[4,144,512]{2,1,0:T(8,128)(2,1)}, u32[]{:S(2)}, u32[]{:S(2)}) %collective-permute-start.53) | collective-permute-done | bytes 589856 | tf_op jit(solution)/shard_map/ppermute | solution.py:799
  769.6 9.2 %collective-permute-start.51 = (f32[2,1,6912]{2,1,0:T(1,128)S(1)}, f32[2,1,6912]{2,1,0:T(1,128)S(1)}, u32[]{:S(2)}, u32[]{:S(2)}) collective-permute-start(f32[2,1,6912]{2,1,0:T(1,128)S(1)} %constant_dynamic-update-slice_fusion), channel_id=1, source_target_pairs={{0,16},{1,17},{2,18},{3,19},{4,20},{5,21},{6,22},{7,23},{8,24},{9,... | collective-permute-start | bytes 165896 | tf_op jit(solution)/shard_map/ppermute | solution.py:819
  789.0 9.1 %collective-permute-start.63 = (f32[2,1,6912]{2,1,0:T(1,128)S(1)}, f32[2,1,6912]{2,1,0:T(1,128)S(1)}, u32[]{:S(2)}, u32[]{:S(2)}) collective-permute-start(f32[2,1,6912]{2,1,0:T(1,128)S(1)} %add.159), channel_id=1, source_target_pairs={{0,8},{1,9},{2,10},{3,11},{4,12},{5,13},{6,14},{7,15},{8,0},{9,1},... | collective-permute-start | bytes 165896 | tf_op jit(solution)/shard_map/ppermute | solution.py:819
  843.3 22.6 %collective-permute-done.71.refs_2_ = bf16[144,1152]{1,0:T(8,128)(2,1)S(1)} collective-permute-done((bf16[144,1152]{1,0:T(8,128)(2,1)}, bf16[144,1152]{1,0:T(8,128)(2,1)S(1)}, u32[]{:S(2)}, u32[]{:S(2)}) %collective-permute-start.71) | collective-permute-done | bytes 331808 | tf_op jit(solution)/shard_map/ppermute | solution.py:799
  873.6 10.1 %collective-permute-done.77 = f32[8,2,1,72]{3,1,0,2:T(2,128)S(1)} collective-permute-done((f32[8,2,1,72]{3,1,0,2:T(2,128)S(1)}, f32[8,2,1,72]{3,1,0,2:T(2,128)S(1)}, u32[]{:S(2)}, u32[]{:S(2)}) %collective-permute-start.77) | collective-permute-done | bytes 4640 | tf_op jit(solution)/shard_map/ppermute | solution.py:819
  (401 shorter events, 371.9 us)
Async XLA Ops:
  43.0 44.9 %all-to-all-start = ((bf16[1,16,16,1152]{3,2,0,1:T(8,128)(2,1)}), bf16[1,16,16,1152]{3,2,0,1:T(8,128)(2,1)S(1)}, u32[]{:S(2)}, u32[]{:S(2)}) async-start(bf16[1,16,16,1152]{3,2,0,1:T(8,128)(2,1)} %bitcast.16), calls=%async_computation | async-start | bytes 1179648 | tf_op jit(solution)/shard_map/all_to_all | solution.py:1482
  46.9 207.9 %all-gather.3.cloned.1.call-start = ((), (), s32[]{:S(2)}) async-start(), calls=%async_computation.14 | async-start | bytes 5160960 | tf_op jit(solution)/shard_map/all_gather | solution.py:977
  114.6 45.1 %collective-permute-start.11 = (bf16[144,2432]{1,0:T(8,128)(2,1)S(1)}, bf16[144,2432]{1,0:T(8,128)(2,1)S(1)}, u32[]{:S(2)}, u32[]{:S(2)}) collective-permute-start(bf16[144,2432]{1,0:T(8,128)(2,1)S(1)} %copy-done.29), channel_id=1, source_target_pairs={{0,16},{1,17},{2,18},{3,19},{4,20},{5,21},{6,22},{7,23},{8,24},{9,... | collective-permute-start | bytes 2101256 | tf_op jit(solution)/shard_map/ppermute | solution.py:799
  116.1 43.7 %collective-permute-start.10 = (bf16[144,2432]{1,0:T(8,128)(2,1)S(1)}, bf16[144,2432]{1,0:T(8,128)(2,1)S(1)}, u32[]{:S(2)}, u32[]{:S(2)}) collective-permute-start(bf16[144,2432]{1,0:T(8,128)(2,1)S(1)} %copy-done.29), channel_id=1, source_target_pairs={{0,24},{1,25},{2,26},{3,27},{4,28},{5,29},{6,30},{7,31},{8,0},{9,1... | collective-permute-start | bytes 2101256 | tf_op jit(solution)/shard_map/ppermute | solution.py:799
  198.7 65.1 %collective-permute-start.21 = (bf16[2,4,144,1280]{3,2,1,0:T(8,128)(2,1)S(1)}, bf16[2,4,144,1280]{3,2,1,0:T(8,128)(2,1)}, u32[]{:S(2)}, u32[]{:S(2)}) collective-permute-start(bf16[2,4,144,1280]{3,2,1,0:T(8,128)(2,1)S(1)} %pad_maximum_fusion.refs_1_.refs_6_), channel_id=1, source_target_pairs={{0,1},{1,0},{2,3},{3,2},{4,5},{5,4},{6,7},{7,6},{8,9},{9,8},{10,11... | collective-permute-start | bytes 8847368 | tf_op jit(solution)/shard_map/ppermute | solution.py:799
  199.4 64.4 %collective-permute-start.19 = (bf16[2,4,144,1152]{3,2,1,0:T(8,128)(2,1)}, bf16[2,4,144,1152]{3,2,1,0:T(8,128)(2,1)}, u32[]{:S(2)}, u32[]{:S(2)}) collective-permute-start(bf16[2,4,144,1152]{3,2,1,0:T(8,128)(2,1)} %pad_maximum_fusion.1.refs_5_.refs_4_), channel_id=1, source_target_pairs={{0,4},{1,5},{2,6},{3,7},{4,0},{5,1},{6,2},{7,3},{8,12},{9,13},{10,... | collective-permute-start | bytes 7962632 | tf_op jit(solution)/shard_map/ppermute | solution.py:799
  300.5 88.9 %collective-permute-start.29 = (bf16[2,4,144,1152]{3,2,1,0:T(8,128)(2,1)S(1)}, bf16[2,4,144,1152]{3,2,1,0:T(8,128)(2,1)}, u32[]{:S(2)}, u32[]{:S(2)}) collective-permute-start(bf16[2,4,144,1152]{3,2,1,0:T(8,128)(2,1)S(1)} %pad_maximum_fusion.3.refs_5_.refs_4_), channel_id=1, source_target_pairs={{0,1},{1,0},{2,3},{3,2},{4,5},{5,4},{6,7},{7,6},{8,9},{9,8},{10,11... | collective-permute-start | bytes 7962632 | tf_op jit(solution)/shard_map/ppermute | solution.py:799
  301.1 88.4 %collective-permute-start.28 = (bf16[2,4,144,1152]{3,2,1,0:T(8,128)(2,1)}, bf16[2,4,144,1152]{3,2,1,0:T(8,128)(2,1)}, u32[]{:S(2)}, u32[]{:S(2)}) collective-permute-start(bf16[2,4,144,1152]{3,2,1,0:T(8,128)(2,1)} %pad_maximum_fusion.2.refs_3_.refs_1_), channel_id=1, source_target_pairs={{0,4},{1,5},{2,6},{3,7},{4,0},{5,1},{6,2},{7,3},{8,12},{9,13},{10,... | collective-permute-start | bytes 7962632 | tf_op jit(solution)/shard_map/ppermute | solution.py:799
  468.1 46.9 %collective-permute-start.39 = (bf16[4,288,576]{2,1,0:T(8,128)(2,1)}, bf16[4,288,576]{2,1,0:T(8,128)(2,1)S(1)}, u32[]{:S(2)}, u32[]{:S(2)}) collective-permute-start(bf16[4,288,576]{2,1,0:T(8,128)(2,1)} %get-tuple-element.689), channel_id=1, source_target_pairs={{0,4},{1,5},{2,6},{3,7},{4,0},{5,1},{6,2},{7,3},{8,12},{9,13},{10,... | collective-permute-start | bytes 3981320 | tf_op jit(solution)/shard_map/ppermute | solution.py:799
  476.7 38.3 %collective-permute-start.38 = (bf16[4,144,1152]{2,1,0:T(8,128)(2,1)}, bf16[4,144,1152]{2,1,0:T(8,128)(2,1)}, u32[]{:S(2)}, u32[]{:S(2)}) collective-permute-start(bf16[4,144,1152]{2,1,0:T(8,128)(2,1)} %get-tuple-element.688), channel_id=1, source_target_pairs={{0,1},{1,0},{2,3},{3,2},{4,5},{5,4},{6,7},{7,6},{8,9},{9,8},{10,11... | collective-permute-start | bytes 3981320 | tf_op jit(solution)/shard_map/ppermute | solution.py:799
  504.4 40.9 %collective-permute-start.36 = (bf16[4,288,576]{2,1,0:T(8,128)(2,1)}, bf16[4,288,576]{2,1,0:T(8,128)(2,1)S(1)}, u32[]{:S(2)}, u32[]{:S(2)}) collective-permute-start(bf16[4,288,576]{2,1,0:T(8,128)(2,1)} %get-tuple-element.676), channel_id=1, source_target_pairs={{0,4},{1,5},{2,6},{3,7},{4,0},{5,1},{6,2},{7,3},{8,12},{9,13},{10,... | collective-permute-start | bytes 3981320 | tf_op jit(solution)/shard_map/ppermute | solution.py:799
  536.7 275.7 %reduce-scatter.6.cloned.1.call-start = ((), (), s32[]{:S(2)}) async-start(), calls=%async_computation.9 | async-start | bytes 1658880 | tf_op jit(solution)/shard_map/reduce_scatter | solution.py:935
  537.9 66.3 %collective-permute-start.46 = (bf16[4,144,1152]{2,1,0:T(8,128)(2,1)}, bf16[4,144,1152]{2,1,0:T(8,128)(2,1)}, u32[]{:S(2)}, u32[]{:S(2)}) collective-permute-start(bf16[4,144,1152]{2,1,0:T(8,128)(2,1)} %get-tuple-element.716), channel_id=1, source_target_pairs={{0,1},{1,0},{2,3},{3,2},{4,5},{5,4},{6,7},{7,6},{8,9},{9,8},{10,11... | collective-permute-start | bytes 3981320 | tf_op jit(solution)/shard_map/ppermute | solution.py:799
  543.3 60.9 %collective-permute-start.47 = (bf16[4,144,1152]{2,1,0:T(8,128)(2,1)}, bf16[4,144,1152]{2,1,0:T(8,128)(2,1)}, u32[]{:S(2)}, u32[]{:S(2)}) collective-permute-start(bf16[4,144,1152]{2,1,0:T(8,128)(2,1)} %add_all.12), channel_id=1, source_target_pairs={{0,4},{1,5},{2,6},{3,7},{4,0},{5,1},{6,2},{7,3},{8,12},{9,13},{10,... | collective-permute-start | bytes 3981320 | tf_op jit(solution)/shard_map/ppermute | solution.py:799
  556.9 72.2 %collective-permute-start.45 = (bf16[4,288,576]{2,1,0:T(8,128)(2,1)}, bf16[4,288,576]{2,1,0:T(8,128)(2,1)}, u32[]{:S(2)}, u32[]{:S(2)}) collective-permute-start(bf16[4,288,576]{2,1,0:T(8,128)(2,1)} %add_all.13), channel_id=1, source_target_pairs={{0,1},{1,0},{2,3},{3,2},{4,5},{5,4},{6,7},{7,6},{8,9},{9,8},{10,11... | collective-permute-start | bytes 3981320 | tf_op jit(solution)/shard_map/ppermute | solution.py:799
  609.0 212.0 %reduce-scatter.8.cloned.1.call-start = ((), (), s32[]{:S(2)}) async-start(), calls=%async_computation.10 | async-start | bytes 1658880 | tf_op jit(solution)/shard_map/reduce_scatter | solution.py:935
  609.2 61.4 %collective-permute-start.48 = (bf16[4,144,1152]{2,1,0:T(8,128)(2,1)}, bf16[4,144,1152]{2,1,0:T(8,128)(2,1)}, u32[]{:S(2)}, u32[]{:S(2)}) collective-permute-start(bf16[4,144,1152]{2,1,0:T(8,128)(2,1)} %get-tuple-element.727), channel_id=1, source_target_pairs={{0,4},{1,5},{2,6},{3,7},{4,0},{5,1},{6,2},{7,3},{8,12},{9,13},{10,... | collective-permute-start | bytes 3981320 | tf_op jit(solution)/shard_map/ppermute | solution.py:799
  611.3 59.5 %collective-permute-start.54 = (bf16[4,144,1152]{2,1,0:T(8,128)(2,1)}, bf16[4,144,1152]{2,1,0:T(8,128)(2,1)}, u32[]{:S(2)}, u32[]{:S(2)}) collective-permute-start(bf16[4,144,1152]{2,1,0:T(8,128)(2,1)} %get-tuple-element.747), channel_id=1, source_target_pairs={{0,4},{1,5},{2,6},{3,7},{4,0},{5,1},{6,2},{7,3},{8,12},{9,13},{10,... | collective-permute-start | bytes 3981320 | tf_op jit(solution)/shard_map/ppermute | solution.py:799
  611.4 60.3 %collective-permute-start.55 = (bf16[4,288,576]{2,1,0:T(8,128)(2,1)}, bf16[4,288,576]{2,1,0:T(8,128)(2,1)S(1)}, u32[]{:S(2)}, u32[]{:S(2)}) collective-permute-start(bf16[4,288,576]{2,1,0:T(8,128)(2,1)} %get-tuple-element.748), channel_id=1, source_target_pairs={{0,1},{1,0},{2,3},{3,2},{4,5},{5,4},{6,7},{7,6},{8,9},{9,8},{10,11... | collective-permute-start | bytes 3981320 | tf_op jit(solution)/shard_map/ppermute | solution.py:799
  629.1 63.1 %collective-permute-start.49 = (bf16[4,288,576]{2,1,0:T(8,128)(2,1)}, bf16[4,288,576]{2,1,0:T(8,128)(2,1)S(1)}, u32[]{:S(2)}, u32[]{:S(2)}) collective-permute-start(bf16[4,288,576]{2,1,0:T(8,128)(2,1)} %get-tuple-element.728), channel_id=1, source_target_pairs={{0,1},{1,0},{2,3},{3,2},{4,5},{5,4},{6,7},{7,6},{8,9},{9,8},{10,11... | collective-permute-start | bytes 3981320 | tf_op jit(solution)/shard_map/ppermute | solution.py:799
  651.0 58.4 %collective-permute-start.60 = (bf16[4,144,1152]{2,1,0:T(8,128)(2,1)}, bf16[4,144,1152]{2,1,0:T(8,128)(2,1)}, u32[]{:S(2)}, u32[]{:S(2)}) collective-permute-start(bf16[4,144,1152]{2,1,0:T(8,128)(2,1)} %add_all.16), channel_id=1, source_target_pairs={{0,4},{1,5},{2,6},{3,7},{4,0},{5,1},{6,2},{7,3},{8,12},{9,13},{10,... | collective-permute-start | bytes 3981320 | tf_op jit(solution)/shard_map/ppermute | solution.py:799
  670.7 38.6 %collective-permute-start.58 = (bf16[4,144,640]{2,1,0:T(8,128)(2,1)}, bf16[4,144,640]{2,1,0:T(8,128)(2,1)}, u32[]{:S(2)}, u32[]{:S(2)}) collective-permute-start(bf16[4,144,640]{2,1,0:T(8,128)(2,1)} %get-tuple-element.759), channel_id=1, source_target_pairs={{0,1},{1,0},{2,3},{3,2},{4,5},{5,4},{6,7},{7,6},{8,9},{9,8},{10,11... | collective-permute-start | bytes 2211848 | tf_op jit(solution)/shard_map/ppermute | solution.py:799
  714.2 109.0 %reduce-scatter.14.cloned.1.call-start = ((), (), s32[]{:S(2)}) async-start(), calls=%async_computation.13 | async-start | bytes 1843200 | tf_op jit(solution)/shard_map/reduce_scatter | solution.py:935
  714.8 157.0 %reduce-scatter.10.cloned.1.call-start = ((), (), s32[]{:S(2)}) async-start(), calls=%async_computation.11 | async-start | bytes 1658880 | tf_op jit(solution)/shard_map/reduce_scatter | solution.py:935
  714.8 46.1 %collective-permute-start.56 = (bf16[4,144,1152]{2,1,0:T(8,128)(2,1)}, bf16[4,144,1152]{2,1,0:T(8,128)(2,1)}, u32[]{:S(2)}, u32[]{:S(2)}) collective-permute-start(bf16[4,144,1152]{2,1,0:T(8,128)(2,1)} %add_all.17), channel_id=1, source_target_pairs={{0,1},{1,0},{2,3},{3,2},{4,5},{5,4},{6,7},{7,6},{8,9},{9,8},{10,11... | collective-permute-start | bytes 3981320 | tf_op jit(solution)/shard_map/ppermute | solution.py:799
  716.0 44.9 %collective-permute-start.57 = (bf16[4,288,576]{2,1,0:T(8,128)(2,1)S(1)}, bf16[4,288,576]{2,1,0:T(8,128)(2,1)S(1)}, u32[]{:S(2)}, u32[]{:S(2)}) collective-permute-start(bf16[4,288,576]{2,1,0:T(8,128)(2,1)S(1)} %copy-done.23), channel_id=1, source_target_pairs={{0,4},{1,5},{2,6},{3,7},{4,0},{5,1},{6,2},{7,3},{8,12},{9,13},{10,... | collective-permute-start | bytes 3981320 | tf_op jit(solution)/shard_map/ppermute | solution.py:799
  717.3 43.6 %collective-permute-start.52 = (bf16[4,144,640]{2,1,0:T(8,128)(2,1)}, bf16[4,144,640]{2,1,0:T(8,128)(2,1)}, u32[]{:S(2)}, u32[]{:S(2)}) collective-permute-start(bf16[4,144,640]{2,1,0:T(8,128)(2,1)} %get-tuple-element.743), channel_id=1, source_target_pairs={{0,1},{1,0},{2,3},{3,2},{4,5},{5,4},{6,7},{7,6},{8,9},{9,8},{10,11... | collective-permute-start | bytes 2211848 | tf_op jit(solution)/shard_map/ppermute | solution.py:799
  718.2 42.7 %collective-permute-start.53 = (bf16[4,144,512]{2,1,0:T(8,128)(2,1)}, bf16[4,144,512]{2,1,0:T(8,128)(2,1)}, u32[]{:S(2)}, u32[]{:S(2)}) collective-permute-start(bf16[4,144,512]{2,1,0:T(8,128)(2,1)} %get-tuple-element.744), channel_id=1, source_target_pairs={{0,4},{1,5},{2,6},{3,7},{4,0},{5,1},{6,2},{7,3},{8,12},{9,13},{10,... | collective-permute-start | bytes 1769480 | tf_op jit(solution)/shard_map/ppermute | solution.py:799
  765.8 119.9 %reduce-scatter.12.cloned.1.call-start = ((), (), s32[]{:S(2)}) async-start(), calls=%async_computation.12 | async-start | bytes 1843200 | tf_op jit(solution)/shard_map/reduce_scatter | solution.py:935
  807.3 58.5 %collective-permute-start.71 = (bf16[144,1152]{1,0:T(8,128)(2,1)}, bf16[144,1152]{1,0:T(8,128)(2,1)S(1)}, u32[]{:S(2)}, u32[]{:S(2)}) collective-permute-start(bf16[144,1152]{1,0:T(8,128)(2,1)} %get-tuple-element.842), channel_id=1, source_target_pairs={{0,16},{1,17},{2,18},{3,19},{4,20},{5,21},{6,22},{7,23},{8,24},{9,... | collective-permute-start | bytes 995336 | tf_op jit(solution)/shard_map/ppermute | solution.py:799
  811.0 54.9 %collective-permute-start.70 = (bf16[144,1152]{1,0:T(8,128)(2,1)}, bf16[144,1152]{1,0:T(8,128)(2,1)S(1)}, u32[]{:S(2)}, u32[]{:S(2)}) collective-permute-start(bf16[144,1152]{1,0:T(8,128)(2,1)} %get-tuple-element.841), channel_id=1, source_target_pairs={{0,8},{1,9},{2,10},{3,11},{4,12},{5,13},{6,14},{7,15},{8,16},{9,17... | collective-permute-start | bytes 995336 | tf_op jit(solution)/shard_map/ppermute | solution.py:799
  835.7 53.2 %all-to-all-start.3 = ((bf16[16,2,9216]{2,1,0:T(2,128)(2,1)}), bf16[16,2,9216]{2,1,0:T(2,128)(2,1)S(1)}, u32[]{:S(2)}, u32[]{:S(2)}) async-start(bf16[16,2,9216]{2,1,0:T(2,128)(2,1)} %reshape.684), calls=%async_computation.5 | async-start | bytes 1179648 | tf_op jit(solution)/shard_map/all_to_all | solution.py:1495
  (101 other events, 1409.1 us)
Sparse Core Ops, SparseCore 0:
  161.7 93.0 all-gather.2
  609.1 39.7 reduce-scatter.5
  714.3 38.9 reduce-scatter.7
  755.5 33.7 reduce-scatter.13
  791.5 47.3 reduce-scatter.9
  841.2 44.2 reduce-scatter.11

commit v3 on v2

--- a/solution.py
+++ b/solution.py
@@ -960,15 +960,13 @@
             parts = self.tie(*parts)
             return [Arriving(self, part, k % 2 == 0) for k, part in enumerate(parts)]
 
-        rows = self.fly(rows, to_frames)
         pieces = self.gather_z(qkv_s)
         list(mod_steps)
         mods = mods()
         one = stacked(pieces, [0, cut, cols[0]])
         for strip in one:
             strip.first()
-        self.land(rows)
-        rows = self.both(rows.value)
+        rows = self.both(rows)
         pieces = self.gather_z(mlp_s)
         for strip in one:
             strip.second()
@@ -1136,6 +1134,8 @@
         up_s.first(0)
         down_s.first(0)
         up_z = self.across_z(up_t.sum)
+        down_t.total()
+        down_z = self.across_z(down_t.sum)
         grad_mid, grad_branch, sums_two, grad_qkv = self.run(
             attend_grad,
             part,
@@ -1160,8 +1160,6 @@
         )
         part = self.run(qkv_part, grad_qkv, qkv_w, features)
         came = self.fly(part, flip)
-        down_t.total()
-        down_z = self.across_z(down_t.sum)
         self.land()
 
         early.first(0)
@@ -1177,6 +1175,7 @@
         late.first(1)
         up_s.fly_second()
         down_s.fly_second()
+        chain = Chain(self, condition_steps(mods_s, mods_t))
         qkv_t.total()
         qkv_z = self.across_z(qkv_t.sum)
         early.add_second()
@@ -1192,7 +1191,6 @@
         self.land()
         self.strict = True
         self.token, _ = lax.optimization_barrier((start, self.token))
-        chain = Chain(self, condition_steps(mods_s, mods_t))
         own, *planes = self.run(
             add_planes,
             [early.near[1], late.near[1]],
@@ -1627,10 +1625,13 @@
         plan = Split(grid, head, hidden // patch, whose[0])
         hold = plan.tie
         marks = (place_of.reshape(-1, 1), place_of.reshape(1, -1))
+        early = plan.fly(tokens, to_frames)
         shards = plan.prepare(spatial_shards, temporal_shards)
         steps = mod_steps(hold)
         for _ in range(2):
             next(steps)
+
+        plan.land(early)
 
         def mods_of():
             return [
@@ -1639,7 +1640,7 @@
             ]
 
         result, spatial_state, temporal_state = plan.forward(
-            tokens,
+            early.value,
             mods_of,
             steps,
             shards,

time: 909 us -> 899 us (0.989)
    ppermute x67, waiting for transfers between devices: 229 us -> 203 us  [send(): return lax.ppermute(array, self.every, self.moves(step))]
    reduce_scatter x5, waiting for transfers between devices: 0.07 us -> 15.9 us  [across_z(): lax.psum_scatter(array, self.grid.chips[0], scatter_dimension=0, tiled=Fa...]
    unnamed x100 -> x112, local copies, waits for them, and re-layouts: 21.5 us -> 22.1 us
  transfers between devices with their start and end apart: 87 -> 87, of which waited for: 30 -> 31; matrix products, arithmetic and copies ran while one was open for 7% -> 8% of each run, Pallas kernels for 31% -> 32%
where the time goes in v3:
time: 899 us; the launch traced here: 892 us
  Pallas kernels  315 us (35%)
  waiting for transfers between devices  307 us (34%)
  starting transfers between devices  123 us (14%)
  blocking collectives  45.9 us (5%)
  local copies, waits for them, and re-layouts  38.4 us (4%)
  other arithmetic  37 us (4%)
  between operations  17.6 us (2%)
    pallas_call x30, Pallas kernels, call(): pl.pallas_call(kernel, out_shape=outs, in_specs=[pl.BlockSpec(memory_spac...  208 us
    ppermute x67, waiting for transfers between devices, send(): return lax.ppermute(array, self.every, self.moves(step))  203 us
    ppermute x67, starting transfers between devices, send(): return lax.ppermute(array, self.every, self.moves(step))  67.3 us
    all_gather x1, waiting for transfers between devices, forward(): held_t = lax.all_gather(self.tie(packed), grid.chips[0], axis=0)  56.2 us
    pallas_call x12, Pallas kernels, add_all(): pl.pallas_call(kernel, out_shape=shape((depth, rows, cols), LOW), grid_sp...  55.3 us
    pallas_call x6, Pallas kernels, weight_grad(): pl.pallas_call(kernel, out_shape=[shape((depth, rows, w), LOW) for w in w...  52.4 us
    all_to_all x1, blocking collectives, to_patches(): lax.all_to_all(array.reshape(groups, own_frames, -1, features), patch_axe...  45.9 us
    ppermute x11, starting transfers between devices, xor_patch(): return lax.ppermute(array, self.every, pairs)  29.2 us
  transfers between devices with their start and end apart: 87, of which 31 were waited for; matrix products, arithmetic and copies ran while one was open for 8% of the time, Pallas kernels for 32%

profile of v3, /device:TPU:0, one launch (start us, length us, event | category | flops | bytes accessed | tf_op | source)
XLA Modules:
  0.0 892.0 jit_solution(10906106622010905046)
XLA Ops:
  28.3 8.3 collective-permute-done.1
  56.2 8.8 collective-permute-done.6
  65.0 13.2 %collective-permute-done.5 = bf16[144,1152]{1,0:T(8,128)(2,1)S(1)} collective-permute-done((bf16[144,1152]{1,0:T(8,128)(2,1)}, bf16[144,1152]{1,0:T(8,128)(2,1)S(1)}, u32[]{:S(2)}, u32[]{:S(2)}) %collective-permute-start.5) | collective-permute-done | bytes 331808 | tf_op jit(solution)/shard_map/ppermute | solution.py:799
  81.6 13.7 %collective-permute-done.13 = bf16[4,144,640]{2,1,0:T(8,128)(2,1)S(1)} collective-permute-done((bf16[4,144,640]{2,1,0:T(8,128)(2,1)S(1)}, bf16[4,144,640]{2,1,0:T(8,128)(2,1)S(1)}, u32[]{:S(2)}, u32[]{:S(2)}) %collective-permute-start.13) | collective-permute-done | bytes 737312 | tf_op jit(solution)/shard_map/ppermute | solution.py:799
  109.0 13.2 %collective-permute-done.16.refs_6_.refs_4_ = bf16[2,4,144,512]{3,2,1,0:T(8,128)(2,1)S(1)} collective-permute-done((bf16[2,4,144,512]{3,2,1,0:T(8,128)(2,1)S(1)}, bf16[2,4,144,512]{3,2,1,0:T(8,128)(2,1)S(1)}, u32[]{:S(2)}, u32[]{:S(2)}) %collective-permute-start.16) | collective-permute-done | bytes 1179680 | tf_op jit(solution)/shard_map/ppermute | solution.py:799
  127.1 22.1 %collective-permute-done.11 = bf16[144,2432]{1,0:T(8,128)(2,1)S(1)} collective-permute-done((bf16[144,2432]{1,0:T(8,128)(2,1)S(1)}, bf16[144,2432]{1,0:T(8,128)(2,1)S(1)}, u32[]{:S(2)}, u32[]{:S(2)}) %collective-permute-start.11) | collective-permute-done | bytes 700448 | tf_op jit(solution)/shard_map/ppermute | solution.py:799
  163.8 10.1 %attend_out.2 = (bf16[1,512,576]{2,1,0:T(8,128)(2,1)}, bf16[512,1152]{1,0:T(8,128)(2,1)}) custom-call(s32[4]{0:T(128)} %pad_add_fusion.1.where_ref.where, bf16[2,512,864]{2,1,0:T(8,128)(2,1)} %get-tuple-element.531.refs_0_.refs_9_, bf16[2,576,576]{2,1,0:T(8,128)(2,1)} %get-tuple-element.532.refs_1_.refs_8_), custom_call_target="tpu_custom_call" | custom-call | flops 1 | bytes 1 | tf_op jit(solution)/shard_map/attend_out/pallas_call | solution.py:145
  189.3 56.2 %all-gather.3.cloned.1.call-done = bf16[576,3584]{1,0:T(8,128)(2,1)} async-done(((bf16[144,3584]{1,0:T(8,128)(2,1)}), bf16[576,3584]{1,0:T(8,128)(2,1)}) %all-gather.3.cloned.1.call-update) | async-done | bytes 4128784 | tf_op jit(solution)/shard_map/all_gather | solution.py:975
  254.5 10.7 %norm_up.2 = (f32[512,1152]{1,0:T(8,128)}, f32[512,1152]{1,0:T(8,128)}, bf16[1,512,1152]{2,1,0:T(8,128)(2,1)}, bf16[2,512,1152]{2,1,0:T(8,128)(2,1)}, bf16[2,512,1152]{2,1,0:T(8,128)(2,1)}) custom-call(s32[4]{0:T(128)} %pad_add_fusion.1.where_ref.where, bf16[512,1152]{1,0:T(8,128)(2,1)} %get-tuple-element.563.refs_0_, ...), custom_call_target="tpu_custom_call" | custom-call | flops 1 | bytes 1 | tf_op jit(solution)/shard_map/norm_up/pallas_call | solution.py:145
  265.2 9.2 %down_part.2.refs_0_ = bf16[512,1152]{1,0:T(8,128)(2,1)} custom-call(s32[4]{0:T(128)} %pad_add_fusion.1.where_ref.where, bf16[2,512,1152]{2,1,0:T(8,128)(2,1)} %get-tuple-element.712.refs_0_, bf16[2,4,144,1280]{3,2,1,0:T(8,128)(2,1)} %copy-done.1, bf16[2,4,144,1280]{3,2,1,0:T(8,128)(2,1)} %collective-permute-done.21.refs_2_.refs_7_), custom_call_target="tpu_custom_call" | custom-call | flops 1 | bytes 1 | tf_op jit(solution)/shard_map/down_part/pallas_call | solution.py:145
  296.6 11.4 %collective-permute-done.27 = bf16[4,144,640]{2,1,0:T(8,128)(2,1)} collective-permute-done((bf16[4,144,640]{2,1,0:T(8,128)(2,1)}, bf16[4,144,640]{2,1,0:T(8,128)(2,1)}, u32[]{:S(2)}, u32[]{:S(2)}) %collective-permute-start.27) | collective-permute-done | bytes 737312 | tf_op jit(solution)/shard_map/ppermute | solution.py:799
  324.3 45.9 %all_to_all.16 = bf16[16,2,9216]{2,1,0:T(2,128)(2,1)} all-to-all(bf16[16,2,9216]{2,1,0:T(2,128)(2,1)} %reshape.682), channel_id=1, replica_groups=mesh['z'=4,'y'=2,'core'=2,'x'=2] {'z','y','core'}, dimensions={0} | all-to-all | bytes 1179648 | tf_op jit(solution)/shard_map/all_to_all | solution.py:1493
  387.8 10.0 %attend_out.3 = (bf16[1,512,576]{2,1,0:T(8,128)(2,1)}, bf16[512,1152]{1,0:T(8,128)(2,1)}) custom-call(s32[4]{0:T(128)} %pad_add_fusion.1.where_ref.where, bf16[2,512,864]{2,1,0:T(8,128)(2,1)} %get-tuple-element.630.refs_0_.refs_9_, bf16[2,576,576]{2,1,0:T(8,128)(2,1)} %get-tuple-element.631.refs_1_.refs_8_, s32[256,1]{1,0:T(8,128)} %fusion.refs_2_.refs_10_, ...), custom_call_target="tpu_custom_call" | custom-call | flops 1 | bytes 1 | tf_op jit(solution)/shard_map/attend_out/pallas_call | solution.py:145
  401.8 11.2 %norm_up.3 = (f32[512,1152]{1,0:T(8,128)}, f32[512,1152]{1,0:T(8,128)}, bf16[1,512,1152]{2,1,0:T(8,128)(2,1)}, bf16[2,512,1152]{2,1,0:T(8,128)(2,1)}, bf16[2,512,1152]{2,1,0:T(8,128)(2,1)}) custom-call(s32[4]{0:T(128)} %pad_add_fusion.1.where_ref.where, bf16[512,1152]{1,0:T(8,128)(2,1)} %get-tuple-element.640.refs_0_, bf16[512,1152]{1,0:T(8,128)(2,1)} %copy-done.27, ...), custom_call_target="tpu_custom_call" | custom-call | flops 1 | bytes 1 | tf_op jit(solution)/shard_map/norm_up/pallas_call | solution.py:145
  413.1 9.3 %down_part.3.refs_0_ = bf16[512,1152]{1,0:T(8,128)(2,1)} custom-call(s32[4]{0:T(128)} %pad_add_fusion.1.where_ref.where, bf16[2,512,1152]{2,1,0:T(8,128)(2,1)} %get-tuple-element.655.refs_0_, bf16[2,4,144,640]{3,2,1,0:T(8,128)(2,1)} %pad_maximum_fusion.6.refs_1_.refs_6_, bf16[2,4,144,640]{3,2,1,0:T(8,128)(2,1)} %collective-permute-done.32.refs_2_.refs_7_, ...), custom_call_target="tpu_custom_call" | custom-call | flops 1 | bytes 1 | tf_op jit(solution)/shard_map/down_part/pallas_call | solution.py:145
  431.9 17.8 %mlp_back.2 = (bf16[2,512,576]{2,1,0:T(8,128)(2,1)}, bf16[2,512,1152]{2,1,0:T(8,128)(2,1)}, bf16[512,1152]{1,0:T(8,128)(2,1)}) custom-call(s32[4]{0:T(128)} %pad_add_fusion.1.where_ref.where, bf16[256,1152]{1,0:T(8,128)(2,1)} %bitcast.177, bf16[256,1152]{1,0:T(8,128)(2,1)} %copy-done.16, f32[8,1152]{1,0:T(8,128)} %pad.8.refs_2_.refs_4_.refs_3_, ...), custom_call_target="tpu_custom_call" | custom-call | flops 1 | bytes 1 | tf_op jit(solution)/shard_map/mlp_back/pallas_call | solution.py:145
  449.9 8.8 weight_grad.6
  469.8 16.0 %attend_grad.2 = (f32[512,1152]{1,0:T(8,128)}, bf16[2,512,576]{2,1,0:T(8,128)(2,1)}, f32[8,1152]{1,0:T(8,128)}, bf16[2,512,864]{2,1,0:T(8,128)(2,1)}) custom-call(s32[4]{0:T(128)} %pad_add_fusion.1.where_ref.where, bf16[512,1152]{1,0:T(8,128)(2,1)} %get-tuple-element.680.refs_0_, bf16[512,1152]{1,0:T(8,128)(2,1)} %copy-done.25, bf16[256,1152]{1,0:T(8,128)(2,1)} %bitcast.178, ...), custom_call_target="tpu_custom_call" | custom-call | flops 1 | bytes 1 | tf_op jit(solution)/shard_map/attend_grad/pallas_call | solution.py:145
  496.3 9.3 %weight_grad.8 = (bf16[4,144,1152]{2,1,0:T(8,128)(2,1)}, bf16[4,144,1152]{2,1,0:T(8,128)(2,1)}, bf16[4,144,1152]{2,1,0:T(8,128)(2,1)}, bf16[4,144,1152]{2,1,0:T(8,128)(2,1)}) custom-call(s32[4]{0:T(128)} %pad_add_fusion.1.where_ref.where, bf16[1,512,1152]{2,1,0:T(8,128)(2,1)} %get-tuple-element.691.refs_0_, ...), custom_call_target="tpu_custom_call" | custom-call | flops 1 | bytes 1 | tf_op jit(solution)/shard_map/weight_grad/pallas_call | solution.py:583
  511.2 14.4 %all-to-all-start.2 = ((bf16[1,16,16,1152]{3,2,0,1:T(8,128)(2,1)}), bf16[1,16,16,1152]{3,2,0,1:T(8,128)(2,1)S(1)}, u32[]{:S(2)}, u32[]{:S(2)}) async-start(bf16[1,16,16,1152]{3,2,0,1:T(8,128)(2,1)} %bitcast.186), calls=%async_computation.2 | async-start | bytes 1179648 | tf_op jit(solution)/shard_map/all_to_all | solution.py:1480
  546.8 11.3 %collective-permute-done.42.refs_1_ = bf16[4,144,1152]{2,1,0:T(8,128)(2,1)} collective-permute-done((bf16[4,144,1152]{2,1,0:T(8,128)(2,1)}, bf16[4,144,1152]{2,1,0:T(8,128)(2,1)}, u32[]{:S(2)}, u32[]{:S(2)}) %collective-permute-start.42) | collective-permute-done | bytes 1327136 | tf_op jit(solution)/shard_map/ppermute | solution.py:799
  558.9 17.6 %mlp_back.3 = (bf16[2,512,576]{2,1,0:T(8,128)(2,1)}, bf16[2,512,1152]{2,1,0:T(8,128)(2,1)}, bf16[512,1152]{1,0:T(8,128)(2,1)}) custom-call(s32[4]{0:T(128)} %pad_add_fusion.1.where_ref.where, bf16[256,1152]{1,0:T(8,128)(2,1)} %bitcast.167, bf16[256,1152]{1,0:T(8,128)(2,1)} %copy-done.15, f32[8,1152]{1,0:T(8,128)} %pad.7.refs_2_.refs_4_.refs_3_, ...), custom_call_target="tpu_custom_call" | custom-call | flops 1 | bytes 1 | tf_op jit(solution)/shard_map/mlp_back/pallas_call | solution.py:145
  584.3 8.9 weight_grad.10
  601.3 16.8 %collective-permute-done.45.refs_2_ = bf16[4,288,576]{2,1,0:T(8,128)(2,1)} collective-permute-done((bf16[4,288,576]{2,1,0:T(8,128)(2,1)}, bf16[4,288,576]{2,1,0:T(8,128)(2,1)}, u32[]{:S(2)}, u32[]{:S(2)}) %collective-permute-start.45) | collective-permute-done | bytes 1327136 | tf_op jit(solution)/shard_map/ppermute | solution.py:799
  623.9 16.1 %attend_grad.3 = (f32[512,1152]{1,0:T(8,128)}, bf16[2,512,576]{2,1,0:T(8,128)(2,1)}, f32[8,1152]{1,0:T(8,128)}, bf16[2,512,864]{2,1,0:T(8,128)(2,1)}) custom-call(s32[4]{0:T(128)} %pad_add_fusion.1.where_ref.where, bf16[512,1152]{1,0:T(8,128)(2,1)} %get-tuple-element.720.refs_0_, bf16[512,1152]{1,0:T(8,128)(2,1)} %collective-permute-done.44.refs_1_, ...), custom_call_target="tpu_custom_call" | custom-call | flops 1 | bytes 1 | tf_op jit(solution)/shard_map/attend_grad/pallas_call | solution.py:145
  646.4 9.6 %weight_grad.11 = (bf16[4,144,640]{2,1,0:T(8,128)(2,1)}, bf16[4,144,640]{2,1,0:T(8,128)(2,1)}, bf16[4,144,640]{2,1,0:T(8,128)(2,1)}, bf16[4,144,640]{2,1,0:T(8,1...) custom-call(s32[4]{0:T(128)} %pad_add_fusion.1.where_ref.where, ...), custom_call_target="tpu_custom_call" | custom-call | flops 1 | bytes 1 | tf_op jit(solution)/shard_map/weight_grad/pallas_call | solution.py:583
  665.7 15.5 %collective-permute-done.49.refs_1_ = bf16[4,288,576]{2,1,0:T(8,128)(2,1)S(1)} collective-permute-done((bf16[4,288,576]{2,1,0:T(8,128)(2,1)}, bf16[4,288,576]{2,1,0:T(8,128)(2,1)S(1)}, u32[]{:S(2)}, u32[]{:S(2)}) %collective-permute-start.49) | collective-permute-done | bytes 1327136 | tf_op jit(solution)/shard_map/ppermute | solution.py:799
  711.1 9.7 %collective-permute-start.57 = (f32[2,1,6912]{2,1,0:T(1,128)S(1)}, f32[2,1,6912]{2,1,0:T(1,128)S(1)}, u32[]{:S(2)}, u32[]{:S(2)}) collective-permute-start(f32[2,1,6912]{2,1,0:T(1,128)S(1)} %constant_dynamic-update-slice_fusion), channel_id=1, source_target_pairs={{0,16},{1,17},{2,18},{3,19},{4,20},{5,21},{6,22},{7,23},{8,24},{9,... | collective-permute-start | bytes 165896 | tf_op jit(solution)/shard_map/ppermute | solution.py:819
  729.0 21.9 %collective-permute-done.55.refs_2_ = bf16[4,144,1152]{2,1,0:T(8,128)(2,1)} collective-permute-done((bf16[4,144,1152]{2,1,0:T(8,128)(2,1)}, bf16[4,144,1152]{2,1,0:T(8,128)(2,1)}, u32[]{:S(2)}, u32[]{:S(2)}) %collective-permute-start.55) | collective-permute-done | bytes 1327136 | tf_op jit(solution)/shard_map/ppermute | solution.py:799
  775.6 10.0 %collective-permute-start.63 = (f32[2,1,6912]{2,1,0:T(1,128)S(1)}, f32[2,1,6912]{2,1,0:T(1,128)S(1)}, u32[]{:S(2)}, u32[]{:S(2)}) collective-permute-start(f32[2,1,6912]{2,1,0:T(1,128)S(1)} %add.159), channel_id=1, source_target_pairs={{0,8},{1,9},{2,10},{3,11},{4,12},{5,13},{6,14},{7,15},{8,0},{9,1},... | collective-permute-start | bytes 165896 | tf_op jit(solution)/shard_map/ppermute | solution.py:819
  830.4 16.1 %collective-permute-done.71.refs_2_ = bf16[144,1152]{1,0:T(8,128)(2,1)S(1)} collective-permute-done((bf16[144,1152]{1,0:T(8,128)(2,1)}, bf16[144,1152]{1,0:T(8,128)(2,1)S(1)}, u32[]{:S(2)}, u32[]{:S(2)}) %collective-permute-start.71) | collective-permute-done | bytes 331808 | tf_op jit(solution)/shard_map/ppermute | solution.py:799
  859.3 15.8 %reduce-scatter.12.cloned.1.call-done = bf16[1,288,576]{2,1,0:T(8,128)(2,1)} async-done(((bf16[4,288,576]{2,1,0:T(8,128)(2,1)}), bf16[1,288,576]{2,1,0:T(8,128)(2,1)}) %reduce-scatter.12.cloned.1.call-update) | async-done | bytes 331792 | tf_op jit(solution)/shard_map/reduce_scatter | solution.py:935
  (413 shorter events, 385.4 us)
Async XLA Ops:
  11.6 37.6 %all-to-all-start = ((bf16[1,16,16,1152]{3,2,0,1:T(8,128)(2,1)}), bf16[1,16,16,1152]{3,2,0,1:T(8,128)(2,1)S(1)}, u32[]{:S(2)}, u32[]{:S(2)}) async-start(bf16[1,16,16,1152]{3,2,0,1:T(8,128)(2,1)} %bitcast.185), calls=%async_computation | async-start | bytes 1179648 | tf_op jit(solution)/shard_map/all_to_all | solution.py:1480
  17.6 227.9 %all-gather.3.cloned.1.call-start = ((), (), s32[]{:S(2)}) async-start(), calls=%async_computation.14 | async-start | bytes 5160960 | tf_op jit(solution)/shard_map/all_gather | solution.py:975
  106.4 42.8 %collective-permute-start.11 = (bf16[144,2432]{1,0:T(8,128)(2,1)S(1)}, bf16[144,2432]{1,0:T(8,128)(2,1)S(1)}, u32[]{:S(2)}, u32[]{:S(2)}) collective-permute-start(bf16[144,2432]{1,0:T(8,128)(2,1)S(1)} %copy-done.31), channel_id=1, source_target_pairs={{0,16},{1,17},{2,18},{3,19},{4,20},{5,21},{6,22},{7,23},{8,24},{9,... | collective-permute-start | bytes 2101256 | tf_op jit(solution)/shard_map/ppermute | solution.py:799
  106.4 42.9 %collective-permute-start.10 = (bf16[144,2432]{1,0:T(8,128)(2,1)S(1)}, bf16[144,2432]{1,0:T(8,128)(2,1)S(1)}, u32[]{:S(2)}, u32[]{:S(2)}) collective-permute-start(bf16[144,2432]{1,0:T(8,128)(2,1)S(1)} %copy-done.31), channel_id=1, source_target_pairs={{0,24},{1,25},{2,26},{3,27},{4,28},{5,29},{6,30},{7,31},{8,0},{9,1... | collective-permute-start | bytes 2101256 | tf_op jit(solution)/shard_map/ppermute | solution.py:799
  187.2 67.3 %collective-permute-start.21 = (bf16[2,4,144,1280]{3,2,1,0:T(8,128)(2,1)S(1)}, bf16[2,4,144,1280]{3,2,1,0:T(8,128)(2,1)}, u32[]{:S(2)}, u32[]{:S(2)}) collective-permute-start(bf16[2,4,144,1280]{3,2,1,0:T(8,128)(2,1)S(1)} %pad_maximum_fusion.refs_1_.refs_6_), channel_id=1, source_target_pairs={{0,1},{1,0},{2,3},{3,2},{4,5},{5,4},{6,7},{7,6},{8,9},{9,8},{10,11... | collective-permute-start | bytes 8847368 | tf_op jit(solution)/shard_map/ppermute | solution.py:799
  188.7 65.8 %collective-permute-start.19 = (bf16[2,4,144,1152]{3,2,1,0:T(8,128)(2,1)}, bf16[2,4,144,1152]{3,2,1,0:T(8,128)(2,1)}, u32[]{:S(2)}, u32[]{:S(2)}) collective-permute-start(bf16[2,4,144,1152]{3,2,1,0:T(8,128)(2,1)} %pad_maximum_fusion.1.refs_5_.refs_4_), channel_id=1, source_target_pairs={{0,4},{1,5},{2,6},{3,7},{4,0},{5,1},{6,2},{7,3},{8,12},{9,13},{10,... | collective-permute-start | bytes 7962632 | tf_op jit(solution)/shard_map/ppermute | solution.py:799
  291.2 88.9 %collective-permute-start.29 = (bf16[2,4,144,1152]{3,2,1,0:T(8,128)(2,1)S(1)}, bf16[2,4,144,1152]{3,2,1,0:T(8,128)(2,1)}, u32[]{:S(2)}, u32[]{:S(2)}) collective-permute-start(bf16[2,4,144,1152]{3,2,1,0:T(8,128)(2,1)S(1)} %pad_maximum_fusion.3.refs_5_.refs_4_), channel_id=1, source_target_pairs={{0,1},{1,0},{2,3},{3,2},{4,5},{5,4},{6,7},{7,6},{8,9},{9,8},{10,11... | collective-permute-start | bytes 7962632 | tf_op jit(solution)/shard_map/ppermute | solution.py:799
  291.8 88.3 %collective-permute-start.28 = (bf16[2,4,144,1152]{3,2,1,0:T(8,128)(2,1)}, bf16[2,4,144,1152]{3,2,1,0:T(8,128)(2,1)}, u32[]{:S(2)}, u32[]{:S(2)}) collective-permute-start(bf16[2,4,144,1152]{3,2,1,0:T(8,128)(2,1)} %pad_maximum_fusion.2.refs_3_.refs_1_), channel_id=1, source_target_pairs={{0,4},{1,5},{2,6},{3,7},{4,0},{5,1},{6,2},{7,3},{8,12},{9,13},{10,... | collective-permute-start | bytes 7962632 | tf_op jit(solution)/shard_map/ppermute | solution.py:799
  376.1 36.9 %collective-permute-start.33 = (bf16[2,4,144,640]{3,2,1,0:T(8,128)(2,1)}, bf16[2,4,144,640]{3,2,1,0:T(8,128)(2,1)}, u32[]{:S(2)}, u32[]{:S(2)}) collective-permute-start(bf16[2,4,144,640]{3,2,1,0:T(8,128)(2,1)} %pad_maximum_fusion.7.refs_3_.refs_8_), channel_id=1, source_target_pairs={{0,1},{1,0},{2,3},{3,2},{4,5},{5,4},{6,7},{7,6},{8,9},{9,8},{10,11... | collective-permute-start | bytes 4423688 | tf_op jit(solution)/shard_map/ppermute | solution.py:799
  376.8 36.3 %collective-permute-start.32 = (bf16[2,4,144,640]{3,2,1,0:T(8,128)(2,1)}, bf16[2,4,144,640]{3,2,1,0:T(8,128)(2,1)}, u32[]{:S(2)}, u32[]{:S(2)}) collective-permute-start(bf16[2,4,144,640]{3,2,1,0:T(8,128)(2,1)} %pad_maximum_fusion.6.refs_1_.refs_6_), channel_id=1, source_target_pairs={{0,4},{1,5},{2,6},{3,7},{4,0},{5,1},{6,2},{7,3},{8,12},{9,13},{10,... | collective-permute-start | bytes 4423688 | tf_op jit(solution)/shard_map/ppermute | solution.py:799
  458.7 46.9 %collective-permute-start.39 = (bf16[4,288,576]{2,1,0:T(8,128)(2,1)}, bf16[4,288,576]{2,1,0:T(8,128)(2,1)S(1)}, u32[]{:S(2)}, u32[]{:S(2)}) collective-permute-start(bf16[4,288,576]{2,1,0:T(8,128)(2,1)} %get-tuple-element.689), channel_id=1, source_target_pairs={{0,4},{1,5},{2,6},{3,7},{4,0},{5,1},{6,2},{7,3},{8,12},{9,13},{10,... | collective-permute-start | bytes 3981320 | tf_op jit(solution)/shard_map/ppermute | solution.py:799
  467.4 38.3 %collective-permute-start.38 = (bf16[4,144,1152]{2,1,0:T(8,128)(2,1)}, bf16[4,144,1152]{2,1,0:T(8,128)(2,1)}, u32[]{:S(2)}, u32[]{:S(2)}) collective-permute-start(bf16[4,144,1152]{2,1,0:T(8,128)(2,1)} %get-tuple-element.688), channel_id=1, source_target_pairs={{0,1},{1,0},{2,3},{3,2},{4,5},{5,4},{6,7},{7,6},{8,9},{9,8},{10,11... | collective-permute-start | bytes 3981320 | tf_op jit(solution)/shard_map/ppermute | solution.py:799
  495.0 39.3 %collective-permute-start.36 = (bf16[4,288,576]{2,1,0:T(8,128)(2,1)}, bf16[4,288,576]{2,1,0:T(8,128)(2,1)S(1)}, u32[]{:S(2)}, u32[]{:S(2)}) collective-permute-start(bf16[4,288,576]{2,1,0:T(8,128)(2,1)} %get-tuple-element.676), channel_id=1, source_target_pairs={{0,4},{1,5},{2,6},{3,7},{4,0},{5,1},{6,2},{7,3},{8,12},{9,13},{10,... | collective-permute-start | bytes 3981320 | tf_op jit(solution)/shard_map/ppermute | solution.py:799
  525.7 273.6 %reduce-scatter.6.cloned.1.call-start = ((), (), s32[]{:S(2)}) async-start(), calls=%async_computation.9 | async-start | bytes 1658880 | tf_op jit(solution)/shard_map/reduce_scatter | solution.py:935
  526.7 66.5 %collective-permute-start.46 = (bf16[4,144,1152]{2,1,0:T(8,128)(2,1)}, bf16[4,144,1152]{2,1,0:T(8,128)(2,1)}, u32[]{:S(2)}, u32[]{:S(2)}) collective-permute-start(bf16[4,144,1152]{2,1,0:T(8,128)(2,1)} %get-tuple-element.717), channel_id=1, source_target_pairs={{0,1},{1,0},{2,3},{3,2},{4,5},{5,4},{6,7},{7,6},{8,9},{9,8},{10,11... | collective-permute-start | bytes 3981320 | tf_op jit(solution)/shard_map/ppermute | solution.py:799
  532.3 60.9 %collective-permute-start.47 = (bf16[4,144,1152]{2,1,0:T(8,128)(2,1)}, bf16[4,144,1152]{2,1,0:T(8,128)(2,1)}, u32[]{:S(2)}, u32[]{:S(2)}) collective-permute-start(bf16[4,144,1152]{2,1,0:T(8,128)(2,1)} %add_all.12), channel_id=1, source_target_pairs={{0,4},{1,5},{2,6},{3,7},{4,0},{5,1},{6,2},{7,3},{8,12},{9,13},{10,... | collective-permute-start | bytes 3981320 | tf_op jit(solution)/shard_map/ppermute | solution.py:799
  545.9 72.2 %collective-permute-start.45 = (bf16[4,288,576]{2,1,0:T(8,128)(2,1)}, bf16[4,288,576]{2,1,0:T(8,128)(2,1)}, u32[]{:S(2)}, u32[]{:S(2)}) collective-permute-start(bf16[4,288,576]{2,1,0:T(8,128)(2,1)} %add_all.13), channel_id=1, source_target_pairs={{0,1},{1,0},{2,3},{3,2},{4,5},{5,4},{6,7},{7,6},{8,9},{9,8},{10,11... | collective-permute-start | bytes 3981320 | tf_op jit(solution)/shard_map/ppermute | solution.py:799
  598.0 210.3 %reduce-scatter.8.cloned.1.call-start = ((), (), s32[]{:S(2)}) async-start(), calls=%async_computation.10 | async-start | bytes 1658880 | tf_op jit(solution)/shard_map/reduce_scatter | solution.py:935
  598.2 66.0 %collective-permute-start.48 = (bf16[4,144,1152]{2,1,0:T(8,128)(2,1)}, bf16[4,144,1152]{2,1,0:T(8,128)(2,1)}, u32[]{:S(2)}, u32[]{:S(2)}) collective-permute-start(bf16[4,144,1152]{2,1,0:T(8,128)(2,1)} %get-tuple-element.730), channel_id=1, source_target_pairs={{0,4},{1,5},{2,6},{3,7},{4,0},{5,1},{6,2},{7,3},{8,12},{9,13},{10,... | collective-permute-start | bytes 3981320 | tf_op jit(solution)/shard_map/ppermute | solution.py:799
  600.3 64.1 %collective-permute-start.53 = (bf16[4,144,1152]{2,1,0:T(8,128)(2,1)}, bf16[4,144,1152]{2,1,0:T(8,128)(2,1)}, u32[]{:S(2)}, u32[]{:S(2)}) collective-permute-start(bf16[4,144,1152]{2,1,0:T(8,128)(2,1)} %get-tuple-element.744), channel_id=1, source_target_pairs={{0,4},{1,5},{2,6},{3,7},{4,0},{5,1},{6,2},{7,3},{8,12},{9,13},{10,... | collective-permute-start | bytes 3981320 | tf_op jit(solution)/shard_map/ppermute | solution.py:799
  600.4 65.2 %collective-permute-start.54 = (bf16[4,288,576]{2,1,0:T(8,128)(2,1)}, bf16[4,288,576]{2,1,0:T(8,128)(2,1)S(1)}, u32[]{:S(2)}, u32[]{:S(2)}) collective-permute-start(bf16[4,288,576]{2,1,0:T(8,128)(2,1)} %get-tuple-element.745), channel_id=1, source_target_pairs={{0,1},{1,0},{2,3},{3,2},{4,5},{5,4},{6,7},{7,6},{8,9},{9,8},{10,11... | collective-permute-start | bytes 3981320 | tf_op jit(solution)/shard_map/ppermute | solution.py:799
  618.1 63.1 %collective-permute-start.49 = (bf16[4,288,576]{2,1,0:T(8,128)(2,1)}, bf16[4,288,576]{2,1,0:T(8,128)(2,1)S(1)}, u32[]{:S(2)}, u32[]{:S(2)}) collective-permute-start(bf16[4,288,576]{2,1,0:T(8,128)(2,1)} %get-tuple-element.731), channel_id=1, source_target_pairs={{0,1},{1,0},{2,3},{3,2},{4,5},{5,4},{6,7},{7,6},{8,9},{9,8},{10,11... | collective-permute-start | bytes 3981320 | tf_op jit(solution)/shard_map/ppermute | solution.py:799
  644.5 53.9 %collective-permute-start.60 = (bf16[4,144,1152]{2,1,0:T(8,128)(2,1)}, bf16[4,144,1152]{2,1,0:T(8,128)(2,1)}, u32[]{:S(2)}, u32[]{:S(2)}) collective-permute-start(bf16[4,144,1152]{2,1,0:T(8,128)(2,1)} %add_all.16), channel_id=1, source_target_pairs={{0,4},{1,5},{2,6},{3,7},{4,0},{5,1},{6,2},{7,3},{8,12},{9,13},{10,... | collective-permute-start | bytes 3981320 | tf_op jit(solution)/shard_map/ppermute | solution.py:799
  703.2 107.2 %reduce-scatter.14.cloned.1.call-start = ((), (), s32[]{:S(2)}) async-start(), calls=%async_computation.13 | async-start | bytes 1843200 | tf_op jit(solution)/shard_map/reduce_scatter | solution.py:935
  703.8 148.6 %reduce-scatter.10.cloned.1.call-start = ((), (), s32[]{:S(2)}) async-start(), calls=%async_computation.11 | async-start | bytes 1658880 | tf_op jit(solution)/shard_map/reduce_scatter | solution.py:935
  708.4 42.5 %collective-permute-start.55 = (bf16[4,144,1152]{2,1,0:T(8,128)(2,1)}, bf16[4,144,1152]{2,1,0:T(8,128)(2,1)}, u32[]{:S(2)}, u32[]{:S(2)}) collective-permute-start(bf16[4,144,1152]{2,1,0:T(8,128)(2,1)} %add_all.17), channel_id=1, source_target_pairs={{0,1},{1,0},{2,3},{3,2},{4,5},{5,4},{6,7},{7,6},{8,9},{9,8},{10,11... | collective-permute-start | bytes 3981320 | tf_op jit(solution)/shard_map/ppermute | solution.py:799
  709.6 41.3 %collective-permute-start.56 = (bf16[4,288,576]{2,1,0:T(8,128)(2,1)S(1)}, bf16[4,288,576]{2,1,0:T(8,128)(2,1)S(1)}, u32[]{:S(2)}, u32[]{:S(2)}) collective-permute-start(bf16[4,288,576]{2,1,0:T(8,128)(2,1)S(1)} %copy-done.23), channel_id=1, source_target_pairs={{0,4},{1,5},{2,6},{3,7},{4,0},{5,1},{6,2},{7,3},{8,12},{9,13},{10,... | collective-permute-start | bytes 3981320 | tf_op jit(solution)/shard_map/ppermute | solution.py:799
  756.0 119.1 %reduce-scatter.12.cloned.1.call-start = ((), (), s32[]{:S(2)}) async-start(), calls=%async_computation.12 | async-start | bytes 1843200 | tf_op jit(solution)/shard_map/reduce_scatter | solution.py:935
  794.0 36.4 %collective-permute-start.72 = (bf16[144,1152]{1,0:T(8,128)(2,1)}, bf16[144,1152]{1,0:T(8,128)(2,1)S(1)}, u32[]{:S(2)}, u32[]{:S(2)}) collective-permute-start(bf16[144,1152]{1,0:T(8,128)(2,1)} %get-tuple-element.843), channel_id=1, source_target_pairs={{0,24},{1,25},{2,26},{3,27},{4,28},{5,29},{6,30},{7,31},{8,0},{9,1... | collective-permute-start | bytes 995336 | tf_op jit(solution)/shard_map/ppermute | solution.py:799
  794.0 52.4 %collective-permute-start.71 = (bf16[144,1152]{1,0:T(8,128)(2,1)}, bf16[144,1152]{1,0:T(8,128)(2,1)S(1)}, u32[]{:S(2)}, u32[]{:S(2)}) collective-permute-start(bf16[144,1152]{1,0:T(8,128)(2,1)} %get-tuple-element.842), channel_id=1, source_target_pairs={{0,16},{1,17},{2,18},{3,19},{4,20},{5,21},{6,22},{7,23},{8,24},{9,... | collective-permute-start | bytes 995336 | tf_op jit(solution)/shard_map/ppermute | solution.py:799
  798.0 48.5 %collective-permute-start.70 = (bf16[144,1152]{1,0:T(8,128)(2,1)}, bf16[144,1152]{1,0:T(8,128)(2,1)S(1)}, u32[]{:S(2)}, u32[]{:S(2)}) collective-permute-start(bf16[144,1152]{1,0:T(8,128)(2,1)} %get-tuple-element.841), channel_id=1, source_target_pairs={{0,8},{1,9},{2,10},{3,11},{4,12},{5,13},{6,14},{7,15},{8,16},{9,17... | collective-permute-start | bytes 995336 | tf_op jit(solution)/shard_map/ppermute | solution.py:799
  823.1 55.2 %all-to-all-start.3 = ((bf16[16,2,9216]{2,1,0:T(2,128)(2,1)}), bf16[16,2,9216]{2,1,0:T(2,128)(2,1)S(1)}, u32[]{:S(2)}, u32[]{:S(2)}) async-start(bf16[16,2,9216]{2,1,0:T(2,128)(2,1)} %reshape.684), calls=%async_computation.5 | async-start | bytes 1179648 | tf_op jit(solution)/shard_map/all_to_all | solution.py:1493
  (107 other events, 1442.4 us)
Sparse Core Ops, SparseCore 0:
  151.2 94.2 all-gather.2
  598.1 39.3 reduce-scatter.5
  703.3 39.7 reduce-scatter.7
  745.3 32.7 reduce-scatter.13
  780.4 47.9 reduce-scatter.9
  830.6 44.4 reduce-scatter.11
